TPU v7x, 32 devices: a whole 2x2x4 slice. The times are simulated.
32 devices in a mesh: fsdp: 16 (over z, y, core), tp: 2 (over x).
Axes of the slice: x: 2, y: 2, z: 4, core: 2. Of those that a mesh axis runs over, the one named last changes fastest.
Arguments:
- patches: bfloat16 [7168, 3072], P('fsdp'), may hold values from -500 to 500
- cotangent: bfloat16 [7168, 3072], P('fsdp'), may hold values from -6 to 6
- counts: int32 [16, 4], replicated, may hold values from 32 to 112, as said below
- masks: int32 [4], replicated, may hold values from 0 to 15, as said below
- norm_gain: float32 [3072], replicated, may hold values from 0.25 to 1.75
- qk_gain: float32 [2, 128], replicated, may hold values from 0.25 to 1.75
- qkv_weight: bfloat16 [3072, 9216], P('fsdp', 'tp'), may hold values from -0.109375 to 0.109375
- out_weight: bfloat16 [3072, 3072], P('fsdp', 'tp'), may hold values from -0.109375 to 0.109375
Outputs:
- attended: bfloat16 [7168, 3072], P('fsdp', 'tp')
- grad_rows: bfloat16 [7168, 3072], P('fsdp', 'tp')
- grad_qkv_weight: float32 [3072, 9216], P('fsdp', 'tp')
- grad_out_weight: float32 [3072, 3072], P('fsdp', 'tp')
Inputs may be any that keep to these rules, and one draw needn't show every extreme that they name: `masks`: in every draw some slot's mask is 15. `counts`: in every draw some run block holds 112 patches in each of its slots.
All inputs are finite; a program needn't handle non-finite values.
Results may differ from a plain program's by a relative error of at most 0.02.
Values may be sent and summed in bfloat16 or wider, within the bound.
No kernel may reach another device: no remote copies, remote signals or barrier semaphores. Data moves between devices by JAX's collectives and lax.ppermute only.
A program may use at most 192 MiB of HBM per device.

v0:
```python
import jax
import jax.numpy as jnp
from jax import lax
from jax.sharding import PartitionSpec as P

epsilon = 1e-06


def partner_2(value, axis, stride):
    mask = 2**stride
    pairs = [(source, source ^ mask) for source in range(lax.axis_size(axis))]
    return lax.ppermute(value, axis, pairs)


def norm_rows(values):
    row_mean = jnp.mean(values, axis=-1, keepdims=True)
    centred = values - row_mean
    factor = lax.rsqrt(jnp.mean(centred * centred, axis=-1, keepdims=True) + epsilon)
    return (centred * factor, factor)


def norm_back(upstream, normed, factor):
    return factor * (
        upstream
        - jnp.mean(upstream, axis=-1, keepdims=True)
        - normed * jnp.mean(upstream * normed, axis=-1, keepdims=True)
    )


def per_device(patches, cotangent, counts, masks, norm_gain, qk_gain, qkv_weight, out_weight):
    replicas = lax.axis_size("fsdp")
    groups = lax.axis_size("tp")
    my_replica = lax.axis_index("fsdp")
    my_group = lax.axis_index("tp")
    tok_rows = patches.shape[0]
    images = counts.shape[1]
    slot_rows = tok_rows // images
    model_width = norm_gain.shape[0]
    share_width = model_width // groups
    head_dim = qk_gain.shape[1]
    qkv_cols = qkv_weight.shape[1]
    out_cols = out_weight.shape[1]
    local_heads = out_cols // head_dim
    row_slot = jnp.arange(tok_rows, dtype=jnp.int32) // slot_rows
    holding = lax.dynamic_slice_in_dim(patches, my_group * share_width, share_width, 1)
    digit_count = replicas.bit_length() - 1
    digit_order = list(range(digit_count))
    for bit_place in digit_order:
        partner = partner_2(holding, "fsdp", bit_place)
        moving = jnp.bitwise_and(jnp.right_shift(masks, bit_place), 1) == 1
        take_rows = jnp.take(moving, row_slot)
        holding = jnp.where(take_rows[:, None], partner, holding)
    replica_ids = jnp.arange(replicas, dtype=jnp.int32)
    sources = jnp.bitwise_xor(my_replica, masks)
    run_counts = jnp.sum(jnp.where(replica_ids[:, None] == sources[None, :], counts, 0), axis=0)
    places = jnp.arange(slot_rows, dtype=jnp.int32)
    live_slots = places[None, :] < run_counts[:, None]
    is_live = live_slots.reshape(tok_rows)
    allowed = live_slots[:, :, None] & live_slots[:, None, :] | jnp.eye(slot_rows, dtype=bool)[None]
    packed = jnp.where(is_live[:, None], holding, jnp.zeros((), holding.dtype))
    block_rows = lax.all_gather(packed, "tp", axis=1, tiled=True)
    qkv_full, out_full = (
        lax.all_gather(qkv_weight, "fsdp", axis=0, tiled=True),
        lax.all_gather(out_weight, "fsdp", axis=0, tiled=True),
    )
    centred_rows, row_factor = norm_rows(block_rows.astype(jnp.float32))
    normed = (centred_rows * norm_gain).astype(jnp.bfloat16)
    projected = jnp.dot(normed, qkv_full, preferred_element_type=jnp.float32).reshape(
        images, slot_rows, local_heads, 3, head_dim
    )
    query_hat, query_factor = norm_rows(projected[:, :, :, 0])
    key_hat, key_factor = norm_rows(projected[:, :, :, 1])
    query_scale = qk_gain[0] * head_dim ** (-0.5)
    key_scale = qk_gain[1]
    query = (query_hat * query_scale).astype(jnp.bfloat16)
    key_rows = (key_hat * key_scale).astype(jnp.bfloat16)
    values = projected[:, :, :, 2].astype(jnp.bfloat16)
    scores = jnp.einsum("sqhe,skhe->shqk", query, key_rows, preferred_element_type=jnp.float32)
    raised = jnp.where(allowed[:, None], jnp.exp(scores), 0.0)
    attention = raised / jnp.sum(raised, axis=-1, keepdims=True)
    rounded_attention = attention.astype(jnp.bfloat16)
    mixed = jnp.einsum(
        "shqk,skhe->sqhe", rounded_attention, values, preferred_element_type=jnp.float32
    )
    mixed = mixed.astype(jnp.bfloat16).reshape(tok_rows, out_cols)
    partial_value = lax.dot_general(
        mixed, out_full, (((1,), (1,)), ((), ())), preferred_element_type=jnp.float32
    )
    attended = lax.psum_scatter(
        partial_value.astype(jnp.bfloat16), "tp", scatter_dimension=1, tiled=True
    ).astype(jnp.float32)
    attended = jnp.where(is_live[:, None], attended, 0.0).astype(jnp.bfloat16)
    upstream_rows = jnp.where(is_live[:, None], cotangent, jnp.zeros((), cotangent.dtype))
    grad_mixed = jnp.dot(upstream_rows, out_full, preferred_element_type=jnp.float32).astype(
        jnp.bfloat16
    )
    grad_heads = grad_mixed.reshape(images, slot_rows, local_heads, head_dim)
    grad_value = jnp.einsum(
        "shqk,sqhe->skhe", rounded_attention, grad_heads, preferred_element_type=jnp.float32
    )
    grad_attention = jnp.einsum(
        "sqhe,skhe->shqk", grad_heads, values, preferred_element_type=jnp.float32
    )
    grad_scores = attention * (
        grad_attention - jnp.sum(attention * grad_attention, axis=-1, keepdims=True)
    )
    grad_scores = grad_scores.astype(jnp.bfloat16)
    grad_query = jnp.einsum(
        "shqk,skhe->sqhe", grad_scores, key_rows, preferred_element_type=jnp.float32
    )
    grad_key = jnp.einsum("shqk,sqhe->skhe", grad_scores, query, preferred_element_type=jnp.float32)
    query_grad = norm_back(grad_query * query_scale, query_hat, query_factor)
    key_grad = norm_back(grad_key * key_scale, key_hat, key_factor)
    grad_qkv = (
        jnp.stack([query_grad, key_grad, grad_value], axis=3)
        .astype(jnp.bfloat16)
        .reshape(tok_rows, qkv_cols)
    )
    qkv_term = lax.dot_general(
        normed, grad_qkv, (((0,), (0,)), ((), ())), preferred_element_type=jnp.float32
    )
    out_term = lax.dot_general(
        upstream_rows, mixed, (((0,), (0,)), ((), ())), preferred_element_type=jnp.float32
    )
    stacked = lax.psum_scatter(
        jnp.concatenate([qkv_term, out_term], axis=1).astype(jnp.bfloat16),
        "fsdp",
        scatter_dimension=0,
        tiled=True,
    ).astype(jnp.float32)
    grad_qkv_weight = stacked[:, :qkv_cols]
    grad_out_weight = stacked[:, qkv_cols:]
    partial_back = lax.dot_general(
        grad_qkv, qkv_full, (((1,), (1,)), ((), ())), preferred_element_type=jnp.float32
    )
    summed = lax.psum(partial_back.astype(jnp.bfloat16), "tp").astype(jnp.float32)
    grad_full = norm_back(summed * norm_gain, centred_rows, row_factor)
    grad_share = lax.dynamic_slice_in_dim(grad_full, my_group * share_width, share_width, 1)
    grad_rows = grad_share.astype(jnp.bfloat16)
    return (attended, grad_rows, grad_qkv_weight, grad_out_weight)


def solution(mesh):
    in_specs = (
        P("fsdp", None),
        P("fsdp", None),
        P(),
        P(),
        P(),
        P(),
        P("fsdp", "tp"),
        P("fsdp", "tp"),
    )
    out_specs = (P("fsdp", "tp"), P("fsdp", "tp"), P("fsdp", "tp"), P("fsdp", "tp"))
    return jax.shard_map(
        per_device, mesh=mesh, in_specs=in_specs, out_specs=out_specs, check_vma=False
    )
```

profile of v0, /device:TPU:0, one launch (start us, length us, event | category | flops | bytes accessed | tf_op | source)
XLA Modules:
  0.0 1038.7 jit_solution(15759587940942123946)
XLA Ops:
  13.0 2.6 collective-permute-start.1
  18.2 28.2 %collective-permute-done.1 = bf16[448,1536]{1,0:T(8,128)(2,1)S(1)} collective-permute-done((bf16[448,1536]{1,0:T(8,128)(2,1)S(1)}, bf16[448,1536]{1,0:T(8,128)(2,1)S(1)}, u32[]{:S(2)}, u32[]{:S(2)}) %collective-permute-start.1) | collective-permute-done | bytes 1376288 | tf_op jit(solution)/shard_map/ppermute | solution.py:12
  51.7 27.0 %collective-permute-done.2 = bf16[448,1536]{1,0:T(8,128)(2,1)S(1)} collective-permute-done((bf16[448,1536]{1,0:T(8,128)(2,1)S(1)}, bf16[448,1536]{1,0:T(8,128)(2,1)S(1)}, u32[]{:S(2)}, u32[]{:S(2)}) %collective-permute-start.2) | collective-permute-done | bytes 1376288 | tf_op jit(solution)/shard_map/ppermute | solution.py:12
  78.9 2.7 collective-permute-start.3
  81.9 2.6 select_select_fusion.4
  84.5 56.0 %collective-permute-done.3 = bf16[448,1536]{1,0:T(8,128)(2,1)S(1)} collective-permute-done((bf16[448,1536]{1,0:T(8,128)(2,1)S(1)}, bf16[448,1536]{1,0:T(8,128)(2,1)S(1)}, u32[]{:S(2)}, u32[]{:S(2)}) %collective-permute-start.3) | collective-permute-done | bytes 1376288 | tf_op jit(solution)/shard_map/ppermute | solution.py:12
  143.5 39.9 %all-gather.4.cloned.1.call-done = bf16[448,3072]{1,0:T(8,128)(2,1)} async-done(((bf16[448,1536]{1,0:T(8,128)(2,1)}), bf16[448,3072]{1,0:T(8,128)(2,1)}) %all-gather.4.cloned.1.call-update) | async-done | bytes 2752528 | tf_op jit(solution)/shard_map/all_gather | solution.py:61
  186.9 80.3 %all-gather.8.cloned.1.call-done = bf16[3072,1536]{1,0:T(8,128)(2,1)} async-done(((bf16[192,1536]{1,0:T(8,128)(2,1)}), bf16[3072,1536]{1,0:T(8,128)(2,1)}) %all-gather.8.cloned.1.call-update) | async-done | bytes 9437200 | tf_op jit(solution)/shard_map/all_gather | solution.py:64
  267.2 10.1 convolution_convert_fusion.4
  277.2 4.3 reshape.162
  281.5 128.9 %all-gather.6.cloned.1.call-done = bf16[3072,4608]{1,0:T(8,128)(2,1)} async-done(((bf16[192,4608]{1,0:T(8,128)(2,1)}), bf16[3072,4608]{1,0:T(8,128)(2,1)}) %all-gather.6.cloned.1.call-update) | async-done | bytes 28311568 | tf_op jit(solution)/shard_map/all_gather | solution.py:63
  410.4 21.1 %fusion.28 = f32[448,4608]{0,1:T(8,128)} fusion(bf16[3072,4608]{1,0:T(8,128)(2,1)} %all-gather.6.cloned.1.call-done, f32[3072]{0:T(1024)S(1)} %copy-done.11, bf16[448,3072]{1,0:T(8,128)(2,1)S(1)} %copy-done.2, f32[448]{0:T(512)S(1)} %add_rsqrt_fusion.2, f32[448]{0:T(512)S(1)} %broadcast_multiply_fusion.8), kind=kOutput, calls=%fused_computation.65 | convolution fusion | flops 12690456576 | bytes 39337472 | tf_op jit(solution)/shard_map/dot_general | solution.py:68
  431.4 12.0 %reshape.160 = f32[4,112,12,3,128]{1,0,4,3,2:T(4,128)} reshape(f32[448,4608]{0,1:T(8,128)} %fusion.28) | data formatting | bytes 16515072 | tf_op jit(solution)/shard_map/reshape | solution.py:68
  445.9 5.4 fusion.49
  453.6 3.1 copy.37
  458.5 3.1 copy.36
  463.6 3.2 fusion.17
  471.0 8.2 bitcast_reduce_fusion
  479.2 8.3 bitcast_reduce_fusion.1
  487.5 3.5 fusion.22
  491.1 3.6 fusion.21
  496.8 8.2 copy.29
  505.1 8.9 convert_element_type.71
  513.9 22.0 %convolution_convert_fusion.2 = bf16[448,3072]{1,0:T(8,128)(2,1)} fusion(bf16[448,4608]{0,1:T(8,128)(2,1)} %convert_element_type.71, bf16[3072,4608]{1,0:T(8,128)(2,1)} %all-gather.6.cloned.1.call-done), kind=kOutput, calls=%fused_computation.11 | convolution fusion | flops 12684951552 | bytes 35192832 | tf_op jit(solution)/shard_map/dot_general | solution.py:133
  541.5 11.0 %convolution_convert_fusion.3 = bf16[448,3072]{1,0:T(8,128)(2,1)} fusion(bf16[3072,1536]{1,0:T(8,128)(2,1)} %all-gather.8.cloned.1.call-done, bf16[56,8,12,128]{3,2,1,0:T(8,128)(2,1)S(1)} %bitcast.124), kind=kOutput, calls=%fused_computation.12 | convolution fusion | flops 4229234688 | bytes 13565952 | tf_op jit(solution)/shard_map/dot_general | solution.py:86
  552.6 9.9 convolution_convert_fusion.1
  562.5 22.1 %convolution_convert_fusion = bf16[3072,4608]{1,0:T(8,128)(2,1)} fusion(bf16[448,4608]{0,1:T(8,128)(2,1)} %convert_element_type.71, f32[3072]{0:T(1024)S(1)} %copy-done.11, bf16[448,3072]{1,0:T(8,128)(2,1)S(1)} %copy-done.3, f32[448]{0:T(512)S(1)} %add_rsqrt_fusion.2, f32[448]{0:T(512)S(1)} %broadcast_multiply_fusion.8), kind=kOutput, calls=%fused_computation.1 | convolution fusion | flops 12704612352 | bytes 35208704 | tf_op jit(solution)/shard_map/dot_general | solution.py:119
  584.6 26.2 %pad_maximum_fusion = bf16[3072,6144]{1,0:T(8,128)(2,1)} fusion(bf16[3072,1536]{1,0:T(8,128)(2,1)} %convolution_convert_fusion.1, bf16[3072,4608]{1,0:T(8,128)(2,1)} %convolution_convert_fusion), kind=kLoop, calls=%fused_computation | loop fusion | flops 75497472 | bytes 75497472 | tf_op jit(solution)/shard_map/concatenate | solution.py:126
  613.3 3.4 fusion.18
  618.3 36.8 %reduce-scatter.3.cloned.1.call-done = bf16[448,1536]{1,0:T(8,128)(2,1)} async-done(((bf16[448,3072]{1,0:T(8,128)(2,1)}), bf16[448,1536]{1,0:T(8,128)(2,1)}) %reduce-scatter.3.cloned.1.call-update) | async-done | bytes 1376272 | tf_op jit(solution)/shard_map/reduce_scatter | solution.py:89
  655.1 2.7 select_convert_fusion
  657.9 369.2 %reduce-scatter.5.cloned.1.call-done = bf16[192,6144]{1,0:T(8,128)(2,1)} async-done(((bf16[3072,6144]{1,0:T(8,128)(2,1)}), bf16[192,6144]{1,0:T(8,128)(2,1)}) %reduce-scatter.5.cloned.1.call-update) | async-done | bytes 2359312 | tf_op jit(solution)/shard_map/reduce_scatter | solution.py:125
  (91 shorter events, 49.5 us)
Async XLA Ops:
  7.2 5.4 copy-start.7
  7.2 2.2 copy-start.14
  7.2 176.2 %all-gather.4.cloned.1.call-start = ((), (), s32[]{:S(2)}) async-start(), calls=%async_computation.2 | async-start | bytes 4128768 | tf_op jit(solution)/shard_map/all_gather | solution.py:61
  8.8 3.7 collective-permute-start
  13.0 33.4 %collective-permute-start.1 = (bf16[448,1536]{1,0:T(8,128)(2,1)S(1)}, bf16[448,1536]{1,0:T(8,128)(2,1)S(1)}, u32[]{:S(2)}, u32[]{:S(2)}) collective-permute-start(bf16[448,1536]{1,0:T(8,128)(2,1)S(1)} %broadcast_select_fusion.1), channel_id=1, source_target_pairs={{0,4},{2,6},{4,0},{6,2},{8,12},{10,14},{12,8},{14,10},{16,20},{18,... | collective-permute-start | bytes 4128776 | tf_op jit(solution)/shard_map/ppermute | solution.py:12
  46.6 35.0 %copy-start.12 = (s32[16,4]{0,1:T(4,128)S(1)}, s32[16,4]{0,1:T(4,128)}, u32[]{:S(2)}) copy-start(s32[16,4]{0,1:T(4,128)} %param.12) | copy-start | bytes 772
  46.6 32.1 %collective-permute-start.2 = (bf16[448,1536]{1,0:T(8,128)(2,1)S(1)}, bf16[448,1536]{1,0:T(8,128)(2,1)S(1)}, u32[]{:S(2)}, u32[]{:S(2)}) collective-permute-start(bf16[448,1536]{1,0:T(8,128)(2,1)S(1)} %broadcast_select_fusion.2), channel_id=1, source_target_pairs={{0,8},{2,10},{4,12},{6,14},{8,0},{10,2},{12,4},{14,6},{16,24},{18,... | collective-permute-start | bytes 4128776 | tf_op jit(solution)/shard_map/ppermute | solution.py:12
  78.9 61.6 %collective-permute-start.3 = (bf16[448,1536]{1,0:T(8,128)(2,1)S(1)}, bf16[448,1536]{1,0:T(8,128)(2,1)S(1)}, u32[]{:S(2)}, u32[]{:S(2)}) collective-permute-start(bf16[448,1536]{1,0:T(8,128)(2,1)S(1)} %broadcast_select_fusion.3), channel_id=1, source_target_pairs={{0,16},{2,18},{4,20},{6,22},{8,24},{10,26},{12,28},{14,30},{16,0},... | collective-permute-start | bytes 4128776 | tf_op jit(solution)/shard_map/ppermute | solution.py:12
  141.8 1.6 copy-start.13
  141.8 125.3 %all-gather.8.cloned.1.call-start = ((), (), s32[]{:S(2)}) async-start(), calls=%async_computation.4 | async-start | bytes 10027008 | tf_op jit(solution)/shard_map/all_gather | solution.py:64
  142.6 267.8 %all-gather.6.cloned.1.call-start = ((), (), s32[]{:S(2)}) async-start(), calls=%async_computation.3 | async-start | bytes 30081024 | tf_op jit(solution)/shard_map/all_gather | solution.py:63
  143.3 470.0 %all-reduce.2.cloned.1.call-start = ((), (), s32[]{:S(2)}) async-start(), calls=%async_computation.6 | async-start | bytes 5505024 | tf_op jit(solution)/shard_map/psum | solution.py:136
  183.4 2.6 copy-start.2
  277.2 133.1 %copy-start.11 = (f32[3072]{0:T(1024)S(1)}, f32[3072]{0:T(1024)}, u32[]{:S(2)}) copy-start(f32[3072]{0:T(1024)} %param.14) | copy-start | bytes 36868
  456.7 1.8 copy-start
  461.6 1.9 copy-start.1
  463.6 3.2 copy-start.8
  466.8 3.4 copy-start.4
  466.8 2.3 copy-start.10
  535.9 1.8 copy-start.5
  536.0 119.2 %reduce-scatter.3.cloned.1.call-start = ((), (), s32[]{:S(2)}) async-start(), calls=%async_computation.5 | async-start | bytes 4128768 | tf_op jit(solution)/shard_map/reduce_scatter | solution.py:89
  540.2 1.3 copy-start.9
  552.5 10.0 copy-start.3
  552.5 474.6 %reduce-scatter.5.cloned.1.call-start = ((), (), s32[]{:S(2)}) async-start(), calls=%async_computation.7 | async-start | bytes 40108032 | tf_op jit(solution)/shard_map/reduce_scatter | solution.py:125
  1027.1 2.4 copy-start.6
Sparse Core Ops, SparseCore 0:
  141.9 41.4 all-gather.3
  185.7 81.4 all-gather.7
  268.8 141.5 all-gather.5
  536.1 77.1 all-reduce.1
  616.1 39.0 reduce-scatter.2
  659.2 367.8 reduce-scatter.4
where the time goes:
time: 1040 us
  waiting for transfers between devices  770 us (74%)
  matrix products  120 us (12%)
  other arithmetic  69.2 us (7%)
  local copies, waits for them, and re-layouts  56.9 us (5%)
  between operations  14.8 us (1%)
    reduce_scatter x1, waiting for transfers between devices, per_device(): lax.psum_scatter(jnp.concatenate([qkv_term, out_term], axis=1).astype(jnp...  369 us
    all_gather x1, waiting for transfers between devices, per_device(): lax.all_gather(qkv_weight, 'fsdp', axis=0, tiled=True)  129 us
    ppermute x4, waiting for transfers between devices, partner_2(): return lax.ppermute(value, axis, pairs)  111 us
    all_gather x1, waiting for transfers between devices, per_device(): lax.all_gather(out_weight, 'fsdp', axis=0, tiled=True)  80.3 us
    all_gather x1, waiting for transfers between devices, per_device(): block_rows = lax.all_gather(packed, 'tp', axis=1, tiled=True)  39.9 us
    reduce_scatter x1, waiting for transfers between devices, per_device(): lax.psum_scatter(partial_value.astype(jnp.bfloat16), 'tp', scatter_dimens...  36.8 us
    concatenate x1, other arithmetic, per_device(): jnp.concatenate([qkv_term, out_term], axis=1).astype(jnp.bfloat16)  26.2 us
    dot_general x1, matrix products, per_device(): lax.dot_general(normed, grad_qkv, (((0,), (0,)), ((), ())), preferred_ele...  22.1 us
  transfers between devices with their start and end apart: 10, of which 9 were waited for; matrix products, arithmetic and copies ran while one was open for 11% of the time, Pallas kernels for 0%

commit v1 on v0

--- a/solution.py
+++ b/solution.py
@@ -1,9 +1,13 @@
+import functools
 import jax
 import jax.numpy as jnp
 from jax import lax
+from jax.experimental import pallas as pl
+from jax.experimental.pallas import tpu as pltpu
 from jax.sharding import PartitionSpec as P
 
 epsilon = 1e-06
+PLANE = 4
 
 
 def partner_2(value, axis, stride):
@@ -140,7 +144,545 @@
     return (attended, grad_rows, grad_qkv_weight, grad_out_weight)
 
 
+def swap_fsdp(value, mask):
+    pairs = [(source, source ^ mask) for source in range(lax.axis_size("fsdp"))]
+    return lax.ppermute(value, "fsdp", pairs)
+
+
+def swap_tp(value):
+    return lax.ppermute(value, "tp", [(0, 1), (1, 0)])
+
+
+def shift_planes(value, step, senders):
+    pairs = [
+        (plane * PLANE + place, (plane + step) * PLANE + place)
+        for plane in senders
+        for place in range(PLANE)
+    ]
+    return lax.ppermute(value, "fsdp", pairs)
+
+
+def after(value, *earlier):
+    return lax.optimization_barrier((value,) + earlier)[0]
+
+
+class PlaneGather:
+    def __init__(self, own, planes, my_plane):
+        self.own, self.planes, self.my_plane = (own, planes, my_plane)
+        self.rights, self.lefts = ([], [])
+        self.right = self.left = own
+
+    def step(self, *earlier):
+        step = len(self.rights) + 1
+        right = after(self.right, *earlier) if earlier else self.right
+        left = after(self.left, *earlier) if earlier else self.left
+        self.right = shift_planes(right, 1, range(step - 1, self.planes - 1))
+        self.left = shift_planes(left, -1, range(1, self.planes - step + 1))
+        self.rights.append(self.right)
+        self.lefts.append(self.left)
+
+    def last(self):
+        return (self.right, self.left)
+
+    def whole(self):
+        own, planes, my_plane = (self.own, self.planes, self.my_plane)
+        whole = jnp.zeros((planes,) + own.shape, own.dtype)
+        whole = lax.dynamic_update_index_in_dim(whole, own, my_plane, 0)
+        for step in range(1, planes):
+            piece = jnp.where(
+                my_plane >= step, self.rights[step - 1], self.lefts[planes - step - 1]
+            )
+            place = lax.rem(my_plane - step + planes, planes)
+            whole = lax.dynamic_update_index_in_dim(whole, piece, place, 0)
+        return whole.reshape((planes * own.shape[0],) + own.shape[1:])
+
+
+def add_rounded(left, right):
+    return (left.astype(jnp.float32) + right.astype(jnp.float32)).astype(jnp.bfloat16)
+
+
+class PlaneReduce:
+    def __init__(self, terms, planes, my_plane):
+        self.terms, self.planes, self.my_plane = (terms, planes, my_plane)
+        self.right = self.left = None
+        self.steps = 0
+
+    def part(self, place):
+        return lax.dynamic_index_in_dim(
+            self.terms, jnp.clip(place, 0, self.planes - 1), 0, keepdims=False
+        )
+
+    def step(self, *earlier):
+        self.steps += 1
+        step, planes = (self.steps, self.planes)
+        right = self.part(self.my_plane + planes - step)
+        left = self.part(self.my_plane - planes + step)
+        if step > 1:
+            right = add_rounded(self.right, right)
+            left = add_rounded(self.left, left)
+        if earlier:
+            right = after(right, *earlier)
+            left = after(left, *earlier)
+        self.right = shift_planes(right, 1, range(0, step))
+        self.left = shift_planes(left, -1, range(planes - step, planes))
+
+    def last(self):
+        return (self.right, self.left)
+
+    def total(self):
+        total = self.part(self.my_plane).astype(jnp.float32) + self.right.astype(jnp.float32)
+        return (total + self.left.astype(jnp.float32)).astype(jnp.bfloat16)
+
+
+def rows_kernel(pick_ref, count_ref, *refs):
+    low_a, low_b, high_a, high_b, gain_ref = refs[:5]
+    normed_ref, stats_ref = refs[-2:]
+    at = pl.program_id(0)
+    rows = low_a.shape[3]
+    half = low_a.shape[4]
+    width = 2 * half
+    live = lax.broadcasted_iota(jnp.int32, (rows, 1), 0) < count_ref[at]
+    near = (pick_ref[at] & 1) == 1
+
+    def read(here, there):
+        value = jnp.where(near, there[0, 0, 0], here[0, 0, 0])
+        return jnp.where(live, value.astype(jnp.float32), 0.0)
+
+    low = read(low_a, low_b)
+    high = read(high_a, high_b)
+    mean = (
+        jnp.sum(low, axis=-1, keepdims=True) + jnp.sum(high, axis=-1, keepdims=True)
+    ) / width
+    low = low - mean
+    high = high - mean
+    variance = (
+        jnp.sum(low * low, axis=-1, keepdims=True) + jnp.sum(high * high, axis=-1, keepdims=True)
+    ) / width
+    factor = lax.rsqrt(variance + epsilon)
+    normed_ref[:, :half] = (low * factor * gain_ref[:, :half]).astype(normed_ref.dtype)
+    normed_ref[:, half:] = (high * factor * gain_ref[:, half:]).astype(normed_ref.dtype)
+    lane = lax.broadcasted_iota(jnp.int32, (rows, stats_ref.shape[1]), 1)
+    stats_ref[...] = jnp.where(lane == 0, mean, factor)
+
+
+def norm_block(here, there, picks, live_counts, norm_gain, my_group, part, parts, before):
+    _, _, slots, rows, half = here.shape
+    width = 2 * half
+    steps = PLANE * slots
+    picks = jnp.concatenate([picks, my_group[None]])
+
+    def source(group_xor):
+        return pl.BlockSpec(
+            (1, 1, 1, rows, half),
+            lambda at, pick, count: (pick[at] >> 1, pick[steps] ^ group_xor, at % slots, 0, 0),
+        )
+
+    out_specs = [
+        pl.BlockSpec((rows, width), lambda at, pick, count: (at + part * steps, 0)),
+        pl.BlockSpec((rows, 128), lambda at, pick, count: (at + part * steps, 0)),
+    ]
+    total = parts * steps * rows
+    extra = [] if before is None else list(before)
+    return pl.pallas_call(
+        rows_kernel,
+        grid_spec=pltpu.PrefetchScalarGridSpec(
+            num_scalar_prefetch=2,
+            grid=(steps,),
+            in_specs=[
+                source(0),
+                source(0),
+                source(1),
+                source(1),
+                pl.BlockSpec((1, width), lambda at, pick, count: (0, 0)),
+            ]
+            + [pl.BlockSpec(memory_space=pl.ANY)] * len(extra),
+            out_specs=out_specs,
+        ),
+        out_shape=[
+            jax.ShapeDtypeStruct((total, width), jnp.bfloat16),
+            jax.ShapeDtypeStruct((total, 128), jnp.float32),
+        ],
+        input_output_aliases={7: 0, 8: 1} if extra else {},
+        compiler_params=pltpu.CompilerParams(vmem_limit_bytes=32 * 1024 * 1024),
+        cost_estimate=pl.CostEstimate(
+            flops=10 * steps * rows * width,
+            bytes_accessed=6 * steps * rows * width,
+            transcendentals=0,
+        ),
+        name="norm_rows",
+    )(picks, live_counts, here, there, here, there, norm_gain[None, :], *extra)
+
+
+def mm(left, right, left_dim, right_dim):
+    return lax.dot_general(
+        left,
+        right,
+        (((left_dim,), (right_dim,)), ((), ())),
+        preferred_element_type=jnp.float32,
+    )
+
+
+def attend_image(projected, grad_mixed, scales, live, rows, head_dim):
+    query_hat, query_factor = norm_rows(projected[:, :head_dim])
+    key_hat, key_factor = norm_rows(projected[:, head_dim : 2 * head_dim])
+    query_scale = scales[0:1, :]
+    key_scale = scales[1:2, :]
+    query = (query_hat * query_scale).astype(jnp.bfloat16)
+    key_rows = (key_hat * key_scale).astype(jnp.bfloat16)
+    values = projected[:, 2 * head_dim :].astype(jnp.bfloat16)
+    row_id = lax.broadcasted_iota(jnp.int32, (rows, rows), 0)
+    col_id = lax.broadcasted_iota(jnp.int32, (rows, rows), 1)
+    allowed = ((row_id < live) & (col_id < live)) | (row_id == col_id)
+    raised = jnp.where(allowed, jnp.exp(mm(query, key_rows, 1, 1)), 0.0)
+    attention = raised / jnp.sum(raised, axis=-1, keepdims=True)
+    rounded = attention.astype(jnp.bfloat16)
+    mixed = mm(rounded, values, 1, 0).astype(jnp.bfloat16)
+    grad_value = mm(rounded, grad_mixed, 0, 0)
+    grad_attention = mm(grad_mixed, values, 1, 1)
+    grad_scores = attention * (
+        grad_attention - jnp.sum(attention * grad_attention, axis=-1, keepdims=True)
+    )
+    grad_scores = grad_scores.astype(jnp.bfloat16)
+    grad_query = mm(grad_scores, key_rows, 1, 0)
+    grad_key = mm(grad_scores, query, 0, 0)
+    query_grad = norm_back(grad_query * query_scale, query_hat, query_factor)
+    key_grad = norm_back(grad_key * key_scale, key_hat, key_factor)
+    return (mixed, query_grad, key_grad, grad_value)
+
+
+def attention_kernel(per_step, count_ref, proj_ref, grad_ref, scale_ref, mixed_ref, back_ref):
+    at = pl.program_id(0)
+    rows = proj_ref.shape[0] // per_step
+    head_dim = grad_ref.shape[1]
+    scales = scale_ref[...]
+    for image in range(per_step):
+        span = slice(image * rows, (image + 1) * rows)
+        mixed, query_grad, key_grad, grad_value = attend_image(
+            proj_ref[span, :],
+            grad_ref[span, :],
+            scales,
+            count_ref[at * per_step + image],
+            rows,
+            head_dim,
+        )
+        mixed_ref[span, :] = mixed
+        back_ref[span, :head_dim] = query_grad.astype(jnp.bfloat16)
+        back_ref[span, head_dim : 2 * head_dim] = key_grad.astype(jnp.bfloat16)
+        back_ref[span, 2 * head_dim :] = grad_value.astype(jnp.bfloat16)
+
+
+def attend(projected, grad_mixed, scales, live_counts, rows):
+    total, head_dim = grad_mixed.shape
+    image_count = total // rows
+    per_step = 4
+    block = per_step * rows
+    return pl.pallas_call(
+        functools.partial(attention_kernel, per_step),
+        grid_spec=pltpu.PrefetchScalarGridSpec(
+            num_scalar_prefetch=1,
+            grid=(image_count // per_step,),
+            in_specs=[
+                pl.BlockSpec((block, 3 * head_dim), lambda at, count: (at, 0)),
+                pl.BlockSpec((block, head_dim), lambda at, count: (at, 0)),
+                pl.BlockSpec((2, head_dim), lambda at, count: (0, 0)),
+            ],
+            out_specs=[
+                pl.BlockSpec((block, head_dim), lambda at, count: (at, 0)),
+                pl.BlockSpec((block, 3 * head_dim), lambda at, count: (at, 0)),
+            ],
+        ),
+        out_shape=[
+            jax.ShapeDtypeStruct((total, head_dim), jnp.bfloat16),
+            jax.ShapeDtypeStruct((total, 3 * head_dim), jnp.bfloat16),
+        ],
+        compiler_params=pltpu.CompilerParams(vmem_limit_bytes=32 * 1024 * 1024),
+        cost_estimate=pl.CostEstimate(
+            flops=12 * total * rows * head_dim,
+            bytes_accessed=12 * total * head_dim * 2,
+            transcendentals=total * rows,
+        ),
+        name="attend_images",
+    )(live_counts, projected, grad_mixed, scales)
+
+
+def scatter_partial(partial, share_width, my_group, *earlier):
+    parts, _, rows, width = partial.shape
+
+    def block(place):
+        return partial[:, place].reshape(parts * rows, width)
+
+    sent_far, sent_near = (block(3), block(1))
+    if earlier:
+        sent_far = after(sent_far, *earlier)
+        sent_near = after(sent_near, *earlier)
+    got_far = swap_fsdp(sent_far, 1)
+    got_near = swap_fsdp(sent_near, 1)
+    far = add_rounded(block(2), got_far)
+    near = add_rounded(block(0), got_near)
+
+    def halves(value):
+        mine = lax.dynamic_slice_in_dim(value, my_group * share_width, share_width, 1)
+        other = lax.dynamic_slice_in_dim(value, (1 - my_group) * share_width, share_width, 1)
+        return (mine, other)
+
+    far_mine, far_other = halves(far)
+    far_got = swap_tp(far_other)
+    near_mine, near_other = halves(near)
+    near_got = swap_tp(after(near_other, far_got))
+    far_sum = swap_fsdp(add_rounded(far_mine, far_got), 2)
+    return (
+        near_mine.astype(jnp.float32)
+        + near_got.astype(jnp.float32)
+        + far_sum.astype(jnp.float32)
+    )
+
+
+def per_plane(patches, cotangent, counts, masks, norm_gain, qk_gain, qkv_weight, out_weight):
+    replicas = lax.axis_size("fsdp")
+    groups = lax.axis_size("tp")
+    planes = replicas // PLANE
+    my_replica = lax.axis_index("fsdp")
+    my_group = lax.axis_index("tp")
+    my_plane = my_replica // PLANE
+    my_place = lax.rem(my_replica, PLANE)
+    tok_rows = patches.shape[0]
+    images = counts.shape[1]
+    slot_rows = tok_rows // images
+    model_width = norm_gain.shape[0]
+    share_width = model_width // groups
+    head_dim = qk_gain.shape[1]
+    shard_rows = qkv_weight.shape[0]
+    local_heads = out_weight.shape[1] // head_dim
+    heads = local_heads // PLANE
+    qkv_width = 3 * head_dim
+    head_width = 4 * head_dim
+    parts = 2
+    slots = images // parts
+    part_rows = slots * slot_rows
+
+    replica_ids = jnp.arange(replicas, dtype=jnp.int32)
+    relative = jnp.arange(PLANE, dtype=jnp.int32)
+    sources = (my_replica ^ relative)[:, None] ^ masks[None, :]
+    live_counts = jnp.sum(
+        jnp.where(replica_ids[:, None, None] == sources[None], counts[:, None, :], 0), axis=0
+    ).astype(jnp.int32)
+    picks = (relative[:, None] ^ (masks & (PLANE - 1))[None, :]).astype(jnp.int32)
+    places = jnp.arange(slot_rows, dtype=jnp.int32)
+    is_live = (places[None, :] < live_counts[0][:, None]).reshape(tok_rows)
+
+    def by_part(table):
+        return jnp.transpose(table.reshape(PLANE, parts, slots), (1, 0, 2)).reshape(parts, -1)
+
+    part_counts = by_part(live_counts)
+    part_picks = by_part(picks)
+    flat_counts = part_counts.reshape(-1)
+
+    holding = lax.dynamic_slice_in_dim(patches, my_group * share_width, share_width, 1)
+    holding = holding.reshape(parts, slots, slot_rows, share_width)
+    moved = [holding[part] for part in range(parts)]
+    for bit_place in range(2, replicas.bit_length() - 1):
+        previous = None
+        for part in range(parts):
+            piece = moved[part] if previous is None else after(moved[part], previous)
+            partner = swap_fsdp(piece, 2**bit_place)
+            moving = jnp.right_shift(masks[part * slots : (part + 1) * slots], bit_place) & 1
+            moved[part] = jnp.where((moving == 1)[:, None, None], partner, moved[part])
+            previous = partner
+
+    def head_columns(place):
+        qkv_part = lax.dynamic_slice_in_dim(
+            qkv_weight, place * heads * qkv_width, heads * qkv_width, 1
+        ).reshape(shard_rows, heads, qkv_width)
+        out_part = lax.dynamic_slice_in_dim(
+            out_weight, place * heads * head_dim, heads * head_dim, 1
+        ).reshape(shard_rows, heads, head_dim)
+        return jnp.concatenate([qkv_part, out_part], axis=2).reshape(
+            shard_rows, heads * head_width
+        )
+
+    shards = [head_columns(my_place)]
+    for step in range(1, PLANE):
+        shards.append(swap_fsdp(head_columns(my_place ^ step), step))
+    plane_shard = jnp.zeros((PLANE, shard_rows, heads * head_width), qkv_weight.dtype)
+    for step in range(PLANE):
+        plane_shard = lax.dynamic_update_index_in_dim(
+            plane_shard, shards[step], my_place ^ step, 0
+        )
+    plane_shard = plane_shard.reshape(PLANE * shard_rows, heads * head_width)
+
+    upstream_own = jnp.where(is_live[:, None], cotangent, jnp.zeros((), cotangent.dtype))
+    up_own = [upstream_own[:part_rows], upstream_own[part_rows:]]
+    up_near = swap_fsdp(upstream_own, 1)
+    up_far = [swap_fsdp(after(up_own[0], shards[2], shards[3]), 2), None]
+
+    here, there = ([], [])
+    for part in range(parts):
+        own = moved[part]
+        over = swap_tp(own)
+        far = swap_fsdp(own, 2)
+        far_over = swap_tp(far)
+        here.append(
+            jnp.stack([own, over, far, far_over]).reshape(
+                2, 2, slots, slot_rows, share_width
+            )
+        )
+        there.append(swap_fsdp(here[part], 1))
+    up_far[1] = swap_fsdp(after(up_own[1], far), 2)
+    up_both = [swap_fsdp(value, 1) for value in up_far]
+    upstream = jnp.concatenate(
+        [
+            value
+            for part in range(parts)
+            for value in (
+                up_own[part],
+                up_near[part * part_rows : (part + 1) * part_rows],
+                up_far[part],
+                up_both[part],
+            )
+        ]
+    )
+
+    shard_of = [
+        plane_shard[:, head * head_width : (head + 1) * head_width] for head in range(heads)
+    ]
+    gathers = [PlaneGather(shard, planes, my_plane) for shard in shard_of]
+    reduces = [None] * heads
+    gathers[0].step(moved[1])
+    for step in range(2, planes):
+        gathers[0].step()
+
+    normed_stats = None
+    for part in range(parts):
+        normed_stats = norm_block(
+            here[part],
+            there[part],
+            part_picks[part],
+            part_counts[part],
+            norm_gain,
+            my_group,
+            part,
+            parts,
+            normed_stats,
+        )
+    normed, stats = normed_stats
+
+    scales = jnp.concatenate([qk_gain[0:1] * head_dim ** (-0.5), qk_gain[1:2]])
+    weights, mixed_parts, back_parts, grads = ([], [], [], [])
+    for head in range(heads):
+        weight = gathers[head].whole()
+        weights.append(weight)
+        if head + 1 < heads:
+            gathers[head + 1].step(*gathers[head].last())
+        out_head = weight[:, qkv_width:]
+        grad_mixed = mm(upstream, out_head, 1, 0).astype(jnp.bfloat16)
+        projected = mm(normed, weight[:, :qkv_width], 1, 0)
+        if head > 0:
+            projected = after(projected, *reduces[head - 1].last())
+            reduces[head - 1].step()
+        mixed, back = attend(projected, grad_mixed, scales, flat_counts, slot_rows)
+        mixed_parts.append(mixed)
+        back_parts.append(back)
+        frontier = []
+        if head + 1 < heads:
+            frontier += gathers[head + 1].last()
+        if head > 0:
+            frontier += reduces[head - 1].last()
+        held_back, held_mixed = (back, mixed)
+        if frontier:
+            held_back = after(back, *frontier)
+            held_mixed = after(mixed, *frontier)
+        if head + 1 < heads:
+            for step in range(2, planes):
+                gathers[head + 1].step(mixed)
+        if head > 0:
+            reduces[head - 1].step(mixed)
+        qkv_term = mm(normed, held_back, 0, 0).astype(jnp.bfloat16)
+        out_term = mm(upstream, held_mixed, 0, 0).astype(jnp.bfloat16)
+        terms = jnp.concatenate([qkv_term, out_term], axis=1).reshape(
+            planes, PLANE * shard_rows, head_width
+        )
+        reduces[head] = PlaneReduce(terms, planes, my_plane)
+        reduces[head].step()
+    while reduces[-1].steps < planes - 1:
+        reduces[-1].step()
+
+    back_all = jnp.concatenate(back_parts, axis=1)
+    qkv_all = jnp.concatenate([weight[:, :qkv_width] for weight in weights], axis=1)
+    partial_back = mm(back_all, qkv_all, 1, 1).astype(jnp.bfloat16)
+    grad_normed = scatter_partial(
+        partial_back.reshape(parts, PLANE, part_rows, model_width), share_width, my_group
+    )
+    mixed_all = jnp.concatenate(mixed_parts, axis=1)
+    out_all = jnp.concatenate([weight[:, qkv_width:] for weight in weights], axis=1)
+    partial_out = mm(mixed_all, out_all, 1, 1).astype(jnp.bfloat16)
+    attended = scatter_partial(
+        partial_out.reshape(parts, PLANE, part_rows, model_width), share_width, my_group
+    )
+    attended = jnp.where(is_live[:, None], attended, 0.0).astype(jnp.bfloat16)
+
+    def own_slot(part, slot):
+        pick = part_picks[part, slot]
+        mine = lax.dynamic_index_in_dim(here[part][:, 0, slot], pick >> 1, 0, keepdims=False)
+        other = lax.dynamic_index_in_dim(there[part][:, 0, slot], pick >> 1, 0, keepdims=False)
+        return jnp.where((pick & 1) == 1, other, mine)
+
+    own_rows = jnp.concatenate(
+        [own_slot(part, slot) for part in range(parts) for slot in range(slots)]
+    ).astype(jnp.float32)
+    own_rows = jnp.where(is_live[:, None], own_rows, 0.0)
+    own_stats = jnp.concatenate(
+        [
+            stats[part * PLANE * part_rows : part * PLANE * part_rows + part_rows, 0:2]
+            for part in range(parts)
+        ]
+    )
+    mean = own_stats[:, 0:1]
+    factor = own_stats[:, 1:2]
+    centred = (own_rows - mean) * factor
+    gain_share = lax.dynamic_slice_in_dim(norm_gain, my_group * share_width, share_width, 0)
+    weighted = grad_normed * gain_share
+    sums = jnp.stack([jnp.sum(weighted, axis=-1), jnp.sum(weighted * centred, axis=-1)])
+    sums = (sums + swap_tp(sums)) / model_width
+    grad_rows = factor * (weighted - sums[0][:, None] - centred * sums[1][:, None])
+    grad_rows = grad_rows.astype(jnp.bfloat16)
+
+    def bring_home(sums_of):
+        summed = jnp.stack(sums_of).reshape(
+            len(sums_of), PLANE, shard_rows, head_width
+        )
+        blocks = []
+        for step in range(PLANE):
+            block = lax.dynamic_index_in_dim(summed, my_place ^ step, 1, keepdims=False)
+            blocks.append(block if step == 0 else swap_fsdp(block, step))
+        return jnp.stack(blocks)
+
+    early = bring_home([reduce.total() for reduce in reduces[:-1]])
+    late = bring_home([reduces[-1].total()])
+    stacked = jnp.concatenate([early, late], axis=1)
+    stacked = jnp.take(stacked, my_place ^ relative, axis=0).astype(jnp.float32)
+    stacked = jnp.transpose(stacked, (2, 0, 1, 3))
+    grad_qkv_weight = stacked[..., :qkv_width].reshape(shard_rows, local_heads * qkv_width)
+    grad_out_weight = stacked[..., qkv_width:].reshape(shard_rows, local_heads * head_dim)
+    return (attended, grad_rows, grad_qkv_weight, grad_out_weight)
+
+
 def solution(mesh):
+    def body(patches, cotangent, counts, masks, norm_gain, qk_gain, qkv_weight, out_weight):
+        replicas = mesh.shape["fsdp"]
+        local_heads = out_weight.shape[1] // qk_gain.shape[1]
+        planar = (
+            mesh.shape["tp"] == 2
+            and replicas == 4 * PLANE
+            and replicas & (replicas - 1) == 0
+            and local_heads % PLANE == 0
+            and qk_gain.shape[1] == 128
+            and counts.shape[1] == 4
+        )
+        plan = per_plane if planar else per_device
+        return plan(
+            patches, cotangent, counts, masks, norm_gain, qk_gain, qkv_weight, out_weight
+        )
+
     in_specs = (
         P("fsdp", None),
         P("fsdp", None),
@@ -153,5 +695,5 @@
     )
     out_specs = (P("fsdp", "tp"), P("fsdp", "tp"), P("fsdp", "tp"), P("fsdp", "tp"))
     return jax.shard_map(
-        per_device, mesh=mesh, in_specs=in_specs, out_specs=out_specs, check_vma=False
-    )
+        body, mesh=mesh, in_specs=in_specs, out_specs=out_specs, check_vma=False
+    )

time: 1040 us -> 671 us (0.65)
  waiting for transfers between devices: 770 us -> 204 us
  starting transfers between devices: 7.9 us -> 136 us
  local copies, waits for them, and re-layouts: 56.9 us -> 119 us
  Pallas kernels: 0 us -> 40.2 us
  matrix products: 120 us -> 87.7 us
    reduce_scatter x2 -> x0, waiting for transfers between devices: 406 us -> none  [the longest x1 369 us: per_device(): lax.psum_scatter(jnp.concatenate([qkv_term, out_term], axis=1).astype(jnp...]
    all_gather x3 -> x0, waiting for transfers between devices: 249 us -> none  [the longest x1 129 us: per_device(): lax.all_gather(qkv_weight, 'fsdp', axis=0, tiled=True)]
    ppermute x4 -> x73, starting transfers between devices: 7.66 us -> 136 us  [the longest x36 109 us: shift_planes(): return lax.ppermute(value, 'fsdp', pairs)]
    ppermute x4 -> x73, waiting for transfers between devices: 111 us -> 204 us  [the longest x28 92.7 us: swap_fsdp(): return lax.ppermute(value, 'fsdp', pairs)]
    pallas_call x0 -> x5, Pallas kernels: none -> 40.2 us  [the longest x3 30.7 us: attend(): pl.pallas_call(functools.partial(attention_kernel, per_step), grid_spec=p...]
    slice x3 -> x28, local copies, waits for them, and re-layouts: 6.98 us -> 47.1 us  [the longest x2 10.5 us: block(): return partial[:, place].reshape(parts * rows, width)]
    dot_general x12 -> x14, matrix products: 120 us -> 87.7 us  [mm(): lax.dot_general(left, right, (((left_dim,), (right_dim,)), ((), ())), pre...]
    convert_element_type x3 -> x17, other arithmetic: 5.15 us -> 32 us  [the longest x12 20.5 us: add_rounded(): (left.astype(jnp.float32) + right.astype(jnp.float32)).astype(jnp.bfloat16)]
  transfers between devices with their start and end apart: 10 -> 73, of which waited for: 9 -> 19; matrix products, arithmetic and copies ran while one was open for 11% -> 35% of each run, Pallas kernels for 0% -> 6%
where the time goes in v1:
time: 671 us; the launch traced here: 661 us
  waiting for transfers between devices  204 us (30%)
  starting transfers between devices  136 us (20%)
  local copies, waits for them, and re-layouts  119 us (18%)
  matrix products  87.7 us (13%)
  other arithmetic  66.4 us (10%)
  Pallas kernels  40.2 us (6%)
  between operations  8.39 us (1%)
    ppermute x36, starting transfers between devices, shift_planes(): return lax.ppermute(value, 'fsdp', pairs)  109 us
    ppermute x28, waiting for transfers between devices, swap_fsdp(): return lax.ppermute(value, 'fsdp', pairs)  92.7 us
    dot_general x14, matrix products, mm(): lax.dot_general(left, right, (((left_dim,), (right_dim,)), ((), ())), pre...  87.7 us
    ppermute x9, waiting for transfers between devices, swap_tp(): return lax.ppermute(value, 'tp', [(0, 1), (1, 0)])  60.5 us
    ppermute x36, waiting for transfers between devices, shift_planes(): return lax.ppermute(value, 'fsdp', pairs)  50.8 us
    pallas_call x3, Pallas kernels, attend(): pl.pallas_call(functools.partial(attention_kernel, per_step), grid_spec=p...  30.7 us
    convert_element_type x12, other arithmetic, add_rounded(): (left.astype(jnp.float32) + right.astype(jnp.float32)).astype(jnp.bfloat16)  20.5 us
    ppermute x28, starting transfers between devices, swap_fsdp(): return lax.ppermute(value, 'fsdp', pairs)  18.9 us
  transfers between devices with their start and end apart: 73, of which 19 were waited for; matrix products, arithmetic and copies ran while one was open for 35% of the time, Pallas kernels for 6%

profile of v1, /device:TPU:0, one launch (start us, length us, event | category | flops | bytes accessed | tf_op | source)
XLA Modules:
  0.0 660.9 jit_solution(80693194955257657)
XLA Ops:
  51.3 26.8 %collective-permute-done.1 = bf16[2,112,1536]{2,1,0:T(8,128)(2,1)S(1)} collective-permute-done((bf16[2,112,1536]{2,1,0:T(8,128)(2,1)S(1)}, bf16[2,112,1536]{2,1,0:T(8,128)(2,1)S(1)}, u32[]{:S(2)}, u32[]{:S(2)}) %collective-permute-start.1) | collective-permute-done | bytes 688160 | tf_op jit(solution)/shard_map/ppermute | solution.py:149
  83.9 26.8 %collective-permute-done.3 = bf16[2,112,1536]{2,1,0:T(8,128)(2,1)S(1)} collective-permute-done((bf16[2,112,1536]{2,1,0:T(8,128)(2,1)S(1)}, bf16[2,112,1536]{2,1,0:T(8,128)(2,1)S(1)}, u32[]{:S(2)}, u32[]{:S(2)}) %collective-permute-start.3) | collective-permute-done | bytes 688160 | tf_op jit(solution)/shard_map/ppermute | solution.py:149
  115.8 16.5 %collective-permute-done.10 = bf16[2,112,1536]{2,1,0:T(8,128)(2,1)S(1)} collective-permute-done((bf16[2,112,1536]{2,1,0:T(8,128)(2,1)S(1)}, bf16[2,112,1536]{2,1,0:T(8,128)(2,1)S(1)}, u32[]{:S(2)}, u32[]{:S(2)}) %collective-permute-start.10) | collective-permute-done | bytes 688160 | tf_op jit(solution)/shard_map/ppermute | solution.py:153
  132.3 16.2 %collective-permute-start.15 = (bf16[768,512]{1,0:T(8,128)(2,1)S(1)}, bf16[768,512]{1,0:T(8,128)(2,1)S(1)}, u32[]{:S(2)}, u32[]{:S(2)}) collective-permute-start(bf16[768,512]{1,0:T(8,128)(2,1)S(1)} %get-tuple-element.48), channel_id=1, source_target_pairs={{0,8},{2,10},{4,12},{6,14},{8,16},{10,18},{12,20},{14,22},{16,24},... | collective-permute-start | bytes 2359304 | tf_op jit(solution)/shard_map/ppermute | solution.py:162
  152.3 10.9 %collective-permute-done.15 = bf16[768,512]{1,0:T(8,128)(2,1)S(1)} collective-permute-done((bf16[768,512]{1,0:T(8,128)(2,1)S(1)}, bf16[768,512]{1,0:T(8,128)(2,1)S(1)}, u32[]{:S(2)}, u32[]{:S(2)}) %collective-permute-start.15) | collective-permute-done | bytes 786464 | tf_op jit(solution)/shard_map/ppermute | solution.py:162
  174.3 8.5 %collective-permute-done.24 = bf16[224,3072]{1,0:T(8,128)(2,1)S(1)} collective-permute-done((bf16[224,3072]{1,0:T(8,128)(2,1)S(1)}, bf16[224,3072]{1,0:T(8,128)(2,1)S(1)}, u32[]{:S(2)}, u32[]{:S(2)}) %collective-permute-start.24) | collective-permute-done | bytes 1376288 | tf_op jit(solution)/shard_map/ppermute | solution.py:149
  184.4 8.4 %collective-permute-done.18 = bf16[768,512]{1,0:T(8,128)(2,1)S(1)} collective-permute-done((bf16[768,512]{1,0:T(8,128)(2,1)S(1)}, bf16[768,512]{1,0:T(8,128)(2,1)S(1)}, u32[]{:S(2)}, u32[]{:S(2)}) %collective-permute-start.18) | collective-permute-done | bytes 786464 | tf_op jit(solution)/shard_map/ppermute | solution.py:162
  194.0 5.7 collective-permute-start.26
  206.6 8.9 %convolution_convert_fusion.10.grad_ref = bf16[1792,128]{1,0:T(8,128)(2,1)S(1)} fusion(bf16[1792,3072]{1,0:T(8,128)(2,1)} %constant_dynamic-update-slice_fusion.1, bf16[3072,512]{1,0:T(8,128)(2,1)S(1)} %bitcast.254), kind=kOutput, calls=%fused_computation.43 | convolution fusion | flops 1409515520 | bytes 12255232 | tf_op jit(solution)/shard_map/dot_general | solution.py:317
  229.5 6.0 fusion.62.proj_ref
  235.6 10.2 %attend_images.3 = (bf16[1792,128]{1,0:T(8,128)(2,1)S(1)}, bf16[1792,384]{1,0:T(8,128)(2,1)S(1)}) custom-call(s32[16]{0:T(128)S(1)} %reshape_reshape.3.count_ref, f32[1792,384]{1,0:T(8,128)S(1)} %fusion.62.proj_ref, bf16[1792,128]{1,0:T(8,128)(2,1)S(1)} %convolution_convert_fusion.10.grad_ref, f32[2,128]{1,0:T(2,128)S(1)} %pad_maximum_fusion.12.scale_ref), custom_call_target="tpu_custom_call" | custom-call | flops 308281344 | bytes 5505024 | tf_op jit(solution)/shard_map/attend_images/pallas_call | solution.py:379
  245.8 6.3 convolution_convert_fusion.7
  253.6 11.5 %collective-permute-start.30 = (bf16[768,512]{1,0:T(8,128)(2,1)}, bf16[768,512]{1,0:T(8,128)(2,1)}, u32[]{:S(2)}, u32[]{:S(2)}) collective-permute-start(bf16[768,512]{1,0:T(8,128)(2,1)} %collective-permute-done.26), channel_id=1, source_target_pairs={{8,16},{10,18},{12,20},{14,22},{16,24},{18,26},{20,28},{22,30},{9,... | collective-permute-start | bytes 2359304 | tf_op jit(solution)/shard_map/ppermute | solution.py:162
  279.0 10.9 %collective-permute-start.32 = (bf16[768,512]{1,0:T(8,128)(2,1)S(1)}, bf16[768,512]{1,0:T(8,128)(2,1)S(1)}, u32[]{:S(2)}, u32[]{:S(2)}) collective-permute-start(bf16[768,512]{1,0:T(8,128)(2,1)S(1)} %get-tuple-element.109), channel_id=1, source_target_pairs={{0,8},{2,10},{4,12},{6,14},{1,9},{3,11},{5,13},{7,15}} | collective-permute-start | bytes 2359304 | tf_op jit(solution)/shard_map/ppermute | solution.py:162
  307.4 7.4 %collective-permute-done.29 = bf16[768,512]{1,0:T(8,128)(2,1)S(1)} collective-permute-done((bf16[768,512]{1,0:T(8,128)(2,1)}, bf16[768,512]{1,0:T(8,128)(2,1)S(1)}, u32[]{:S(2)}, u32[]{:S(2)}) %collective-permute-start.29) | collective-permute-done | bytes 786464 | tf_op jit(solution)/shard_map/ppermute | solution.py:162
  324.7 5.9 fusion.60.proj_ref
  330.6 5.8 convolution_convert_fusion.9.grad_ref
  336.4 10.2 %attend_images.4 = (bf16[1792,128]{1,0:T(8,128)(2,1)S(1)}, bf16[1792,384]{1,0:T(8,128)(2,1)S(1)}) custom-call(s32[16]{0:T(128)S(1)} %reshape_reshape.3.count_ref, f32[1792,384]{1,0:T(8,128)S(1)} %fusion.60.proj_ref, bf16[1792,128]{1,0:T(8,128)(2,1)S(1)} %convolution_convert_fusion.9.grad_ref, f32[2,128]{1,0:T(2,128)S(1)} %pad_maximum_fusion.12.scale_ref), custom_call_target="tpu_custom_call" | custom-call | flops 308281344 | bytes 5505024 | tf_op jit(solution)/shard_map/attend_images/pallas_call | solution.py:379
  372.6 6.1 collective-permute-done.36
  402.8 5.9 fusion.58.proj_ref
  414.6 10.4 %attend_images.5 = (bf16[1792,128]{1,0:T(8,128)(2,1)S(1)}, bf16[1792,384]{1,0:T(8,128)(2,1)S(1)}) custom-call(s32[16]{0:T(128)S(1)} %reshape_reshape.3.count_ref, f32[1792,384]{1,0:T(8,128)S(1)} %fusion.58.proj_ref, bf16[1792,128]{1,0:T(8,128)(2,1)S(1)} %convolution_convert_fusion.8.grad_ref, f32[2,128]{1,0:T(2,128)S(1)} %pad_maximum_fusion.12.scale_ref), custom_call_target="tpu_custom_call" | custom-call | flops 308281344 | bytes 5505024 | tf_op jit(solution)/shard_map/attend_images/pallas_call | solution.py:379
  441.2 6.7 %collective-permute-start.58 = (bf16[768,512]{1,0:T(8,128)(2,1)}, bf16[768,512]{1,0:T(8,128)(2,1)}, u32[]{:S(2)}, u32[]{:S(2)}) collective-permute-start(bf16[768,512]{1,0:T(8,128)(2,1)} %get-tuple-element.78), channel_id=1, source_target_pairs={{0,8},{2,10},{4,12},{6,14},{8,16},{10,18},{12,20},{14,22},{16,24},... | collective-permute-start | bytes 2359304 | tf_op jit(solution)/shard_map/ppermute | solution.py:162
  457.4 20.0 %convolution_convert_fusion = bf16[1792,3072]{1,0:T(8,128)(2,1)} fusion(bf16[3072,384]{1,0:T(8,128)(2,1)} %slice.239, bf16[3072,384]{1,0:T(8,128)(2,1)} %slice.236, bf16[3072,384]{1,0:T(8,128)(2,1)} %slice.229, bf16[1792,384]{1,0:T(8,128)(2,1)} %copy-done.12, bf16[1792,384]{1,0:T(8,128)(2,1)S(1)} %get-tuple-element.68, bf16[1792,384]{1,0:T(8,128)(2,1)S(1)} %copy-done.11), kind=kOutput, calls=%fused_computation.1 | convolution fusion | flops 12722700288 | bytes 22216704 | tf_op jit(solution)/shard_map/dot_general | solution.py:317
  483.4 6.7 %fusion.64 = (bf16[2,1,224,3072]{3,2,1,0:T(8,128)(2,1)S(1)}, bf16[2,1,224,3072]{3,2,1,0:T(8,128)(2,1)S(1)}, bf16[2,1,224,3072]{3,2,1,0:T(8,128)(2,1)}, bf16[2,1,224,3072]{3,2,1,0:T(8,128)(2,1)}) fusion(bf16[2,4,224,3072]{3,2,1,0:T(8,128)(2,1)} %bitcast.263), kind=kLoop, calls=%fused_computation.204 | loop fusion | bytes 22020096 | tf_op jit(solution)/shard_map/slice | solution.py:412
  490.2 7.9 %convolution_convert_fusion.1 = bf16[1792,3072]{1,0:T(8,128)(2,1)S(1)} fusion(bf16[3072,128]{1,0:T(8,128)(2,1)} %slice.240, bf16[3072,128]{1,0:T(8,128)(2,1)} %slice.237, bf16[3072,128]{1,0:T(8,128)(2,1)} %slice.234, bf16[1792,128]{1,0:T(8,128)(2,1)S(1)} %copy-done.16, bf16[1792,128]{1,0:T(8,128)(2,1)S(1)} %copy-done.14, ...), kind=kOutput, calls=%fused_computation.2 | convolution fusion | flops 4244570112 | bytes 14745600 | tf_op jit(solution)/shard_map/dot_general | solution.py:317
  510.8 8.9 %collective-permute-done.66 = bf16[768,512]{1,0:T(8,128)(2,1)S(1)} collective-permute-done((bf16[768,512]{1,0:T(8,128)(2,1)S(1)}, bf16[768,512]{1,0:T(8,128)(2,1)S(1)}, u32[]{:S(2)}, u32[]{:S(2)}) %collective-permute-start.66) | collective-permute-done | bytes 786464 | tf_op jit(solution)/shard_map/ppermute | solution.py:162
  539.6 24.1 %collective-permute-done.51 = bf16[448,1536]{1,0:T(8,128)(2,1)S(1)} collective-permute-done((bf16[448,1536]{1,0:T(8,128)(2,1)S(1)}, bf16[448,1536]{1,0:T(8,128)(2,1)S(1)}, u32[]{:S(2)}, u32[]{:S(2)}) %collective-permute-start.51) | collective-permute-done | bytes 1376288 | tf_op jit(solution)/shard_map/ppermute | solution.py:153
  574.3 27.5 %collective-permute-done.71 = bf16[1,192,512]{2,1,0:T(8,128)(2,1)S(1)} collective-permute-done((bf16[1,192,512]{2,1,0:T(8,128)(2,1)}, bf16[1,192,512]{2,1,0:T(8,128)(2,1)S(1)}, u32[]{:S(2)}, u32[]{:S(2)}) %collective-permute-start.71) | collective-permute-done | bytes 196640 | tf_op jit(solution)/shard_map/ppermute | solution.py:149
  614.4 12.2 %collective-permute-done.52 = bf16[448,1536]{1,0:T(8,128)(2,1)} collective-permute-done((bf16[448,1536]{1,0:T(8,128)(2,1)}, bf16[448,1536]{1,0:T(8,128)(2,1)}, u32[]{:S(2)}, u32[]{:S(2)}) %collective-permute-start.52) | collective-permute-done | bytes 1376288 | tf_op jit(solution)/shard_map/ppermute | solution.py:153
  638.1 6.6 copy.146
  644.6 6.5 reshape.303
  654.6 5.7 multiply_convert_fusion
  (426 shorter events, 294.5 us)
Async XLA Ops:
  3.1 43.3 %collective-permute-start = (bf16[2,112,1536]{2,1,0:T(8,128)(2,1)}, bf16[2,112,1536]{2,1,0:T(8,128)(2,1)}, u32[]{:S(2)}, u32[]{:S(2)}) collective-permute-start(bf16[2,112,1536]{2,1,0:T(8,128)(2,1)} %bitcast.6), channel_id=1, source_target_pairs={{0,8},{2,10},{4,12},{6,14},{8,0},{10,2},{12,4},{14,6},{16,24},{18,... | collective-permute-start | bytes 2064392 | tf_op jit(solution)/shard_map/ppermute | solution.py:149
  20.3 92.7 %collective-permute-start.21 = (bf16[448,3072]{1,0:T(8,128)(2,1)S(1)}, bf16[448,3072]{1,0:T(8,128)(2,1)}, u32[]{:S(2)}, u32[]{:S(2)}) collective-permute-start(bf16[448,3072]{1,0:T(8,128)(2,1)S(1)} %broadcast_select_fusion), channel_id=1, source_target_pairs={{0,2},{2,0},{4,6},{6,4},{8,10},{10,8},{12,14},{14,12},{16,18},{18,... | collective-permute-start | bytes 8257544 | tf_op jit(solution)/shard_map/ppermute | solution.py:149
  40.0 43.9 %collective-permute-start.22 = (bf16[224,3072]{1,0:T(8,128)(2,1)S(1)}, bf16[224,3072]{1,0:T(8,128)(2,1)S(1)}, u32[]{:S(2)}, u32[]{:S(2)}) collective-permute-start(bf16[224,3072]{1,0:T(8,128)(2,1)S(1)} %get-tuple-element.49), channel_id=1, source_target_pairs={{0,4},{2,6},{4,0},{6,2},{8,12},{10,14},{12,8},{14,10},{16,20},{18,... | collective-permute-start | bytes 4128776 | tf_op jit(solution)/shard_map/ppermute | solution.py:149
  83.9 66.2 %collective-permute-start.23 = (bf16[224,3072]{1,0:T(8,128)(2,1)S(1)}, bf16[224,3072]{1,0:T(8,128)(2,1)S(1)}, u32[]{:S(2)}, u32[]{:S(2)}) collective-permute-start(bf16[224,3072]{1,0:T(8,128)(2,1)S(1)} %collective-permute-done.22), channel_id=1, source_target_pairs={{0,2},{2,0},{4,6},{6,4},{8,10},{10,8},{12,14},{14,12},{16,18},{18,... | collective-permute-start | bytes 4128776 | tf_op jit(solution)/shard_map/ppermute | solution.py:149
  110.9 39.2 %collective-permute-start.5 = (bf16[2,112,1536]{2,1,0:T(8,128)(2,1)S(1)}, bf16[2,112,1536]{2,1,0:T(8,128)(2,1)S(1)}, u32[]{:S(2)}, u32[]{:S(2)}) collective-permute-start(bf16[2,112,1536]{2,1,0:T(8,128)(2,1)S(1)} %broadcast_select_fusion.4), channel_id=1, source_target_pairs={{0,4},{2,6},{4,0},{6,2},{8,12},{10,14},{12,8},{14,10},{16,20},{18,... | collective-permute-start | bytes 2064392 | tf_op jit(solution)/shard_map/ppermute | solution.py:149
  111.0 39.6 %collective-permute-start.4 = (bf16[2,112,1536]{2,1,0:T(8,128)(2,1)S(1)}, bf16[2,112,1536]{2,1,0:T(8,128)(2,1)S(1)}, u32[]{:S(2)}, u32[]{:S(2)}) collective-permute-start(bf16[2,112,1536]{2,1,0:T(8,128)(2,1)S(1)} %broadcast_select_fusion.4), channel_id=1, source_target_pairs={{0,1},{1,0},{2,3},{3,2},{4,5},{5,4},{6,7},{7,6},{8,9},{9,8},{10,11... | collective-permute-start | bytes 2064392 | tf_op jit(solution)/shard_map/ppermute | solution.py:153
  114.5 36.5 %collective-permute-start.16 = (bf16[768,512]{1,0:T(8,128)(2,1)S(1)}, bf16[768,512]{1,0:T(8,128)(2,1)S(1)}, u32[]{:S(2)}, u32[]{:S(2)}) collective-permute-start(bf16[768,512]{1,0:T(8,128)(2,1)S(1)} %get-tuple-element.48), channel_id=1, source_target_pairs={{8,0},{10,2},{12,4},{14,6},{16,8},{18,10},{20,12},{22,14},{24,16},... | collective-permute-start | bytes 2359304 | tf_op jit(solution)/shard_map/ppermute | solution.py:162
  150.1 50.5 %collective-permute-start.11 = (bf16[2,2,2,112,1536]{4,3,2,1,0:T(8,128)(2,1)S(1)}, bf16[2,2,2,112,1536]{4,3,2,1,0:T(8,128)(2,1)S(1)}, u32[]{:S(2)}, u32[]{:S(2)}) collective-permute-start(bf16[2,2,2,112,1536]{4,3,2,1,0:T(8,128)(2,1)S(1)} %bitcast.225), channel_id=1, source_target_pairs={{0,2},{2,0},{4,6},{6,4},{8,10},{10,8},{12,14},{14,12},{16,18},{18,... | collective-permute-start | bytes 8257544 | tf_op jit(solution)/shard_map/ppermute | solution.py:149
  168.6 46.8 %collective-permute-start.7 = (bf16[2,2,2,112,1536]{4,3,2,1,0:T(8,128)(2,1)S(1)}, bf16[2,2,2,112,1536]{4,3,2,1,0:T(8,128)(2,1)S(1)}, u32[]{:S(2)}, u32[]{:S(2)}) collective-permute-start(bf16[2,2,2,112,1536]{4,3,2,1,0:T(8,128)(2,1)S(1)} %bitcast.220), channel_id=1, source_target_pairs={{0,2},{2,0},{4,6},{6,4},{8,10},{10,8},{12,14},{14,12},{16,18},{18,... | collective-permute-start | bytes 8257544 | tf_op jit(solution)/shard_map/ppermute | solution.py:149
  192.7 53.0 %collective-permute-start.27 = (bf16[768,512]{1,0:T(8,128)(2,1)S(1)}, bf16[768,512]{1,0:T(8,128)(2,1)}, u32[]{:S(2)}, u32[]{:S(2)}) collective-permute-start(bf16[768,512]{1,0:T(8,128)(2,1)S(1)} %get-tuple-element.52), channel_id=1, source_target_pairs={{8,0},{10,2},{12,4},{14,6},{16,8},{18,10},{20,12},{22,14},{24,16},... | collective-permute-start | bytes 2359304 | tf_op jit(solution)/shard_map/ppermute | solution.py:162
  194.0 51.7 %collective-permute-start.26 = (bf16[768,512]{1,0:T(8,128)(2,1)S(1)}, bf16[768,512]{1,0:T(8,128)(2,1)}, u32[]{:S(2)}, u32[]{:S(2)}) collective-permute-start(bf16[768,512]{1,0:T(8,128)(2,1)S(1)} %get-tuple-element.52), channel_id=1, source_target_pairs={{0,8},{2,10},{4,12},{6,14},{8,16},{10,18},{12,20},{14,22},{16,24},... | collective-permute-start | bytes 2359304 | tf_op jit(solution)/shard_map/ppermute | solution.py:162
  252.1 44.6 %collective-permute-start.28 = (bf16[768,512]{1,0:T(8,128)(2,1)}, bf16[768,512]{1,0:T(8,128)(2,1)}, u32[]{:S(2)}, u32[]{:S(2)}) collective-permute-start(bf16[768,512]{1,0:T(8,128)(2,1)} %collective-permute-done.27), channel_id=1, source_target_pairs={{8,0},{10,2},{12,4},{14,6},{16,8},{18,10},{20,12},{22,14},{9,1},{1... | collective-permute-start | bytes 2359304 | tf_op jit(solution)/shard_map/ppermute | solution.py:162
  253.6 44.6 %collective-permute-start.30 = (bf16[768,512]{1,0:T(8,128)(2,1)}, bf16[768,512]{1,0:T(8,128)(2,1)}, u32[]{:S(2)}, u32[]{:S(2)}) collective-permute-start(bf16[768,512]{1,0:T(8,128)(2,1)} %collective-permute-done.26), channel_id=1, source_target_pairs={{8,16},{10,18},{12,20},{14,22},{16,24},{18,26},{20,28},{22,30},{9,... | collective-permute-start | bytes 2359304 | tf_op jit(solution)/shard_map/ppermute | solution.py:162
  301.7 45.0 %collective-permute-start.41 = (bf16[768,512]{1,0:T(8,128)(2,1)S(1)}, bf16[768,512]{1,0:T(8,128)(2,1)S(1)}, u32[]{:S(2)}, u32[]{:S(2)}) collective-permute-start(bf16[768,512]{1,0:T(8,128)(2,1)S(1)} %get-tuple-element.106), channel_id=1, source_target_pairs={{16,8},{18,10},{20,12},{22,14},{24,16},{26,18},{28,20},{30,22},{17... | collective-permute-start | bytes 2359304 | tf_op jit(solution)/shard_map/ppermute | solution.py:162
  302.4 44.3 %collective-permute-start.40 = (bf16[768,512]{1,0:T(8,128)(2,1)S(1)}, bf16[768,512]{1,0:T(8,128)(2,1)S(1)}, u32[]{:S(2)}, u32[]{:S(2)}) collective-permute-start(bf16[768,512]{1,0:T(8,128)(2,1)S(1)} %get-tuple-element.107), channel_id=1, source_target_pairs={{0,8},{2,10},{4,12},{6,14},{8,16},{10,18},{12,20},{14,22},{1,9},{3... | collective-permute-start | bytes 2359304 | tf_op jit(solution)/shard_map/ppermute | solution.py:162
  314.8 39.2 %collective-permute-start.35 = (bf16[768,512]{1,0:T(8,128)(2,1)S(1)}, bf16[768,512]{1,0:T(8,128)(2,1)}, u32[]{:S(2)}, u32[]{:S(2)}) collective-permute-start(bf16[768,512]{1,0:T(8,128)(2,1)S(1)} %copy-done.42), channel_id=1, source_target_pairs={{8,0},{10,2},{12,4},{14,6},{16,8},{18,10},{20,12},{22,14},{24,16},... | collective-permute-start | bytes 2359304 | tf_op jit(solution)/shard_map/ppermute | solution.py:162
  316.1 37.9 %collective-permute-start.34 = (bf16[768,512]{1,0:T(8,128)(2,1)S(1)}, bf16[768,512]{1,0:T(8,128)(2,1)}, u32[]{:S(2)}, u32[]{:S(2)}) collective-permute-start(bf16[768,512]{1,0:T(8,128)(2,1)S(1)} %copy-done.42), channel_id=1, source_target_pairs={{0,8},{2,10},{4,12},{6,14},{8,16},{10,18},{12,20},{14,22},{16,24},... | collective-permute-start | bytes 2359304 | tf_op jit(solution)/shard_map/ppermute | solution.py:162
  347.1 33.0 %collective-permute-start.56 = (bf16[768,512]{1,0:T(8,128)(2,1)S(1)}, bf16[768,512]{1,0:T(8,128)(2,1)}, u32[]{:S(2)}, u32[]{:S(2)}) collective-permute-start(bf16[768,512]{1,0:T(8,128)(2,1)S(1)} %get-tuple-element.77), channel_id=1, source_target_pairs={{8,0},{10,2},{12,4},{14,6},{16,8},{18,10},{20,12},{22,14},{24,16},... | collective-permute-start | bytes 2359304 | tf_op jit(solution)/shard_map/ppermute | solution.py:162
  348.6 40.3 %collective-permute-start.55 = (bf16[768,512]{1,0:T(8,128)(2,1)S(1)}, bf16[768,512]{1,0:T(8,128)(2,1)}, u32[]{:S(2)}, u32[]{:S(2)}) collective-permute-start(bf16[768,512]{1,0:T(8,128)(2,1)S(1)} %get-tuple-element.76), channel_id=1, source_target_pairs={{0,8},{2,10},{4,12},{6,14},{8,16},{10,18},{12,20},{14,22},{16,24},... | collective-permute-start | bytes 2359304 | tf_op jit(solution)/shard_map/ppermute | solution.py:162
  355.3 36.5 %collective-permute-start.38 = (bf16[768,512]{1,0:T(8,128)(2,1)}, bf16[768,512]{1,0:T(8,128)(2,1)}, u32[]{:S(2)}, u32[]{:S(2)}) collective-permute-start(bf16[768,512]{1,0:T(8,128)(2,1)} %collective-permute-done.34), channel_id=1, source_target_pairs={{8,16},{10,18},{12,20},{14,22},{16,24},{18,26},{20,28},{22,30},{9,... | collective-permute-start | bytes 2359304 | tf_op jit(solution)/shard_map/ppermute | solution.py:162
  441.2 61.0 %collective-permute-start.58 = (bf16[768,512]{1,0:T(8,128)(2,1)}, bf16[768,512]{1,0:T(8,128)(2,1)}, u32[]{:S(2)}, u32[]{:S(2)}) collective-permute-start(bf16[768,512]{1,0:T(8,128)(2,1)} %get-tuple-element.78), channel_id=1, source_target_pairs={{0,8},{2,10},{4,12},{6,14},{8,16},{10,18},{12,20},{14,22},{16,24},... | collective-permute-start | bytes 2359304 | tf_op jit(solution)/shard_map/ppermute | solution.py:162
  447.8 59.4 %collective-permute-start.60 = (bf16[768,512]{1,0:T(8,128)(2,1)}, bf16[768,512]{1,0:T(8,128)(2,1)}, u32[]{:S(2)}, u32[]{:S(2)}) collective-permute-start(bf16[768,512]{1,0:T(8,128)(2,1)} %get-tuple-element.79), channel_id=1, source_target_pairs={{8,0},{10,2},{12,4},{14,6},{16,8},{18,10},{20,12},{22,14},{24,16},... | collective-permute-start | bytes 2359304 | tf_op jit(solution)/shard_map/ppermute | solution.py:162
  490.2 35.0 %collective-permute-start.50 = (bf16[448,3072]{1,0:T(8,128)(2,1)}, bf16[448,3072]{1,0:T(8,128)(2,1)S(1)}, u32[]{:S(2)}, u32[]{:S(2)}) collective-permute-start(bf16[448,3072]{1,0:T(8,128)(2,1)} %bitcast.53), channel_id=1, source_target_pairs={{0,2},{2,0},{4,6},{6,4},{8,10},{10,8},{12,14},{14,12},{16,18},{18,... | collective-permute-start | bytes 8257544 | tf_op jit(solution)/shard_map/ppermute | solution.py:149
  524.0 42.0 %collective-permute-start.61 = (bf16[2,192,512]{2,1,0:T(8,128)(2,1)S(1)}, bf16[2,192,512]{2,1,0:T(8,128)(2,1)S(1)}, u32[]{:S(2)}, u32[]{:S(2)}) collective-permute-start(bf16[2,192,512]{2,1,0:T(8,128)(2,1)S(1)} %get-tuple-element.131), channel_id=1, source_target_pairs={{0,2},{2,0},{4,6},{6,4},{8,10},{10,8},{12,14},{14,12},{16,18},{18,... | collective-permute-start | bytes 1179656 | tf_op jit(solution)/shard_map/ppermute | solution.py:149
  525.1 42.7 %collective-permute-start.62 = (bf16[2,192,512]{2,1,0:T(8,128)(2,1)S(1)}, bf16[2,192,512]{2,1,0:T(8,128)(2,1)S(1)}, u32[]{:S(2)}, u32[]{:S(2)}) collective-permute-start(bf16[2,192,512]{2,1,0:T(8,128)(2,1)S(1)} %get-tuple-element.132), channel_id=1, source_target_pairs={{0,4},{2,6},{4,0},{6,2},{8,12},{10,14},{12,8},{14,10},{16,20},{18,... | collective-permute-start | bytes 1179656 | tf_op jit(solution)/shard_map/ppermute | solution.py:149
  526.4 44.9 %collective-permute-start.63 = (bf16[2,192,512]{2,1,0:T(8,128)(2,1)}, bf16[2,192,512]{2,1,0:T(8,128)(2,1)}, u32[]{:S(2)}, u32[]{:S(2)}) collective-permute-start(bf16[2,192,512]{2,1,0:T(8,128)(2,1)} %get-tuple-element.133), channel_id=1, source_target_pairs={{0,6},{2,4},{4,2},{6,0},{8,14},{10,12},{12,10},{14,8},{16,22},{18,... | collective-permute-start | bytes 1179656 | tf_op jit(solution)/shard_map/ppermute | solution.py:149
  534.7 37.4 %collective-permute-start.72 = (bf16[1,192,512]{2,1,0:T(8,128)(2,1)}, bf16[1,192,512]{2,1,0:T(8,128)(2,1)}, u32[]{:S(2)}, u32[]{:S(2)}) collective-permute-start(bf16[1,192,512]{2,1,0:T(8,128)(2,1)} %get-tuple-element.137), channel_id=1, source_target_pairs={{0,6},{2,4},{4,2},{6,0},{8,14},{10,12},{12,10},{14,8},{16,22},{18,... | collective-permute-start | bytes 589832 | tf_op jit(solution)/shard_map/ppermute | solution.py:149
  563.7 45.1 %collective-permute-start.46 = (bf16[448,1536]{1,0:T(8,128)(2,1)}, bf16[448,1536]{1,0:T(8,128)(2,1)}, u32[]{:S(2)}, u32[]{:S(2)}) collective-permute-start(bf16[448,1536]{1,0:T(8,128)(2,1)} %constant_dynamic-slice_fusion.3), channel_id=1, source_target_pairs={{0,1},{1,0},{2,3},{3,2},{4,5},{5,4},{6,7},{7,6},{8,9},{9,8},{10,11... | collective-permute-start | bytes 4128776 | tf_op jit(solution)/shard_map/ppermute | solution.py:153
  565.9 48.5 %collective-permute-start.53 = (bf16[448,1536]{1,0:T(8,128)(2,1)}, bf16[448,1536]{1,0:T(8,128)(2,1)}, u32[]{:S(2)}, u32[]{:S(2)}) collective-permute-start(bf16[448,1536]{1,0:T(8,128)(2,1)} %add_convert_fusion), channel_id=1, source_target_pairs={{0,4},{2,6},{4,0},{6,2},{8,12},{10,14},{12,8},{14,10},{16,20},{18,... | collective-permute-start | bytes 4128776 | tf_op jit(solution)/shard_map/ppermute | solution.py:149
  567.8 58.8 %collective-permute-start.52 = (bf16[448,1536]{1,0:T(8,128)(2,1)}, bf16[448,1536]{1,0:T(8,128)(2,1)}, u32[]{:S(2)}, u32[]{:S(2)}) collective-permute-start(bf16[448,1536]{1,0:T(8,128)(2,1)} %get-tuple-element.75), channel_id=1, source_target_pairs={{0,1},{1,0},{2,3},{3,2},{4,5},{5,4},{6,7},{7,6},{8,9},{9,8},{10,11... | collective-permute-start | bytes 4128776 | tf_op jit(solution)/shard_map/ppermute | solution.py:153
  608.8 45.8 %collective-permute-start.47 = (bf16[448,1536]{1,0:T(8,128)(2,1)}, bf16[448,1536]{1,0:T(8,128)(2,1)}, u32[]{:S(2)}, u32[]{:S(2)}) collective-permute-start(bf16[448,1536]{1,0:T(8,128)(2,1)} %get-tuple-element.72), channel_id=1, source_target_pairs={{0,1},{1,0},{2,3},{3,2},{4,5},{5,4},{6,7},{7,6},{8,9},{9,8},{10,11... | collective-permute-start | bytes 4128776 | tf_op jit(solution)/shard_map/ppermute | solution.py:153
  613.2 41.4 %collective-permute-start.48 = (bf16[448,1536]{1,0:T(8,128)(2,1)}, bf16[448,1536]{1,0:T(8,128)(2,1)}, u32[]{:S(2)}, u32[]{:S(2)}) collective-permute-start(bf16[448,1536]{1,0:T(8,128)(2,1)} %add_convert_fusion.1), channel_id=1, source_target_pairs={{0,4},{2,6},{4,0},{6,2},{8,12},{10,14},{12,8},{14,10},{16,20},{18,... | collective-permute-start | bytes 4128776 | tf_op jit(solution)/shard_map/ppermute | solution.py:149
  (110 other events, 1829.5 us)

commit v2 on v1

--- a/solution.py
+++ b/solution.py
@@ -8,6 +8,7 @@
 
 epsilon = 1e-06
 PLANE = 4
+ORDER = (1, 3, 0, 2)
 
 
 def partner_2(value, axis, stride):
@@ -153,10 +154,10 @@
     return lax.ppermute(value, "tp", [(0, 1), (1, 0)])
 
 
-def shift_planes(value, step, senders):
+def send_planes(value, plane_pairs):
     pairs = [
-        (plane * PLANE + place, (plane + step) * PLANE + place)
-        for plane in senders
+        (source * PLANE + place, target * PLANE + place)
+        for source, target in plane_pairs
         for place in range(PLANE)
     ]
     return lax.ppermute(value, "fsdp", pairs)
@@ -166,90 +167,108 @@
     return lax.optimization_barrier((value,) + earlier)[0]
 
 
-class PlaneGather:
-    def __init__(self, own, planes, my_plane):
-        self.own, self.planes, self.my_plane = (own, planes, my_plane)
-        self.rights, self.lefts = ([], [])
-        self.right = self.left = own
-
-    def step(self, *earlier):
-        step = len(self.rights) + 1
-        right = after(self.right, *earlier) if earlier else self.right
-        left = after(self.left, *earlier) if earlier else self.left
-        self.right = shift_planes(right, 1, range(step - 1, self.planes - 1))
-        self.left = shift_planes(left, -1, range(1, self.planes - step + 1))
-        self.rights.append(self.right)
-        self.lefts.append(self.left)
-
-    def last(self):
-        return (self.right, self.left)
-
-    def whole(self):
-        own, planes, my_plane = (self.own, self.planes, self.my_plane)
-        whole = jnp.zeros((planes,) + own.shape, own.dtype)
-        whole = lax.dynamic_update_index_in_dim(whole, own, my_plane, 0)
-        for step in range(1, planes):
-            piece = jnp.where(
-                my_plane >= step, self.rights[step - 1], self.lefts[planes - step - 1]
-            )
-            place = lax.rem(my_plane - step + planes, planes)
-            whole = lax.dynamic_update_index_in_dim(whole, piece, place, 0)
-        return whole.reshape((planes * own.shape[0],) + own.shape[1:])
+def spread_places(blocks):
+    near = swap_fsdp(jnp.stack([blocks[1], blocks[3]]), 1)
+    far = swap_fsdp(jnp.stack([blocks[2], near[1]]), 2)
+    return [blocks[0], near[0], far[0], far[1]]
+
+
+class LineGather:
+    def __init__(self, own, my_plane):
+        self.own, self.my_plane = (own, my_plane)
+
+    def pair_up(self, *earlier):
+        self.partner = swap_fsdp(after(self.own, *earlier), PLANE)
+
+    def cross(self, *earlier):
+        even = self.my_plane % 2 == 0
+        partner = after(self.partner, *earlier)
+        low = jnp.where(even, self.own, partner)
+        high = jnp.where(even, partner, self.own)
+        self.pair = jnp.concatenate([low, high])
+        self.crossed = send_planes(self.pair, [(1, 2), (2, 1)])
+
+    def spread(self, *earlier):
+        self.outer = send_planes(after(self.crossed, *earlier), [(1, 0), (2, 3)])
+
+    def whole(self, *earlier):
+        inner = (self.my_plane == 1) | (self.my_plane == 2)
+        crossed, outer = lax.optimization_barrier((self.crossed, self.outer) + earlier)[:2]
+        other = jnp.where(inner, crossed, outer)
+        low = self.my_plane < 2
+        return jnp.concatenate([jnp.where(low, self.pair, other), jnp.where(low, other, self.pair)])
+
+
+def pair_up_both(first, second, *earlier):
+    both = after(jnp.stack([first.own, second.own]), *earlier)
+    both = swap_fsdp(both, PLANE)
+    first.partner, second.partner = (both[0], both[1])
 
 
 def add_rounded(left, right):
     return (left.astype(jnp.float32) + right.astype(jnp.float32)).astype(jnp.bfloat16)
 
 
-class PlaneReduce:
-    def __init__(self, terms, planes, my_plane):
-        self.terms, self.planes, self.my_plane = (terms, planes, my_plane)
-        self.right = self.left = None
-        self.steps = 0
-
-    def part(self, place):
-        return lax.dynamic_index_in_dim(
-            self.terms, jnp.clip(place, 0, self.planes - 1), 0, keepdims=False
-        )
-
-    def step(self, *earlier):
-        self.steps += 1
-        step, planes = (self.steps, self.planes)
-        right = self.part(self.my_plane + planes - step)
-        left = self.part(self.my_plane - planes + step)
-        if step > 1:
-            right = add_rounded(self.right, right)
-            left = add_rounded(self.left, left)
-        if earlier:
-            right = after(right, *earlier)
-            left = after(left, *earlier)
-        self.right = shift_planes(right, 1, range(0, step))
-        self.left = shift_planes(left, -1, range(planes - step, planes))
-
-    def last(self):
-        return (self.right, self.left)
-
-    def total(self):
-        total = self.part(self.my_plane).astype(jnp.float32) + self.right.astype(jnp.float32)
-        return (total + self.left.astype(jnp.float32)).astype(jnp.bfloat16)
-
-
-def rows_kernel(pick_ref, count_ref, *refs):
-    low_a, low_b, high_a, high_b, gain_ref = refs[:5]
-    normed_ref, stats_ref = refs[-2:]
+class LineReduce:
+    def __init__(self, terms, my_plane):
+        self.terms, self.my_plane = (terms, my_plane)
+        self.rows = terms[0].shape[1] // 4
+        self.far = 2 - 2 * (my_plane // 2)
+
+    def columns(self, start, count):
+        return jnp.concatenate(
+            [
+                lax.dynamic_slice_in_dim(term, start * self.rows, count * self.rows, 1)
+                for term in self.terms
+            ]
+        )
+
+    def inward(self):
+        self.sent = self.columns(self.far, 2)
+        self.arrived = send_planes(self.sent, [(0, 1), (3, 2)])
+
+    def cross(self, *earlier):
+        far = add_rounded(self.columns(self.far, 2), after(self.arrived, *earlier))
+        self.cross_sent = far
+        self.crossed = send_planes(far, [(1, 2), (2, 1)])
+
+    def of_pair(self, plane, *earlier):
+        crossed = after(self.crossed, *earlier)
+        crossed = lax.dynamic_slice_in_dim(crossed, plane % 2 * self.rows, self.rows, 1)
+        return self.columns(plane, 1).astype(jnp.float32) + crossed.astype(jnp.float32)
+
+
+def reduce_pairs(reduces, my_plane, *earlier):
+    sent = jnp.concatenate([reduce.of_pair(my_plane ^ 1, *earlier) for reduce in reduces])
+    sent = sent.astype(jnp.bfloat16)
+    got = swap_fsdp(sent, PLANE)
+
+    def total(*later):
+        kept = jnp.concatenate([reduce.of_pair(my_plane, *later) for reduce in reduces])
+        return (kept + after(got, *later).astype(jnp.float32)).astype(jnp.bfloat16)
+
+    return (sent, total)
+
+
+def rows_kernel(parts, pick_ref, count_ref, *refs):
+    sources, (gain_ref, normed_ref, stats_ref) = (refs[:-3], refs[-3:])
     at = pl.program_id(0)
-    rows = low_a.shape[3]
-    half = low_a.shape[4]
+    rows, half = sources[0].shape[3:]
     width = 2 * half
     live = lax.broadcasted_iota(jnp.int32, (rows, 1), 0) < count_ref[at]
     near = (pick_ref[at] & 1) == 1
-
-    def read(here, there):
-        value = jnp.where(near, there[0, 0, 0], here[0, 0, 0])
+    part = at // (pl.num_programs(0) // parts)
+
+    def read(high):
+        value = None
+        for index in range(parts):
+            here, there = sources[4 * index + high], sources[4 * index + 2 + high]
+            chosen = jnp.where(near, there[0, 0, 0], here[0, 0, 0])
+            value = chosen if value is None else jnp.where(part == index, chosen, value)
         return jnp.where(live, value.astype(jnp.float32), 0.0)
 
-    low = read(low_a, low_b)
-    high = read(high_a, high_b)
+    low = read(0)
+    high = read(1)
     mean = (
         jnp.sum(low, axis=-1, keepdims=True) + jnp.sum(high, axis=-1, keepdims=True)
     ) / width
@@ -265,52 +284,52 @@
     stats_ref[...] = jnp.where(lane == 0, mean, factor)
 
 
-def norm_block(here, there, picks, live_counts, norm_gain, my_group, part, parts, before):
-    _, _, slots, rows, half = here.shape
+def norm_block(here, there, picks, live_counts, norm_gain, my_group):
+    parts = len(here)
+    _, _, slots, rows, half = here[0].shape
     width = 2 * half
     steps = PLANE * slots
+    total = parts * steps
     picks = jnp.concatenate([picks, my_group[None]])
 
-    def source(group_xor):
-        return pl.BlockSpec(
-            (1, 1, 1, rows, half),
-            lambda at, pick, count: (pick[at] >> 1, pick[steps] ^ group_xor, at % slots, 0, 0),
-        )
-
-    out_specs = [
-        pl.BlockSpec((rows, width), lambda at, pick, count: (at + part * steps, 0)),
-        pl.BlockSpec((rows, 128), lambda at, pick, count: (at + part * steps, 0)),
-    ]
-    total = parts * steps * rows
-    extra = [] if before is None else list(before)
+    def source(part, group_xor, near):
+        def index(at, pick, count):
+            at = jnp.clip(at, part * steps, part * steps + steps - 1)
+            first = at // PLANE * PLANE
+            stand_in = jnp.where(at - first < 2, first + 2, first + 1)
+            chosen = pick[jnp.where((pick[at] & 1) == near, at, stand_in)]
+            return (chosen >> 1, pick[total] ^ group_xor, at // PLANE % slots, 0, 0)
+
+        return pl.BlockSpec((1, 1, 1, rows, half), index)
+
+    def target(at, pick, count):
+        slot, place = (at // PLANE, at % PLANE)
+        return (place * parts * slots + slot, 0)
+
+    arrays, specs = ([], [])
+    for part in range(parts):
+        arrays += [here[part], here[part], there[part], there[part]]
+        specs += [source(part, 0, 0), source(part, 1, 0), source(part, 0, 1), source(part, 1, 1)]
     return pl.pallas_call(
-        rows_kernel,
+        functools.partial(rows_kernel, parts),
         grid_spec=pltpu.PrefetchScalarGridSpec(
             num_scalar_prefetch=2,
-            grid=(steps,),
-            in_specs=[
-                source(0),
-                source(0),
-                source(1),
-                source(1),
-                pl.BlockSpec((1, width), lambda at, pick, count: (0, 0)),
-            ]
-            + [pl.BlockSpec(memory_space=pl.ANY)] * len(extra),
-            out_specs=out_specs,
+            grid=(total,),
+            in_specs=specs + [pl.BlockSpec((1, width), lambda at, pick, count: (0, 0))],
+            out_specs=[pl.BlockSpec((rows, width), target), pl.BlockSpec((rows, 128), target)],
         ),
         out_shape=[
-            jax.ShapeDtypeStruct((total, width), jnp.bfloat16),
-            jax.ShapeDtypeStruct((total, 128), jnp.float32),
+            jax.ShapeDtypeStruct((total * rows, width), jnp.bfloat16),
+            jax.ShapeDtypeStruct((total * rows, 128), jnp.float32),
         ],
-        input_output_aliases={7: 0, 8: 1} if extra else {},
-        compiler_params=pltpu.CompilerParams(vmem_limit_bytes=32 * 1024 * 1024),
+        compiler_params=pltpu.CompilerParams(vmem_limit_bytes=28 * 1024 * 1024),
         cost_estimate=pl.CostEstimate(
-            flops=10 * steps * rows * width,
-            bytes_accessed=6 * steps * rows * width,
+            flops=10 * total * rows * width,
+            bytes_accessed=6 * total * rows * width,
             transcendentals=0,
         ),
         name="norm_rows",
-    )(picks, live_counts, here, there, here, there, norm_gain[None, :], *extra)
+    )(picks, live_counts, *arrays, norm_gain[None, :])
 
 
 def mm(left, right, left_dim, right_dim):
@@ -405,36 +424,113 @@
     )(live_counts, projected, grad_mixed, scales)
 
 
-def scatter_partial(partial, share_width, my_group, *earlier):
-    parts, _, rows, width = partial.shape
-
-    def block(place):
-        return partial[:, place].reshape(parts * rows, width)
-
-    sent_far, sent_near = (block(3), block(1))
-    if earlier:
-        sent_far = after(sent_far, *earlier)
-        sent_near = after(sent_near, *earlier)
-    got_far = swap_fsdp(sent_far, 1)
-    got_near = swap_fsdp(sent_near, 1)
-    far = add_rounded(block(2), got_far)
-    near = add_rounded(block(0), got_near)
-
-    def halves(value):
-        mine = lax.dynamic_slice_in_dim(value, my_group * share_width, share_width, 1)
-        other = lax.dynamic_slice_in_dim(value, (1 - my_group) * share_width, share_width, 1)
-        return (mine, other)
-
-    far_mine, far_other = halves(far)
-    far_got = swap_tp(far_other)
-    near_mine, near_other = halves(near)
-    near_got = swap_tp(after(near_other, far_got))
-    far_sum = swap_fsdp(add_rounded(far_mine, far_got), 2)
-    return (
-        near_mine.astype(jnp.float32)
-        + near_got.astype(jnp.float32)
-        + far_sum.astype(jnp.float32)
-    )
+class PlaneScatter:
+    def __init__(self, sent, share_width, my_group):
+        self.share_width, self.my_group = (share_width, my_group)
+        self.got = swap_fsdp(sent, 1)
+
+    def mine(self, value):
+        start = self.my_group * self.share_width
+        return lax.dynamic_slice_in_dim(value, start, self.share_width, value.ndim - 1)
+
+    def other(self, value):
+        start = (1 - self.my_group) * self.share_width
+        return lax.dynamic_slice_in_dim(value, start, self.share_width, value.ndim - 1)
+
+    def add_cores(self, kept, *earlier):
+        got = after(self.got, *earlier) if earlier else self.got
+        half = kept.shape[1] // 2
+        first = add_rounded(kept[:, :half], got[:, :half])
+        near = add_rounded(kept[0, half:], got[0, half:])
+        far = add_rounded(kept[1, half:], got[1, half:])
+        self.first, self.near = (first, near)
+        sent_x = self.other(first)
+        self.over_x = swap_tp(sent_x)
+        self.over_y = swap_fsdp(far, 2)
+        return (first, far, sent_x)
+
+    def turn(self, *earlier):
+        over_x = after(self.over_x, *earlier)
+        over_y = after(self.over_y, *earlier)
+        first = self.mine(self.first).astype(jnp.float32) + over_x.astype(jnp.float32)
+        second = self.near.astype(jnp.float32) + over_y.astype(jnp.float32)
+        self.first_sum = first[0]
+        self.second_sum = self.mine(second)
+        sent_y = first[1].astype(jnp.bfloat16)
+        sent_x = self.other(second).astype(jnp.bfloat16)
+        self.last_y = swap_fsdp(sent_y, 2)
+        self.last_x = swap_tp(sent_x)
+        return (sent_y, sent_x)
+
+    def total(self):
+        return jnp.concatenate(
+            [
+                self.first_sum + self.last_y.astype(jnp.float32),
+                self.second_sum + self.last_x.astype(jnp.float32),
+            ]
+        )
+
+
+def home_kernel(counts, place_ref, *refs):
+    qkv_ref, out_ref = refs[-2:]
+    at, head = (pl.program_id(0), pl.program_id(1))
+    width = qkv_ref.shape[1]
+    first = 0
+    for group, count in enumerate(counts):
+        inside = (head >= first) & (head < first + count)
+        for step in range(PLANE):
+
+            @pl.when((at == step) & inside)
+            def _():
+                value = refs[group * PLANE + step][...].astype(jnp.float32)
+                qkv_ref[...] = value[:, :width]
+                out_ref[...] = value[:, width:]
+
+        first += count
+
+
+def place_home(groups, my_place, heads, head_dim):
+    rows = groups[0][0].shape[0]
+    head_width = 4 * head_dim
+    qkv_width = 3 * head_dim
+    counts = [blocks[0].shape[1] // head_width for blocks in groups]
+
+    def source(first, count):
+        return pl.BlockSpec(
+            (rows, head_width), lambda at, head, place: (0, jnp.clip(head - first, 0, count - 1))
+        )
+
+    specs = []
+    for group, count in enumerate(counts):
+        specs += [source(sum(counts[:group]), count)] * PLANE
+
+    def target(at, head, place):
+        return (0, (place[0] ^ at) * heads + head)
+
+    total = PLANE * heads
+    return pl.pallas_call(
+        functools.partial(home_kernel, counts),
+        grid_spec=pltpu.PrefetchScalarGridSpec(
+            num_scalar_prefetch=1,
+            grid=(PLANE, heads),
+            in_specs=specs,
+            out_specs=[
+                pl.BlockSpec((rows, qkv_width), target),
+                pl.BlockSpec((rows, head_dim), target),
+            ],
+        ),
+        out_shape=[
+            jax.ShapeDtypeStruct((rows, total * qkv_width), jnp.float32),
+            jax.ShapeDtypeStruct((rows, total * head_dim), jnp.float32),
+        ],
+        compiler_params=pltpu.CompilerParams(vmem_limit_bytes=32 * 1024 * 1024),
+        cost_estimate=pl.CostEstimate(
+            flops=total * rows * head_width,
+            bytes_accessed=6 * total * rows * head_width,
+            transcendentals=0,
+        ),
+        name="place_home",
+    )(my_place[None], *[block for blocks in groups for block in blocks])
 
 
 def per_plane(patches, cotangent, counts, masks, norm_gain, qk_gain, qkv_weight, out_weight):
@@ -461,25 +557,25 @@
     part_rows = slots * slot_rows
 
     replica_ids = jnp.arange(replicas, dtype=jnp.int32)
-    relative = jnp.arange(PLANE, dtype=jnp.int32)
+    relative = jnp.array(ORDER, dtype=jnp.int32)
+    own_at = ORDER.index(0)
     sources = (my_replica ^ relative)[:, None] ^ masks[None, :]
     live_counts = jnp.sum(
         jnp.where(replica_ids[:, None, None] == sources[None], counts[:, None, :], 0), axis=0
     ).astype(jnp.int32)
     picks = (relative[:, None] ^ (masks & (PLANE - 1))[None, :]).astype(jnp.int32)
     places = jnp.arange(slot_rows, dtype=jnp.int32)
-    is_live = (places[None, :] < live_counts[0][:, None]).reshape(tok_rows)
+    is_live = (places[None, :] < live_counts[own_at][:, None]).reshape(tok_rows)
 
     def by_part(table):
-        return jnp.transpose(table.reshape(PLANE, parts, slots), (1, 0, 2)).reshape(parts, -1)
-
-    part_counts = by_part(live_counts)
-    part_picks = by_part(picks)
-    flat_counts = part_counts.reshape(-1)
+        return jnp.transpose(table).reshape(-1)
+
+    flat_counts = live_counts.reshape(-1)
 
     holding = lax.dynamic_slice_in_dim(patches, my_group * share_width, share_width, 1)
     holding = holding.reshape(parts, slots, slot_rows, share_width)
     moved = [holding[part] for part in range(parts)]
+    first_moved = None
     for bit_place in range(2, replicas.bit_length() - 1):
         previous = None
         for part in range(parts):
@@ -488,140 +584,174 @@
             moving = jnp.right_shift(masks[part * slots : (part + 1) * slots], bit_place) & 1
             moved[part] = jnp.where((moving == 1)[:, None, None], partner, moved[part])
             previous = partner
+            if first_moved is None:
+                first_moved = moved[0]
+            if part == 0:
+                first_there = partner
+            if part == 1 and bit_place == 2:
+                second_moved = moved[1]
 
     def head_columns(place):
         qkv_part = lax.dynamic_slice_in_dim(
             qkv_weight, place * heads * qkv_width, heads * qkv_width, 1
-        ).reshape(shard_rows, heads, qkv_width)
+        )
         out_part = lax.dynamic_slice_in_dim(
             out_weight, place * heads * head_dim, heads * head_dim, 1
-        ).reshape(shard_rows, heads, head_dim)
-        return jnp.concatenate([qkv_part, out_part], axis=2).reshape(
-            shard_rows, heads * head_width
-        )
-
-    shards = [head_columns(my_place)]
-    for step in range(1, PLANE):
-        shards.append(swap_fsdp(head_columns(my_place ^ step), step))
+        )
+        return jnp.concatenate([qkv_part, out_part], axis=1)
+
+    upstream_own = jnp.where(is_live[:, None], cotangent, jnp.zeros((), cotangent.dtype))
+    up_far = [swap_fsdp(upstream_own[:part_rows], 2)]
+    shards = spread_places([head_columns(my_place ^ step) for step in range(PLANE)])
+    shards = [after(shard, first_moved, up_far[0]) for shard in shards]
     plane_shard = jnp.zeros((PLANE, shard_rows, heads * head_width), qkv_weight.dtype)
     for step in range(PLANE):
         plane_shard = lax.dynamic_update_index_in_dim(
             plane_shard, shards[step], my_place ^ step, 0
         )
     plane_shard = plane_shard.reshape(PLANE * shard_rows, heads * head_width)
-
-    upstream_own = jnp.where(is_live[:, None], cotangent, jnp.zeros((), cotangent.dtype))
-    up_own = [upstream_own[:part_rows], upstream_own[part_rows:]]
-    up_near = swap_fsdp(upstream_own, 1)
-    up_far = [swap_fsdp(after(up_own[0], shards[2], shards[3]), 2), None]
+    shards_of = []
+    for head in range(heads):
+        qkv_at = head * qkv_width
+        out_at = heads * qkv_width + head * head_dim
+        shard = jnp.concatenate(
+            [
+                plane_shard[:, qkv_at : qkv_at + qkv_width],
+                plane_shard[:, out_at : out_at + head_dim],
+            ],
+            axis=1,
+        )
+        shards_of.append(shard)
+
+    gathers = [LineGather(shard, my_plane) for shard in shards_of]
+    gathers[0].pair_up(first_there)
+    gathers[0].cross(moved[-1])
 
     here, there = ([], [])
     for part in range(parts):
         own = moved[part]
         over = swap_tp(own)
-        far = swap_fsdp(own, 2)
-        far_over = swap_tp(far)
+        if part == 0:
+            far = swap_fsdp(after(own, second_moved, *shards), 2)
+            far_over = swap_tp(far)
+        else:
+            far = swap_fsdp(after(own, gathers[0].partner), 2)
+            far_over = swap_tp(after(far, over, here[0]))
+            pair_up_both(gathers[1], gathers[2], gathers[0].partner)
+            up_far.append(swap_fsdp(after(upstream_own[part_rows:], far), 2))
+            own = after(own, gathers[0].crossed, gathers[1].partner)
         here.append(
             jnp.stack([own, over, far, far_over]).reshape(
                 2, 2, slots, slot_rows, share_width
             )
         )
         there.append(swap_fsdp(here[part], 1))
-    up_far[1] = swap_fsdp(after(up_own[1], far), 2)
-    up_both = [swap_fsdp(value, 1) for value in up_far]
+    gathers[0].spread()
+    gathers[1].cross()
+
+    normed, stats = norm_block(
+        here,
+        there,
+        by_part(picks),
+        by_part(live_counts),
+        norm_gain,
+        my_group,
+    )
+    gathers[1].spread(normed)
+    gathers[2].cross(normed)
+    up_far[1] = after(up_far[1], normed)
+    up_other = [
+        swap_fsdp(jnp.stack([upstream_own[:part_rows], up_far[0]]), 1),
+        swap_fsdp(jnp.stack([upstream_own[part_rows:], up_far[1]]), 1),
+    ]
     upstream = jnp.concatenate(
-        [
-            value
-            for part in range(parts)
-            for value in (
-                up_own[part],
-                up_near[part * part_rows : (part + 1) * part_rows],
-                up_far[part],
-                up_both[part],
-            )
-        ]
-    )
-
-    shard_of = [
-        plane_shard[:, head * head_width : (head + 1) * head_width] for head in range(heads)
-    ]
-    gathers = [PlaneGather(shard, planes, my_plane) for shard in shard_of]
-    reduces = [None] * heads
-    gathers[0].step(moved[1])
-    for step in range(2, planes):
-        gathers[0].step()
-
-    normed_stats = None
-    for part in range(parts):
-        normed_stats = norm_block(
-            here[part],
-            there[part],
-            part_picks[part],
-            part_counts[part],
-            norm_gain,
-            my_group,
-            part,
-            parts,
-            normed_stats,
-        )
-    normed, stats = normed_stats
+        [up_other[0][0], up_other[1][0], up_other[0][1], up_other[1][1], upstream_own, *up_far]
+    )
 
     scales = jnp.concatenate([qk_gain[0:1] * head_dim ** (-0.5), qk_gain[1:2]])
-    weights, mixed_parts, back_parts, grads = ([], [], [], [])
+    weights, mixed_parts, back_parts, reduces = ([], [], [], [])
     for head in range(heads):
-        weight = gathers[head].whole()
+        if head == 0:
+            weight = gathers[0].whole(normed, gathers[1].crossed, gathers[2].partner)
+        elif head == 1:
+            weight = gathers[1].whole(qkv_term, out_term, gathers[2].crossed)
+            gathers[2].spread(qkv_term)
+        else:
+            weight = gathers[2].whole(qkv_term, out_term, reduces[0].cross_sent)
         weights.append(weight)
-        if head + 1 < heads:
-            gathers[head + 1].step(*gathers[head].last())
-        out_head = weight[:, qkv_width:]
-        grad_mixed = mm(upstream, out_head, 1, 0).astype(jnp.bfloat16)
+        grad_mixed = mm(upstream, weight[:, qkv_width:], 1, 0).astype(jnp.bfloat16)
         projected = mm(normed, weight[:, :qkv_width], 1, 0)
-        if head > 0:
-            projected = after(projected, *reduces[head - 1].last())
-            reduces[head - 1].step()
         mixed, back = attend(projected, grad_mixed, scales, flat_counts, slot_rows)
         mixed_parts.append(mixed)
         back_parts.append(back)
-        frontier = []
-        if head + 1 < heads:
-            frontier += gathers[head + 1].last()
-        if head > 0:
-            frontier += reduces[head - 1].last()
         held_back, held_mixed = (back, mixed)
-        if frontier:
-            held_back = after(back, *frontier)
-            held_mixed = after(mixed, *frontier)
-        if head + 1 < heads:
-            for step in range(2, planes):
-                gathers[head + 1].step(mixed)
-        if head > 0:
-            reduces[head - 1].step(mixed)
-        qkv_term = mm(normed, held_back, 0, 0).astype(jnp.bfloat16)
-        out_term = mm(upstream, held_mixed, 0, 0).astype(jnp.bfloat16)
-        terms = jnp.concatenate([qkv_term, out_term], axis=1).reshape(
-            planes, PLANE * shard_rows, head_width
-        )
-        reduces[head] = PlaneReduce(terms, planes, my_plane)
-        reduces[head].step()
-    while reduces[-1].steps < planes - 1:
-        reduces[-1].step()
+        if head == 2:
+            mixed_all = after(jnp.concatenate(mixed_parts, axis=1), reduces[1].arrived)
+            out_all = jnp.concatenate([weight[:, qkv_width:] for weight in weights], axis=1)
+            out_sent = mm(mixed_all[: 2 * tok_rows], out_all, 1, 1).astype(jnp.bfloat16)
+            out_scatter = PlaneScatter(
+                out_sent.reshape(2, tok_rows, model_width), share_width, my_group
+            )
+            reduces[1].cross(out_sent)
+            held = after(mixed_all[2 * tok_rows :], out_sent, reduces[1].cross_sent)
+            out_kept = mm(held, out_all, 1, 1).astype(jnp.bfloat16)
+            held_back = after(held_back, out_kept)
+            held_mixed = after(held_mixed, out_kept)
+        qkv_term = mm(held_back, normed, 0, 0).astype(jnp.bfloat16)
+        out_term = mm(held_mixed, upstream, 0, 0).astype(jnp.bfloat16)
+        if head == 1:
+            reduces[0].cross(qkv_term, out_term)
+        reduces.append(LineReduce([qkv_term, out_term], my_plane))
+        reduces[head].inward()
+
+    def send_home(total):
+        count = total.shape[0] // head_width
+        summed = total.T.reshape(PLANE, shard_rows, count * head_width)
+        return spread_places(
+            [
+                lax.dynamic_index_in_dim(summed, my_place ^ step, 0, keepdims=False)
+                for step in range(PLANE)
+            ]
+        )
 
     back_all = jnp.concatenate(back_parts, axis=1)
     qkv_all = jnp.concatenate([weight[:, :qkv_width] for weight in weights], axis=1)
-    partial_back = mm(back_all, qkv_all, 1, 1).astype(jnp.bfloat16)
-    grad_normed = scatter_partial(
-        partial_back.reshape(parts, PLANE, part_rows, model_width), share_width, my_group
-    )
-    mixed_all = jnp.concatenate(mixed_parts, axis=1)
-    out_all = jnp.concatenate([weight[:, qkv_width:] for weight in weights], axis=1)
-    partial_out = mm(mixed_all, out_all, 1, 1).astype(jnp.bfloat16)
-    attended = scatter_partial(
-        partial_out.reshape(parts, PLANE, part_rows, model_width), share_width, my_group
-    )
+    out_added = out_scatter.add_cores(
+        after(out_kept.reshape(2, tok_rows, model_width), qkv_term, out_term)
+    )
+    held = after(back_all[: 2 * tok_rows], *out_added, reduces[2].sent)
+    back_sent = mm(held, qkv_all, 1, 1).astype(jnp.bfloat16)
+    reduces[2].cross(back_sent)
+    sent, early_total = reduce_pairs(reduces[:2], my_plane, back_sent)
+    between = (reduces[2].cross_sent, sent)
+    back_scatter = PlaneScatter(
+        after(
+            back_sent.reshape(2, tok_rows, model_width),
+            out_scatter.over_x,
+            out_scatter.over_y,
+            *between,
+        ),
+        share_width,
+        my_group,
+    )
+    turned = out_scatter.turn(*between)
+    held = after(back_all[2 * tok_rows :], *turned)
+    back_kept = mm(held, qkv_all, 1, 1).astype(jnp.bfloat16)
+    back_added = back_scatter.add_cores(
+        after(
+            back_kept.reshape(2, tok_rows, model_width), out_scatter.last_x, out_scatter.last_y
+        )
+    )
+    sent, late_total = reduce_pairs(reduces[2:], my_plane, *back_added)
+    total = jnp.concatenate([early_total(*back_added), late_total(*back_added)])
+    back_scatter.turn(sent)
+    home = send_home(after(total, back_scatter.over_x, back_scatter.over_y))
+    attended = out_scatter.total()
     attended = jnp.where(is_live[:, None], attended, 0.0).astype(jnp.bfloat16)
+    grad_normed = back_scatter.total()
 
     def own_slot(part, slot):
-        pick = part_picks[part, slot]
+        pick = picks[own_at, part * slots + slot]
         mine = lax.dynamic_index_in_dim(here[part][:, 0, slot], pick >> 1, 0, keepdims=False)
         other = lax.dynamic_index_in_dim(there[part][:, 0, slot], pick >> 1, 0, keepdims=False)
         return jnp.where((pick & 1) == 1, other, mine)
@@ -630,12 +760,7 @@
         [own_slot(part, slot) for part in range(parts) for slot in range(slots)]
     ).astype(jnp.float32)
     own_rows = jnp.where(is_live[:, None], own_rows, 0.0)
-    own_stats = jnp.concatenate(
-        [
-            stats[part * PLANE * part_rows : part * PLANE * part_rows + part_rows, 0:2]
-            for part in range(parts)
-        ]
-    )
+    own_stats = stats[own_at * tok_rows : (own_at + 1) * tok_rows, 0:2]
     mean = own_stats[:, 0:1]
     factor = own_stats[:, 1:2]
     centred = (own_rows - mean) * factor
@@ -646,23 +771,7 @@
     grad_rows = factor * (weighted - sums[0][:, None] - centred * sums[1][:, None])
     grad_rows = grad_rows.astype(jnp.bfloat16)
 
-    def bring_home(sums_of):
-        summed = jnp.stack(sums_of).reshape(
-            len(sums_of), PLANE, shard_rows, head_width
-        )
-        blocks = []
-        for step in range(PLANE):
-            block = lax.dynamic_index_in_dim(summed, my_place ^ step, 1, keepdims=False)
-            blocks.append(block if step == 0 else swap_fsdp(block, step))
-        return jnp.stack(blocks)
-
-    early = bring_home([reduce.total() for reduce in reduces[:-1]])
-    late = bring_home([reduces[-1].total()])
-    stacked = jnp.concatenate([early, late], axis=1)
-    stacked = jnp.take(stacked, my_place ^ relative, axis=0).astype(jnp.float32)
-    stacked = jnp.transpose(stacked, (2, 0, 1, 3))
-    grad_qkv_weight = stacked[..., :qkv_width].reshape(shard_rows, local_heads * qkv_width)
-    grad_out_weight = stacked[..., qkv_width:].reshape(shard_rows, local_heads * head_dim)
+    grad_qkv_weight, grad_out_weight = place_home([home], my_place, heads, head_dim)
     return (attended, grad_rows, grad_qkv_weight, grad_out_weight)
 
 
@@ -674,7 +783,7 @@
             mesh.shape["tp"] == 2
             and replicas == 4 * PLANE
             and replicas & (replicas - 1) == 0
-            and local_heads % PLANE == 0
+            and local_heads == 3 * PLANE
             and qk_gain.shape[1] == 128
             and counts.shape[1] == 4
         )

time: 671 us -> 567 us (0.85)
  local copies, waits for them, and re-layouts: 119 us -> 53.6 us
  starting transfers between devices: 136 us -> 98.5 us
  waiting for transfers between devices: 204 us -> 186 us
  other arithmetic: 66.4 us -> 82.2 us
  Pallas kernels: 40.2 us -> 47 us
    ppermute x36 -> x12, starting transfers between devices: 109 us -> 37.5 us  [send_planes(): return lax.ppermute(value, 'fsdp', pairs)]
    slice x22 -> x8, local copies, waits for them, and re-layouts: 41 us -> 5.53 us  [the longest x1 2.26 us: per_plane(): held = after(back_all[2 * tok_rows:], *turned)]
    ppermute x28 -> x26, starting transfers between devices: 18.9 us -> 52.9 us  [swap_fsdp(): return lax.ppermute(value, 'fsdp', pairs)]
    reshape x13 -> x2, local copies, waits for them, and re-layouts: 29.3 us -> 0.17 us  [the longest x1 0.09 us: by_part(): return jnp.transpose(table).reshape(-1)]
    ppermute x9, waiting for transfers between devices: 60.5 us -> 40.5 us  [swap_tp(): return lax.ppermute(value, 'tp', [(0, 1), (1, 0)])]
    add x0 -> x10, other arithmetic: none -> 12 us  [the longest x2 4.41 us: turn(): second = self.near.astype(jnp.float32) + over_y.astype(jnp.float32)]
    another operation x1 -> x13, other arithmetic: 1.06 us -> 11.8 us  [the longest x1 3.13 us: per_plane(): jnp.stack([upstream_own[:part_rows], up_far[0]])]
    select_n x1 -> x6, other arithmetic: 0.01 us -> 8.33 us  [the longest x2 5.17 us: whole(): jnp.where(low, other, self.pair)]
  transfers between devices with their start and end apart: 73 -> 47, of which waited for: 19 -> 24; matrix products, arithmetic and copies ran while one was open for 35% -> 35% of each run, Pallas kernels for 6% -> 7%
where the time goes in v2:
time: 567 us; the launch traced here: 559 us
  waiting for transfers between devices  186 us (33%)
  starting transfers between devices  98.5 us (17%)
  matrix products  83.5 us (15%)
  other arithmetic  82.2 us (14%)
  local copies, waits for them, and re-layouts  53.6 us (9%)
  Pallas kernels  47 us (8%)
  between operations  7.59 us (1%)
    ppermute x26, waiting for transfers between devices, swap_fsdp(): return lax.ppermute(value, 'fsdp', pairs)  100 us
    dot_general x16, matrix products, mm(): lax.dot_general(left, right, (((left_dim,), (right_dim,)), ((), ())), pre...  83.5 us
    ppermute x26, starting transfers between devices, swap_fsdp(): return lax.ppermute(value, 'fsdp', pairs)  52.9 us
    ppermute x12, waiting for transfers between devices, send_planes(): return lax.ppermute(value, 'fsdp', pairs)  45.7 us
    ppermute x9, waiting for transfers between devices, swap_tp(): return lax.ppermute(value, 'tp', [(0, 1), (1, 0)])  40.5 us
    ppermute x12, starting transfers between devices, send_planes(): return lax.ppermute(value, 'fsdp', pairs)  37.5 us
    pallas_call x3, Pallas kernels, attend(): pl.pallas_call(functools.partial(attention_kernel, per_step), grid_spec=p...  31 us
    unnamed x203, local copies, waits for them, and re-layouts  19 us
  transfers between devices with their start and end apart: 47, of which 24 were waited for; matrix products, arithmetic and copies ran while one was open for 35% of the time, Pallas kernels for 7%

profile of v2, /device:TPU:0, one launch (start us, length us, event | category | flops | bytes accessed | tf_op | source)
XLA Modules:
  0.0 558.8 jit_solution(14819440141679865112)
XLA Ops:
  30.7 20.9 %collective-permute-done.3 = bf16[2,112,1536]{2,1,0:T(8,128)(2,1)S(1)} collective-permute-done((bf16[2,112,1536]{2,1,0:T(8,128)(2,1)S(1)}, bf16[2,112,1536]{2,1,0:T(8,128)(2,1)S(1)}, u32[]{:S(2)}, u32[]{:S(2)}) %collective-permute-start.3) | collective-permute-done | bytes 688160 | tf_op jit(solution)/shard_map/ppermute | solution.py:150
  51.8 5.9 %collective-permute-done.1 = bf16[2,112,1536]{2,1,0:T(8,128)(2,1)S(1)} collective-permute-done((bf16[2,112,1536]{2,1,0:T(8,128)(2,1)S(1)}, bf16[2,112,1536]{2,1,0:T(8,128)(2,1)S(1)}, u32[]{:S(2)}, u32[]{:S(2)}) %collective-permute-start.1) | collective-permute-done | bytes 688160 | tf_op jit(solution)/shard_map/ppermute | solution.py:150
  63.5 7.3 %collective-permute-done.6 = bf16[2,192,1536]{2,1,0:T(8,128)(2,1)S(1)} collective-permute-done((bf16[2,192,1536]{2,1,0:T(8,128)(2,1)S(1)}, bf16[2,192,1536]{2,1,0:T(8,128)(2,1)S(1)}, u32[]{:S(2)}, u32[]{:S(2)}) %collective-permute-start.6) | collective-permute-done | bytes 1179680 | tf_op jit(solution)/shard_map/ppermute | solution.py:150
  73.0 9.6 %collective-permute-start.11 = (bf16[768,512]{1,0:T(8,128)(2,1)S(1)}, bf16[768,512]{1,0:T(8,128)(2,1)S(1)}, u32[]{:S(2)}, u32[]{:S(2)}) collective-permute-start(bf16[768,512]{1,0:T(8,128)(2,1)S(1)} %pad_maximum_fusion.28), channel_id=1, source_target_pairs={{0,8},{2,10},{4,12},{6,14},{8,0},{10,2},{12,4},{14,6},{16,24},{18,... | collective-permute-start | bytes 2359304 | tf_op jit(solution)/shard_map/ppermute | solution.py:150
  90.5 10.8 %collective-permute-done.11 = bf16[768,512]{1,0:T(8,128)(2,1)S(1)} collective-permute-done((bf16[768,512]{1,0:T(8,128)(2,1)S(1)}, bf16[768,512]{1,0:T(8,128)(2,1)S(1)}, u32[]{:S(2)}, u32[]{:S(2)}) %collective-permute-start.11) | collective-permute-done | bytes 786464 | tf_op jit(solution)/shard_map/ppermute | solution.py:150
  104.5 11.8 %collective-permute-done.8 = bf16[2,112,1536]{2,1,0:T(8,128)(2,1)S(1)} collective-permute-done((bf16[2,112,1536]{2,1,0:T(8,128)(2,1)S(1)}, bf16[2,112,1536]{2,1,0:T(8,128)(2,1)S(1)}, u32[]{:S(2)}, u32[]{:S(2)}) %collective-permute-start.8) | collective-permute-done | bytes 688160 | tf_op jit(solution)/shard_map/ppermute | solution.py:154
  128.1 9.8 %collective-permute-done.13 = bf16[2,768,512]{2,1,0:T(8,128)(2,1)} collective-permute-done((bf16[2,768,512]{2,1,0:T(8,128)(2,1)}, bf16[2,768,512]{2,1,0:T(8,128)(2,1)}, u32[]{:S(2)}, u32[]{:S(2)}) %collective-permute-start.13) | collective-permute-done | bytes 1572896 | tf_op jit(solution)/shard_map/ppermute | solution.py:150
  155.1 10.5 %norm_rows.1 = (bf16[1792,3072]{1,0:T(8,128)(2,1)S(1)}, f32[1792,128]{1,0:T(8,128)S(1)}) custom-call(s32[17]{0:T(128)S(1)} %pad_add_fusion.pick_ref, s32[16]{0:T(128)S(1)} %reshape.170.count_ref, bf16[2,2,2,112,1536]{4,3,2,1,0:T(8,128)(2,1)S(1)} %bitcast.158, bf16[2,2,2,112,1536]{4,3,2,1,0:T(8,128)(2,1)S(1)} %bitcast.159, ...), custom_call_target="tpu_custom_call" | custom-call | flops 55050240 | bytes 33030144 | tf_op jit(solution)/shard_map/norm_rows/pallas_call | solution.py:313
  170.0 27.7 %collective-permute-done.18 = bf16[1536,512]{1,0:T(8,128)(2,1)S(1)} collective-permute-done((bf16[1536,512]{1,0:T(8,128)(2,1)}, bf16[1536,512]{1,0:T(8,128)(2,1)S(1)}, u32[]{:S(2)}, u32[]{:S(2)}) %collective-permute-start.18) | collective-permute-done | bytes 1572896 | tf_op jit(solution)/shard_map/ppermute | solution.py:163
  207.2 5.9 %fusion.37.proj_ref = f32[1792,384]{1,0:T(8,128)S(1)} fusion(bf16[1792,3072]{1,0:T(8,128)(2,1)S(1)} %get-tuple-element.75, bf16[3072,384]{1,0:T(8,128)(2,1)S(1)} %fusion.4), kind=kOutput, calls=%fused_computation.221 | convolution fusion | flops 4227858432 | bytes 16121856 | tf_op jit(solution)/shard_map/dot_general | solution.py:336
  224.3 6.2 %convolution_convert_fusion.12.grad_ref = bf16[1792,128]{1,0:T(8,128)(2,1)S(1)} fusion(bf16[1792,3072]{1,0:T(8,128)(2,1)} %constant_dynamic-update-slice_fusion, bf16[3072,128]{1,0:T(8,128)(2,1)S(1)} %pad_maximum_fusion.27), kind=kOutput, calls=%fused_computation.45 | convolution fusion | flops 1409515520 | bytes 12255232 | tf_op jit(solution)/shard_map/dot_general | solution.py:336
  230.6 10.2 %attend_images.3 = (bf16[1792,128]{1,0:T(8,128)(2,1)S(1)}, bf16[1792,384]{1,0:T(8,128)(2,1)S(1)}) custom-call(s32[16]{0:T(128)S(1)} %reshape.169.count_ref, f32[1792,384]{1,0:T(8,128)S(1)} %fusion.37.proj_ref, bf16[1792,128]{1,0:T(8,128)(2,1)S(1)} %convolution_convert_fusion.12.grad_ref, f32[2,128]{1,0:T(2,128)S(1)} %pad_maximum_fusion.33.scale_ref), custom_call_target="tpu_custom_call" | custom-call | flops 308281344 | bytes 5505024 | tf_op jit(solution)/shard_map/attend_images/pallas_call | solution.py:398
  240.8 5.9 %convolution_convert_fusion.9 = bf16[128,3072]{1,0:T(8,128)(2,1)S(1)} fusion(bf16[1792,128]{1,0:T(8,128)(2,1)S(1)} %get-tuple-element.80, bf16[1792,3072]{1,0:T(8,128)(2,1)} %constant_dynamic-update-slice_fusion), kind=kOutput, calls=%fused_computation.12 | convolution fusion | flops 1409679360 | bytes 12255232 | tf_op jit(solution)/shard_map/dot_general | solution.py:336
  262.9 7.0 %collective-permute-start.26 = (bf16[512,1536]{1,0:T(8,128)(2,1)}, bf16[512,1536]{1,0:T(8,128)(2,1)}, u32[]{:S(2)}, u32[]{:S(2)}) collective-permute-start(bf16[512,1536]{1,0:T(8,128)(2,1)} %pad_maximum_fusion.13), channel_id=1, source_target_pairs={{0,8},{2,10},{4,12},{6,14},{24,16},{26,18},{28,20},{30,22},{1,9},{... | collective-permute-start | bytes 4718600 | tf_op jit(solution)/shard_map/ppermute | solution.py:163
  271.4 5.9 %fusion.38.proj_ref = f32[1792,384]{1,0:T(8,128)S(1)} fusion(bf16[1792,3072]{1,0:T(8,128)(2,1)S(1)} %bitcast.166, bf16[3072,384]{1,0:T(8,128)(2,1)S(1)} %copy-done.42), kind=kOutput, calls=%fused_computation.222 | convolution fusion | flops 4227858432 | bytes 16121856 | tf_op jit(solution)/shard_map/dot_general | solution.py:336
  277.3 10.2 %attend_images.4 = (bf16[1792,128]{1,0:T(8,128)(2,1)S(1)}, bf16[1792,384]{1,0:T(8,128)(2,1)S(1)}) custom-call(s32[16]{0:T(128)S(1)} %reshape.169.count_ref, f32[1792,384]{1,0:T(8,128)S(1)} %fusion.38.proj_ref, bf16[1792,128]{1,0:T(8,128)(2,1)S(1)} %convolution_convert_fusion.11.grad_ref, f32[2,128]{1,0:T(2,128)S(1)} %pad_maximum_fusion.33.scale_ref), custom_call_target="tpu_custom_call" | custom-call | flops 308281344 | bytes 5505024 | tf_op jit(solution)/shard_map/attend_images/pallas_call | solution.py:398
  295.3 7.0 %collective-permute-start.27 = (bf16[512,1536]{1,0:T(8,128)(2,1)}, bf16[512,1536]{1,0:T(8,128)(2,1)}, u32[]{:S(2)}, u32[]{:S(2)}) collective-permute-start(bf16[512,1536]{1,0:T(8,128)(2,1)} %pad_maximum_fusion.14), channel_id=1, source_target_pairs={{0,8},{2,10},{4,12},{6,14},{24,16},{26,18},{28,20},{30,22},{1,9},{... | collective-permute-start | bytes 4718600 | tf_op jit(solution)/shard_map/ppermute | solution.py:163
  314.9 5.9 %fusion.39.proj_ref = f32[1792,384]{1,0:T(8,128)S(1)} fusion(bf16[1792,3072]{1,0:T(8,128)(2,1)S(1)} %bitcast.166, bf16[3072,384]{1,0:T(8,128)(2,1)S(1)} %fusion.2), kind=kOutput, calls=%fused_computation.223 | convolution fusion | flops 4227858432 | bytes 16121856 | tf_op jit(solution)/shard_map/dot_general | solution.py:336
  320.9 10.7 %attend_images.5 = (bf16[1792,128]{1,0:T(8,128)(2,1)S(1)}, bf16[1792,384]{1,0:T(8,128)(2,1)S(1)}) custom-call(s32[16]{0:T(128)S(1)} %reshape.169.count_ref, f32[1792,384]{1,0:T(8,128)S(1)} %fusion.39.proj_ref, bf16[1792,128]{1,0:T(8,128)(2,1)S(1)} %convolution_convert_fusion.10.grad_ref, f32[2,128]{1,0:T(2,128)S(1)} %pad_maximum_fusion.33.scale_ref), custom_call_target="tpu_custom_call" | custom-call | flops 308281344 | bytes 5505024 | tf_op jit(solution)/shard_map/attend_images/pallas_call | solution.py:398
  331.7 5.2 collective-permute-done.27
  337.0 4.9 convolution_convert_fusion.3
  366.8 8.1 %collective-permute-start.30 = (bf16[512,1536]{1,0:T(8,128)(2,1)}, bf16[512,1536]{1,0:T(8,128)(2,1)}, u32[]{:S(2)}, u32[]{:S(2)}) collective-permute-start(bf16[512,1536]{1,0:T(8,128)(2,1)} %pad_maximum_fusion.15), channel_id=1, source_target_pairs={{0,8},{2,10},{4,12},{6,14},{24,16},{26,18},{28,20},{30,22},{1,9},{... | collective-permute-start | bytes 4718600 | tf_op jit(solution)/shard_map/ppermute | solution.py:163
  386.6 10.8 %convolution_convert_fusion.1 = bf16[896,3072]{1,0:T(8,128)(2,1)} fusion(bf16[896,1152]{1,0:T(8,128)(2,1)} %get-tuple-element.100, bf16[3072,384]{1,0:T(8,128)(2,1)S(1)} %copy-done.45, bf16[3072,384]{1,0:T(8,128)(2,1)S(1)} %copy-done.43, bf16[3072,384]{1,0:T(8,128)(2,1)S(1)} %copy-done.40), kind=kOutput, calls=%fused_computation.4 | convolution fusion | flops 6365773824 | bytes 14647296 | tf_op jit(solution)/shard_map/dot_general | solution.py:336
  397.4 10.4 %collective-permute-done.30 = bf16[512,1536]{1,0:T(8,128)(2,1)} collective-permute-done((bf16[512,1536]{1,0:T(8,128)(2,1)}, bf16[512,1536]{1,0:T(8,128)(2,1)}, u32[]{:S(2)}, u32[]{:S(2)}) %collective-permute-start.30) | collective-permute-done | bytes 1572896 | tf_op jit(solution)/shard_map/ppermute | solution.py:163
  422.7 14.6 %collective-permute-start.43 = (bf16[1024,768]{1,0:T(8,128)(2,1)}, bf16[1024,768]{1,0:T(8,128)(2,1)}, u32[]{:S(2)}, u32[]{:S(2)}) collective-permute-start(bf16[1024,768]{1,0:T(8,128)(2,1)} %pad_maximum_fusion.16), channel_id=1, source_target_pairs={{0,8},{2,10},{4,12},{6,14},{8,0},{10,2},{12,4},{14,6},{16,24},{18,... | collective-permute-start | bytes 4718600 | tf_op jit(solution)/shard_map/ppermute | solution.py:150
  443.7 9.9 %convolution_convert_fusion = bf16[896,3072]{1,0:T(8,128)(2,1)S(1)} fusion(bf16[896,1152]{1,0:T(8,128)(2,1)} %get-tuple-element.107, bf16[3072,384]{1,0:T(8,128)(2,1)} %copy-done.44, bf16[3072,384]{1,0:T(8,128)(2,1)} %fusion.3, bf16[3072,384]{1,0:T(8,128)(2,1)S(1)} %copy-done.41), kind=kOutput, calls=%fused_computation.3 | convolution fusion | flops 6365773824 | bytes 14647296 | tf_op jit(solution)/shard_map/dot_general | solution.py:336
  465.3 8.8 %collective-permute-start.44 = (bf16[512,768]{1,0:T(8,128)(2,1)S(1)}, bf16[512,768]{1,0:T(8,128)(2,1)S(1)}, u32[]{:S(2)}, u32[]{:S(2)}) collective-permute-start(bf16[512,768]{1,0:T(8,128)(2,1)S(1)} %add_convert_fusion.10), channel_id=1, source_target_pairs={{0,8},{2,10},{4,12},{6,14},{8,0},{10,2},{12,4},{14,6},{16,24},{18,... | collective-permute-start | bytes 2359304 | tf_op jit(solution)/shard_map/ppermute | solution.py:150
  479.9 11.5 %collective-permute-done.44 = bf16[512,768]{1,0:T(8,128)(2,1)S(1)} collective-permute-done((bf16[512,768]{1,0:T(8,128)(2,1)S(1)}, bf16[512,768]{1,0:T(8,128)(2,1)S(1)}, u32[]{:S(2)}, u32[]{:S(2)}) %collective-permute-start.44) | collective-permute-done | bytes 786464 | tf_op jit(solution)/shard_map/ppermute | solution.py:150
  496.5 11.7 %collective-permute-done.37 = bf16[2,224,1536]{2,1,0:T(8,128)(2,1)S(1)} collective-permute-done((bf16[2,224,1536]{2,1,0:T(8,128)(2,1)S(1)}, bf16[2,224,1536]{2,1,0:T(8,128)(2,1)S(1)}, u32[]{:S(2)}, u32[]{:S(2)}) %collective-permute-start.37) | collective-permute-done | bytes 1376288 | tf_op jit(solution)/shard_map/ppermute | solution.py:154
  516.0 5.4 collective-permute-done.41
  535.4 17.7 %collective-permute-done.46 = bf16[2,192,1536]{2,1,0:T(8,128)(2,1)S(1)} collective-permute-done((bf16[2,192,1536]{2,1,0:T(8,128)(2,1)S(1)}, bf16[2,192,1536]{2,1,0:T(8,128)(2,1)S(1)}, u32[]{:S(2)}, u32[]{:S(2)}) %collective-permute-start.46) | collective-permute-done | bytes 1179680 | tf_op jit(solution)/shard_map/ppermute | solution.py:150
  553.2 5.5 place_home.1
  (426 shorter events, 237.6 us)
Async XLA Ops:
  13.3 46.8 %collective-permute-start.4 = (bf16[224,3072]{1,0:T(8,128)(2,1)}, bf16[224,3072]{1,0:T(8,128)(2,1)}, u32[]{:S(2)}, u32[]{:S(2)}) collective-permute-start(bf16[224,3072]{1,0:T(8,128)(2,1)} %get-tuple-element.143), channel_id=1, source_target_pairs={{0,4},{2,6},{4,0},{6,2},{8,12},{10,14},{12,8},{14,10},{16,20},{18,... | collective-permute-start | bytes 4128776 | tf_op jit(solution)/shard_map/ppermute | solution.py:150
  21.9 29.7 %collective-permute-start.3 = (bf16[2,112,1536]{2,1,0:T(8,128)(2,1)S(1)}, bf16[2,112,1536]{2,1,0:T(8,128)(2,1)S(1)}, u32[]{:S(2)}, u32[]{:S(2)}) collective-permute-start(bf16[2,112,1536]{2,1,0:T(8,128)(2,1)S(1)} %bitcast.182), channel_id=1, source_target_pairs={{0,8},{2,10},{4,12},{6,14},{8,0},{10,2},{12,4},{14,6},{16,24},{18,... | collective-permute-start | bytes 2064392 | tf_op jit(solution)/shard_map/ppermute | solution.py:150
  25.0 32.6 %collective-permute-start.1 = (bf16[2,112,1536]{2,1,0:T(8,128)(2,1)S(1)}, bf16[2,112,1536]{2,1,0:T(8,128)(2,1)S(1)}, u32[]{:S(2)}, u32[]{:S(2)}) collective-permute-start(bf16[2,112,1536]{2,1,0:T(8,128)(2,1)S(1)} %broadcast_select_fusion.18), channel_id=1, source_target_pairs={{0,16},{2,18},{4,20},{6,22},{8,24},{10,26},{12,28},{14,30},{16,0},... | collective-permute-start | bytes 2064392 | tf_op jit(solution)/shard_map/ppermute | solution.py:150
  29.2 41.7 %collective-permute-start.6 = (bf16[2,192,1536]{2,1,0:T(8,128)(2,1)S(1)}, bf16[2,192,1536]{2,1,0:T(8,128)(2,1)S(1)}, u32[]{:S(2)}, u32[]{:S(2)}) collective-permute-start(bf16[2,192,1536]{2,1,0:T(8,128)(2,1)S(1)} %pad_maximum_fusion.20), channel_id=1, source_target_pairs={{0,4},{2,6},{4,0},{6,2},{8,12},{10,14},{12,8},{14,10},{16,20},{18,... | collective-permute-start | bytes 3538952 | tf_op jit(solution)/shard_map/ppermute | solution.py:150
  57.8 46.1 %collective-permute-start.2 = (bf16[2,112,1536]{2,1,0:T(8,128)(2,1)S(1)}, bf16[2,112,1536]{2,1,0:T(8,128)(2,1)S(1)}, u32[]{:S(2)}, u32[]{:S(2)}) collective-permute-start(bf16[2,112,1536]{2,1,0:T(8,128)(2,1)S(1)} %broadcast_select_fusion.19), channel_id=1, source_target_pairs={{0,1},{1,0},{2,3},{3,2},{4,5},{5,4},{6,7},{7,6},{8,9},{9,8},{10,11... | collective-permute-start | bytes 2064392 | tf_op jit(solution)/shard_map/ppermute | solution.py:154
  60.1 25.1 %collective-permute-start.10 = (bf16[2,112,1536]{2,1,0:T(8,128)(2,1)S(1)}, bf16[2,112,1536]{2,1,0:T(8,128)(2,1)S(1)}, u32[]{:S(2)}, u32[]{:S(2)}) collective-permute-start(bf16[2,112,1536]{2,1,0:T(8,128)(2,1)S(1)} %broadcast_select_fusion.17), channel_id=1, source_target_pairs={{0,16},{2,18},{4,20},{6,22},{8,24},{10,26},{12,28},{14,30},{16,0},... | collective-permute-start | bytes 2064392 | tf_op jit(solution)/shard_map/ppermute | solution.py:150
  63.2 85.2 %collective-permute-start.20 = (bf16[2,224,3072]{2,1,0:T(8,128)(2,1)}, bf16[2,224,3072]{2,1,0:T(8,128)(2,1)}, u32[]{:S(2)}, u32[]{:S(2)}) collective-permute-start(bf16[2,224,3072]{2,1,0:T(8,128)(2,1)} %pad_maximum_fusion.5), channel_id=1, source_target_pairs={{0,2},{2,0},{4,6},{6,4},{8,10},{10,8},{12,14},{14,12},{16,18},{18,... | collective-permute-start | bytes 8257544 | tf_op jit(solution)/shard_map/ppermute | solution.py:150
  73.0 28.3 %collective-permute-start.11 = (bf16[768,512]{1,0:T(8,128)(2,1)S(1)}, bf16[768,512]{1,0:T(8,128)(2,1)S(1)}, u32[]{:S(2)}, u32[]{:S(2)}) collective-permute-start(bf16[768,512]{1,0:T(8,128)(2,1)S(1)} %pad_maximum_fusion.28), channel_id=1, source_target_pairs={{0,8},{2,10},{4,12},{6,14},{8,0},{10,2},{12,4},{14,6},{16,24},{18,... | collective-permute-start | bytes 2359304 | tf_op jit(solution)/shard_map/ppermute | solution.py:150
  86.2 39.9 %collective-permute-start.14 = (bf16[2,112,1536]{2,1,0:T(8,128)(2,1)}, bf16[2,112,1536]{2,1,0:T(8,128)(2,1)}, u32[]{:S(2)}, u32[]{:S(2)}) collective-permute-start(bf16[2,112,1536]{2,1,0:T(8,128)(2,1)} %broadcast_select_fusion.16), channel_id=1, source_target_pairs={{0,1},{1,0},{2,3},{3,2},{4,5},{5,4},{6,7},{7,6},{8,9},{9,8},{10,11... | collective-permute-start | bytes 2064392 | tf_op jit(solution)/shard_map/ppermute | solution.py:154
  89.1 27.2 %collective-permute-start.8 = (bf16[2,112,1536]{2,1,0:T(8,128)(2,1)S(1)}, bf16[2,112,1536]{2,1,0:T(8,128)(2,1)S(1)}, u32[]{:S(2)}, u32[]{:S(2)}) collective-permute-start(bf16[2,112,1536]{2,1,0:T(8,128)(2,1)S(1)} %collective-permute-done.7), channel_id=1, source_target_pairs={{0,1},{1,0},{2,3},{3,2},{4,5},{5,4},{6,7},{7,6},{8,9},{9,8},{10,11... | collective-permute-start | bytes 2064392 | tf_op jit(solution)/shard_map/ppermute | solution.py:154
  101.3 36.6 %collective-permute-start.13 = (bf16[2,768,512]{2,1,0:T(8,128)(2,1)}, bf16[2,768,512]{2,1,0:T(8,128)(2,1)}, u32[]{:S(2)}, u32[]{:S(2)}) collective-permute-start(bf16[2,768,512]{2,1,0:T(8,128)(2,1)} %pad_maximum_fusion.10), channel_id=1, source_target_pairs={{0,8},{2,10},{4,12},{6,14},{8,0},{10,2},{12,4},{14,6},{16,24},{18,... | collective-permute-start | bytes 4718600 | tf_op jit(solution)/shard_map/ppermute | solution.py:150
  126.1 27.3 %collective-permute-start.9 = (bf16[2,2,2,112,1536]{4,3,2,1,0:T(8,128)(2,1)S(1)}, bf16[2,2,2,112,1536]{4,3,2,1,0:T(8,128)(2,1)S(1)}, u32[]{:S(2)}, u32[]{:S(2)}) collective-permute-start(bf16[2,2,2,112,1536]{4,3,2,1,0:T(8,128)(2,1)S(1)} %bitcast.156), channel_id=1, source_target_pairs={{0,2},{2,0},{4,6},{6,4},{8,10},{10,8},{12,14},{14,12},{16,18},{18,... | collective-permute-start | bytes 8257544 | tf_op jit(solution)/shard_map/ppermute | solution.py:150
  137.9 31.2 %collective-permute-start.21 = (bf16[224,3072]{1,0:T(8,128)(2,1)S(1)}, bf16[224,3072]{1,0:T(8,128)(2,1)S(1)}, u32[]{:S(2)}, u32[]{:S(2)}) collective-permute-start(bf16[224,3072]{1,0:T(8,128)(2,1)S(1)} %copy-done.59), channel_id=1, source_target_pairs={{0,4},{2,6},{4,0},{6,2},{8,12},{10,14},{12,8},{14,10},{16,20},{18,... | collective-permute-start | bytes 4128776 | tf_op jit(solution)/shard_map/ppermute | solution.py:150
  150.9 46.7 %collective-permute-start.18 = (bf16[1536,512]{1,0:T(8,128)(2,1)}, bf16[1536,512]{1,0:T(8,128)(2,1)S(1)}, u32[]{:S(2)}, u32[]{:S(2)}) collective-permute-start(bf16[1536,512]{1,0:T(8,128)(2,1)} %collective-permute-done.12), channel_id=1, source_target_pairs={{8,0},{10,2},{12,4},{14,6},{16,24},{18,26},{20,28},{22,30},{9,1},{... | collective-permute-start | bytes 4718600 | tf_op jit(solution)/shard_map/ppermute | solution.py:163
  198.1 53.5 %collective-permute-start.24 = (bf16[1536,512]{1,0:T(8,128)(2,1)S(1)}, bf16[1536,512]{1,0:T(8,128)(2,1)}, u32[]{:S(2)}, u32[]{:S(2)}) collective-permute-start(bf16[1536,512]{1,0:T(8,128)(2,1)S(1)} %pad_maximum_fusion.12), channel_id=1, source_target_pairs={{8,16},{10,18},{12,20},{14,22},{16,8},{18,10},{20,12},{22,14},{9,1... | collective-permute-start | bytes 4718600 | tf_op jit(solution)/shard_map/ppermute | solution.py:163
  200.0 51.6 %collective-permute-start.23 = (bf16[1536,512]{1,0:T(8,128)(2,1)}, bf16[1536,512]{1,0:T(8,128)(2,1)}, u32[]{:S(2)}, u32[]{:S(2)}) collective-permute-start(bf16[1536,512]{1,0:T(8,128)(2,1)} %collective-permute-done.19), channel_id=1, source_target_pairs={{8,0},{10,2},{12,4},{14,6},{16,24},{18,26},{20,28},{22,30},{9,1},{... | collective-permute-start | bytes 4718600 | tf_op jit(solution)/shard_map/ppermute | solution.py:163
  262.9 40.8 %collective-permute-start.26 = (bf16[512,1536]{1,0:T(8,128)(2,1)}, bf16[512,1536]{1,0:T(8,128)(2,1)}, u32[]{:S(2)}, u32[]{:S(2)}) collective-permute-start(bf16[512,1536]{1,0:T(8,128)(2,1)} %pad_maximum_fusion.13), channel_id=1, source_target_pairs={{0,8},{2,10},{4,12},{6,14},{24,16},{26,18},{28,20},{30,22},{1,9},{... | collective-permute-start | bytes 4718600 | tf_op jit(solution)/shard_map/ppermute | solution.py:163
  269.9 38.7 %collective-permute-start.25 = (bf16[1536,512]{1,0:T(8,128)(2,1)}, bf16[1536,512]{1,0:T(8,128)(2,1)}, u32[]{:S(2)}, u32[]{:S(2)}) collective-permute-start(bf16[1536,512]{1,0:T(8,128)(2,1)} %collective-permute-done.24), channel_id=1, source_target_pairs={{8,0},{10,2},{12,4},{14,6},{16,24},{18,26},{20,28},{22,30},{9,1},{... | collective-permute-start | bytes 4718600 | tf_op jit(solution)/shard_map/ppermute | solution.py:163
  295.3 41.7 %collective-permute-start.27 = (bf16[512,1536]{1,0:T(8,128)(2,1)}, bf16[512,1536]{1,0:T(8,128)(2,1)}, u32[]{:S(2)}, u32[]{:S(2)}) collective-permute-start(bf16[512,1536]{1,0:T(8,128)(2,1)} %pad_maximum_fusion.14), channel_id=1, source_target_pairs={{0,8},{2,10},{4,12},{6,14},{24,16},{26,18},{28,20},{30,22},{1,9},{... | collective-permute-start | bytes 4718600 | tf_op jit(solution)/shard_map/ppermute | solution.py:163
  341.9 35.6 %collective-permute-start.28 = (bf16[2,448,3072]{2,1,0:T(8,128)(2,1)}, bf16[2,448,3072]{2,1,0:T(8,128)(2,1)}, u32[]{:S(2)}, u32[]{:S(2)}) collective-permute-start(bf16[2,448,3072]{2,1,0:T(8,128)(2,1)} %bitcast.196), channel_id=1, source_target_pairs={{0,2},{2,0},{4,6},{6,4},{8,10},{10,8},{12,14},{14,12},{16,18},{18,... | collective-permute-start | bytes 16515080 | tf_op jit(solution)/shard_map/ppermute | solution.py:150
  347.5 49.9 %collective-permute-start.31 = (bf16[512,1536]{1,0:T(8,128)(2,1)}, bf16[512,1536]{1,0:T(8,128)(2,1)}, u32[]{:S(2)}, u32[]{:S(2)}) collective-permute-start(bf16[512,1536]{1,0:T(8,128)(2,1)} %add_convert_fusion.4), channel_id=1, source_target_pairs={{8,16},{10,18},{12,20},{14,22},{16,8},{18,10},{20,12},{22,14},{9,1... | collective-permute-start | bytes 4718600 | tf_op jit(solution)/shard_map/ppermute | solution.py:163
  352.6 44.8 %collective-permute-start.32 = (bf16[512,1536]{1,0:T(8,128)(2,1)}, bf16[512,1536]{1,0:T(8,128)(2,1)}, u32[]{:S(2)}, u32[]{:S(2)}) collective-permute-start(bf16[512,1536]{1,0:T(8,128)(2,1)} %add_convert_fusion.3), channel_id=1, source_target_pairs={{8,16},{10,18},{12,20},{14,22},{16,8},{18,10},{20,12},{22,14},{9,1... | collective-permute-start | bytes 4718600 | tf_op jit(solution)/shard_map/ppermute | solution.py:163
  366.8 41.0 %collective-permute-start.30 = (bf16[512,1536]{1,0:T(8,128)(2,1)}, bf16[512,1536]{1,0:T(8,128)(2,1)}, u32[]{:S(2)}, u32[]{:S(2)}) collective-permute-start(bf16[512,1536]{1,0:T(8,128)(2,1)} %pad_maximum_fusion.15), channel_id=1, source_target_pairs={{0,8},{2,10},{4,12},{6,14},{24,16},{26,18},{28,20},{30,22},{1,9},{... | collective-permute-start | bytes 4718600 | tf_op jit(solution)/shard_map/ppermute | solution.py:163
  380.4 34.6 %collective-permute-start.34 = (bf16[224,3072]{1,0:T(8,128)(2,1)}, bf16[224,3072]{1,0:T(8,128)(2,1)}, u32[]{:S(2)}, u32[]{:S(2)}) collective-permute-start(bf16[224,3072]{1,0:T(8,128)(2,1)} %fusion.6), channel_id=1, source_target_pairs={{0,4},{2,6},{4,0},{6,2},{8,12},{10,14},{12,8},{14,10},{16,20},{18,... | collective-permute-start | bytes 4128776 | tf_op jit(solution)/shard_map/ppermute | solution.py:150
  385.5 31.8 %collective-permute-start.29 = (bf16[2,224,1536]{2,1,0:T(8,128)(2,1)}, bf16[2,224,1536]{2,1,0:T(8,128)(2,1)}, u32[]{:S(2)}, u32[]{:S(2)}) collective-permute-start(bf16[2,224,1536]{2,1,0:T(8,128)(2,1)} %constant_dynamic-slice_fusion.19), channel_id=1, source_target_pairs={{0,1},{1,0},{2,3},{3,2},{4,5},{5,4},{6,7},{7,6},{8,9},{9,8},{10,11... | collective-permute-start | bytes 4128776 | tf_op jit(solution)/shard_map/ppermute | solution.py:154
  417.3 42.7 %collective-permute-start.36 = (bf16[2,448,3072]{2,1,0:T(8,128)(2,1)}, bf16[2,448,3072]{2,1,0:T(8,128)(2,1)S(1)}, u32[]{:S(2)}, u32[]{:S(2)}) collective-permute-start(bf16[2,448,3072]{2,1,0:T(8,128)(2,1)} %bitcast.46), channel_id=1, source_target_pairs={{0,2},{2,0},{4,6},{6,4},{8,10},{10,8},{12,14},{14,12},{16,18},{18,... | collective-permute-start | bytes 16515080 | tf_op jit(solution)/shard_map/ppermute | solution.py:150
  420.9 42.0 %collective-permute-start.38 = (bf16[512,1536]{1,0:T(8,128)(2,1)}, bf16[512,1536]{1,0:T(8,128)(2,1)}, u32[]{:S(2)}, u32[]{:S(2)}) collective-permute-start(bf16[512,1536]{1,0:T(8,128)(2,1)} %add_convert_fusion.2), channel_id=1, source_target_pairs={{8,16},{10,18},{12,20},{14,22},{16,8},{18,10},{20,12},{22,14},{9,1... | collective-permute-start | bytes 4718600 | tf_op jit(solution)/shard_map/ppermute | solution.py:163
  422.7 52.7 %collective-permute-start.43 = (bf16[1024,768]{1,0:T(8,128)(2,1)}, bf16[1024,768]{1,0:T(8,128)(2,1)}, u32[]{:S(2)}, u32[]{:S(2)}) collective-permute-start(bf16[1024,768]{1,0:T(8,128)(2,1)} %pad_maximum_fusion.16), channel_id=1, source_target_pairs={{0,8},{2,10},{4,12},{6,14},{8,0},{10,2},{12,4},{14,6},{16,24},{18,... | collective-permute-start | bytes 4718600 | tf_op jit(solution)/shard_map/ppermute | solution.py:150
  460.6 32.5 %collective-permute-start.40 = (bf16[224,3072]{1,0:T(8,128)(2,1)S(1)}, bf16[224,3072]{1,0:T(8,128)(2,1)S(1)}, u32[]{:S(2)}, u32[]{:S(2)}) collective-permute-start(bf16[224,3072]{1,0:T(8,128)(2,1)S(1)} %fusion.8), channel_id=1, source_target_pairs={{0,4},{2,6},{4,0},{6,2},{8,12},{10,14},{12,8},{14,10},{16,20},{18,... | collective-permute-start | bytes 4128776 | tf_op jit(solution)/shard_map/ppermute | solution.py:150
  465.3 26.2 %collective-permute-start.44 = (bf16[512,768]{1,0:T(8,128)(2,1)S(1)}, bf16[512,768]{1,0:T(8,128)(2,1)S(1)}, u32[]{:S(2)}, u32[]{:S(2)}) collective-permute-start(bf16[512,768]{1,0:T(8,128)(2,1)S(1)} %add_convert_fusion.10), channel_id=1, source_target_pairs={{0,8},{2,10},{4,12},{6,14},{8,0},{10,2},{12,4},{14,6},{16,24},{18,... | collective-permute-start | bytes 2359304 | tf_op jit(solution)/shard_map/ppermute | solution.py:150
  475.1 33.1 %collective-permute-start.37 = (bf16[2,224,1536]{2,1,0:T(8,128)(2,1)S(1)}, bf16[2,224,1536]{2,1,0:T(8,128)(2,1)S(1)}, u32[]{:S(2)}, u32[]{:S(2)}) collective-permute-start(bf16[2,224,1536]{2,1,0:T(8,128)(2,1)S(1)} %constant_dynamic-slice_fusion.12), channel_id=1, source_target_pairs={{0,1},{1,0},{2,3},{3,2},{4,5},{5,4},{6,7},{7,6},{8,9},{9,8},{10,11... | collective-permute-start | bytes 4128776 | tf_op jit(solution)/shard_map/ppermute | solution.py:154
  496.2 25.2 %collective-permute-start.41 = (bf16[224,1536]{1,0:T(8,128)(2,1)}, bf16[224,1536]{1,0:T(8,128)(2,1)}, u32[]{:S(2)}, u32[]{:S(2)}) collective-permute-start(bf16[224,1536]{1,0:T(8,128)(2,1)} %dynamic-slice_convert_fusion), channel_id=1, source_target_pairs={{0,1},{1,0},{2,3},{3,2},{4,5},{5,4},{6,7},{7,6},{8,9},{9,8},{10,11... | collective-permute-start | bytes 2064392 | tf_op jit(solution)/shard_map/ppermute | solution.py:154
  (113 other events, 1316.2 us)

commit v3 on v2

--- a/solution.py
+++ b/solution.py
@@ -227,10 +227,12 @@
         self.sent = self.columns(self.far, 2)
         self.arrived = send_planes(self.sent, [(0, 1), (3, 2)])
 
-    def cross(self, *earlier):
+    def add_far(self, *earlier):
         far = add_rounded(self.columns(self.far, 2), after(self.arrived, *earlier))
         self.cross_sent = far
-        self.crossed = send_planes(far, [(1, 2), (2, 1)])
+
+    def cross(self, *earlier):
+        self.crossed = send_planes(after(self.cross_sent, *earlier), [(1, 2), (2, 1)])
 
     def of_pair(self, plane, *earlier):
         crossed = after(self.crossed, *earlier)
@@ -238,16 +240,19 @@
         return self.columns(plane, 1).astype(jnp.float32) + crossed.astype(jnp.float32)
 
 
-def reduce_pairs(reduces, my_plane, *earlier):
-    sent = jnp.concatenate([reduce.of_pair(my_plane ^ 1, *earlier) for reduce in reduces])
-    sent = sent.astype(jnp.bfloat16)
-    got = swap_fsdp(sent, PLANE)
-
-    def total(*later):
-        kept = jnp.concatenate([reduce.of_pair(my_plane, *later) for reduce in reduces])
-        return (kept + after(got, *later).astype(jnp.float32)).astype(jnp.bfloat16)
-
-    return (sent, total)
+class PairReduce:
+    def __init__(self, reduces, my_plane, *earlier):
+        self.reduces, self.my_plane = (reduces, my_plane)
+        sent = jnp.concatenate([reduce.of_pair(my_plane ^ 1, *earlier) for reduce in reduces])
+        self.sent = sent.astype(jnp.bfloat16)
+
+    def send(self, *earlier):
+        self.got = swap_fsdp(after(self.sent, *earlier), PLANE)
+
+    def total(self, *later):
+        kept = [reduce.of_pair(self.my_plane, *later) for reduce in self.reduces]
+        got = after(self.got, *later).astype(jnp.float32)
+        return (jnp.concatenate(kept) + got).astype(jnp.bfloat16)
 
 
 def rows_kernel(parts, pick_ref, count_ref, *refs):
@@ -602,8 +607,9 @@
 
     upstream_own = jnp.where(is_live[:, None], cotangent, jnp.zeros((), cotangent.dtype))
     up_far = [swap_fsdp(upstream_own[:part_rows], 2)]
+    up_near = swap_fsdp(after(upstream_own, first_moved), 1)
     shards = spread_places([head_columns(my_place ^ step) for step in range(PLANE)])
-    shards = [after(shard, first_moved, up_far[0]) for shard in shards]
+    shards = [after(shard, first_moved, up_near, up_far[0]) for shard in shards]
     plane_shard = jnp.zeros((PLANE, shard_rows, heads * head_width), qkv_weight.dtype)
     for step in range(PLANE):
         plane_shard = lax.dynamic_update_index_in_dim(
@@ -660,13 +666,8 @@
     gathers[1].spread(normed)
     gathers[2].cross(normed)
     up_far[1] = after(up_far[1], normed)
-    up_other = [
-        swap_fsdp(jnp.stack([upstream_own[:part_rows], up_far[0]]), 1),
-        swap_fsdp(jnp.stack([upstream_own[part_rows:], up_far[1]]), 1),
-    ]
-    upstream = jnp.concatenate(
-        [up_other[0][0], up_other[1][0], up_other[0][1], up_other[1][1], upstream_own, *up_far]
-    )
+    up_both = [swap_fsdp(after(up_far[0], normed), 1), swap_fsdp(up_far[1], 1)]
+    upstream = jnp.concatenate([up_near, *up_both, upstream_own, *up_far])
 
     scales = jnp.concatenate([qk_gain[0:1] * head_dim ** (-0.5), qk_gain[1:2]])
     weights, mixed_parts, back_parts, reduces = ([], [], [], [])
@@ -686,13 +687,16 @@
         back_parts.append(back)
         held_back, held_mixed = (back, mixed)
         if head == 2:
-            mixed_all = after(jnp.concatenate(mixed_parts, axis=1), reduces[1].arrived)
+            mixed_all = after(
+                jnp.concatenate(mixed_parts, axis=1), reduces[1].arrived, reduces[0].crossed
+            )
             out_all = jnp.concatenate([weight[:, qkv_width:] for weight in weights], axis=1)
             out_sent = mm(mixed_all[: 2 * tok_rows], out_all, 1, 1).astype(jnp.bfloat16)
             out_scatter = PlaneScatter(
                 out_sent.reshape(2, tok_rows, model_width), share_width, my_group
             )
-            reduces[1].cross(out_sent)
+            reduces[1].add_far(out_sent)
+            reduces[1].cross()
             held = after(mixed_all[2 * tok_rows :], out_sent, reduces[1].cross_sent)
             out_kept = mm(held, out_all, 1, 1).astype(jnp.bfloat16)
             held_back = after(held_back, out_kept)
@@ -700,7 +704,8 @@
         qkv_term = mm(held_back, normed, 0, 0).astype(jnp.bfloat16)
         out_term = mm(held_mixed, upstream, 0, 0).astype(jnp.bfloat16)
         if head == 1:
-            reduces[0].cross(qkv_term, out_term)
+            reduces[0].add_far(qkv_term, out_term)
+            reduces[0].cross()
         reduces.append(LineReduce([qkv_term, out_term], my_plane))
         reduces[head].inward()
 
@@ -721,9 +726,9 @@
     )
     held = after(back_all[: 2 * tok_rows], *out_added, reduces[2].sent)
     back_sent = mm(held, qkv_all, 1, 1).astype(jnp.bfloat16)
-    reduces[2].cross(back_sent)
-    sent, early_total = reduce_pairs(reduces[:2], my_plane, back_sent)
-    between = (reduces[2].cross_sent, sent)
+    reduces[2].add_far(back_sent)
+    early = PairReduce(reduces[:2], my_plane, back_sent)
+    between = (reduces[2].cross_sent, early.sent)
     back_scatter = PlaneScatter(
         after(
             back_sent.reshape(2, tok_rows, model_width),
@@ -735,17 +740,23 @@
         my_group,
     )
     turned = out_scatter.turn(*between)
+    reduces[2].cross(*turned)
+    early.send(*turned)
     held = after(back_all[2 * tok_rows :], *turned)
     back_kept = mm(held, qkv_all, 1, 1).astype(jnp.bfloat16)
     back_added = back_scatter.add_cores(
         after(
-            back_kept.reshape(2, tok_rows, model_width), out_scatter.last_x, out_scatter.last_y
-        )
-    )
-    sent, late_total = reduce_pairs(reduces[2:], my_plane, *back_added)
-    total = jnp.concatenate([early_total(*back_added), late_total(*back_added)])
-    back_scatter.turn(sent)
-    home = send_home(after(total, back_scatter.over_x, back_scatter.over_y))
+            back_kept.reshape(2, tok_rows, model_width),
+            out_scatter.last_x,
+            out_scatter.last_y,
+            reduces[2].crossed,
+        )
+    )
+    late = PairReduce(reduces[2:], my_plane, *back_added)
+    late.send()
+    turned = back_scatter.turn(late.sent)
+    total = jnp.concatenate([early.total(*back_added), late.total(*turned)])
+    home = send_home(after(total, *turned))
     attended = out_scatter.total()
     attended = jnp.where(is_live[:, None], attended, 0.0).astype(jnp.bfloat16)
     grad_normed = back_scatter.total()

time: 567 us -> 545 us (0.961)
  the two profiles are of different devices: /device:TPU:0 before, /device:TPU:20 now
where the time goes in v3:
time: 545 us; the launch traced here: 536 us
  waiting for transfers between devices  214 us (39%)
  matrix products  78 us (14%)
  other arithmetic  75.3 us (14%)
  starting transfers between devices  61.8 us (11%)
  Pallas kernels  50.6 us (9%)
  local copies, waits for them, and re-layouts  48.4 us (9%)
  between operations  7.34 us (1%)
    ppermute x27, waiting for transfers between devices, swap_fsdp(): return lax.ppermute(value, 'fsdp', pairs)  133 us
    dot_general x16, matrix products, mm(): lax.dot_general(left, right, (((left_dim,), (right_dim,)), ((), ())), pre...  78 us
    ppermute x12, waiting for transfers between devices, send_planes(): return lax.ppermute(value, 'fsdp', pairs)  68.1 us
    ppermute x12, starting transfers between devices, send_planes(): return lax.ppermute(value, 'fsdp', pairs)  33.3 us
    pallas_call x3, Pallas kernels, attend(): pl.pallas_call(functools.partial(attention_kernel, per_step), grid_spec=p...  31.4 us
    ppermute x27, starting transfers between devices, swap_fsdp(): return lax.ppermute(value, 'fsdp', pairs)  17.5 us
    convert_element_type x7, other arithmetic, add_rounded(): (left.astype(jnp.float32) + right.astype(jnp.float32)).astype(jnp.bfloat16)  16.8 us
    unnamed x180, local copies, waits for them, and re-layouts  14.8 us
  transfers between devices with their start and end apart: 48, of which 22 were waited for; matrix products, arithmetic and copies ran while one was open for 34% of the time, Pallas kernels for 8%

profile of v3, /device:TPU:20, one launch (start us, length us, event | category | flops | bytes accessed | tf_op | source)
XLA Modules:
  0.0 536.0 jit_solution(14978037161206331825)
XLA Ops:
  12.0 8.5 %collective-permute-done = bf16[2,112,1536]{2,1,0:T(8,128)(2,1)} collective-permute-done((bf16[2,112,1536]{2,1,0:T(8,128)(2,1)}, bf16[2,112,1536]{2,1,0:T(8,128)(2,1)}, u32[]{:S(2)}, u32[]{:S(2)}) %collective-permute-start) | collective-permute-done | bytes 688160 | tf_op jit(solution)/shard_map/ppermute | solution.py:150
  26.2 28.5 %collective-permute-done.3 = bf16[2,112,1536]{2,1,0:T(8,128)(2,1)S(1)} collective-permute-done((bf16[2,112,1536]{2,1,0:T(8,128)(2,1)S(1)}, bf16[2,112,1536]{2,1,0:T(8,128)(2,1)S(1)}, u32[]{:S(2)}, u32[]{:S(2)}) %collective-permute-start.3) | collective-permute-done | bytes 688160 | tf_op jit(solution)/shard_map/ppermute | solution.py:150
  58.2 10.8 %collective-permute-done.7 = bf16[2,192,1536]{2,1,0:T(8,128)(2,1)S(1)} collective-permute-done((bf16[2,192,1536]{2,1,0:T(8,128)(2,1)S(1)}, bf16[2,192,1536]{2,1,0:T(8,128)(2,1)S(1)}, u32[]{:S(2)}, u32[]{:S(2)}) %collective-permute-start.7) | collective-permute-done | bytes 1179680 | tf_op jit(solution)/shard_map/ppermute | solution.py:150
  72.5 14.3 %collective-permute-done.11 = bf16[2,112,1536]{2,1,0:T(8,128)(2,1)S(1)} collective-permute-done((bf16[2,112,1536]{2,1,0:T(8,128)(2,1)S(1)}, bf16[2,112,1536]{2,1,0:T(8,128)(2,1)S(1)}, u32[]{:S(2)}, u32[]{:S(2)}) %collective-permute-start.11) | collective-permute-done | bytes 688160 | tf_op jit(solution)/shard_map/ppermute | solution.py:150
  91.4 11.6 %collective-permute-done.12 = bf16[768,512]{1,0:T(8,128)(2,1)S(1)} collective-permute-done((bf16[768,512]{1,0:T(8,128)(2,1)S(1)}, bf16[768,512]{1,0:T(8,128)(2,1)S(1)}, u32[]{:S(2)}, u32[]{:S(2)}) %collective-permute-start.12) | collective-permute-done | bytes 786464 | tf_op jit(solution)/shard_map/ppermute | solution.py:150
  113.1 5.7 %collective-permute-done.9 = bf16[2,112,1536]{2,1,0:T(8,128)(2,1)S(1)} collective-permute-done((bf16[2,112,1536]{2,1,0:T(8,128)(2,1)}, bf16[2,112,1536]{2,1,0:T(8,128)(2,1)S(1)}, u32[]{:S(2)}, u32[]{:S(2)}) %collective-permute-start.9) | collective-permute-done | bytes 688160 | tf_op jit(solution)/shard_map/ppermute | solution.py:154
  128.1 12.7 %collective-permute-done.14 = bf16[2,768,512]{2,1,0:T(8,128)(2,1)} collective-permute-done((bf16[2,768,512]{2,1,0:T(8,128)(2,1)}, bf16[2,768,512]{2,1,0:T(8,128)(2,1)}, u32[]{:S(2)}, u32[]{:S(2)}) %collective-permute-start.14) | collective-permute-done | bytes 1572896 | tf_op jit(solution)/shard_map/ppermute | solution.py:150
  161.6 13.7 %norm_rows.1 = (bf16[1792,3072]{1,0:T(8,128)(2,1)S(1)}, f32[1792,128]{1,0:T(8,128)S(1)}) custom-call(s32[17]{0:T(128)S(1)} %pad_add_fusion.pick_ref, s32[16]{0:T(128)S(1)} %reshape.170.count_ref, bf16[2,2,2,112,1536]{4,3,2,1,0:T(8,128)(2,1)S(1)} %bitcast.136, bf16[2,2,2,112,1536]{4,3,2,1,0:T(8,128)(2,1)S(1)} %bitcast.137, ...), custom_call_target="tpu_custom_call" | custom-call | flops 55050240 | bytes 33030144 | tf_op jit(solution)/shard_map/norm_rows/pallas_call | solution.py:318
  175.3 15.2 %collective-permute-done.20 = bf16[1536,512]{1,0:T(8,128)(2,1)} collective-permute-done((bf16[1536,512]{1,0:T(8,128)(2,1)}, bf16[1536,512]{1,0:T(8,128)(2,1)}, u32[]{:S(2)}, u32[]{:S(2)}) %collective-permute-start.20) | collective-permute-done | bytes 1572896 | tf_op jit(solution)/shard_map/ppermute | solution.py:163
  206.9 5.9 %fusion.34.proj_ref = f32[1792,384]{1,0:T(8,128)S(1)} fusion(bf16[1792,3072]{1,0:T(8,128)(2,1)S(1)} %get-tuple-element.81, bf16[3072,384]{1,0:T(8,128)(2,1)S(1)} %fusion.4), kind=kOutput, calls=%fused_computation.213 | convolution fusion | flops 4227858432 | bytes 16121856 | tf_op jit(solution)/shard_map/dot_general | solution.py:341
  221.5 10.6 %attend_images.3 = (bf16[1792,128]{1,0:T(8,128)(2,1)S(1)}, bf16[1792,384]{1,0:T(8,128)(2,1)S(1)}) custom-call(s32[16]{0:T(128)S(1)} %reshape.169.count_ref, f32[1792,384]{1,0:T(8,128)S(1)} %fusion.34.proj_ref, bf16[1792,128]{1,0:T(8,128)(2,1)S(1)} %convolution_convert_fusion.12.grad_ref, f32[2,128]{1,0:T(2,128)S(1)} %pad_maximum_fusion.31.scale_ref), custom_call_target="tpu_custom_call" | custom-call | flops 308281344 | bytes 5505024 | tf_op jit(solution)/shard_map/attend_images/pallas_call | solution.py:403
  233.8 4.7 convolution_convert_fusion.6
  249.5 7.0 %collective-permute-start.26 = (bf16[1536,512]{1,0:T(8,128)(2,1)}, bf16[1536,512]{1,0:T(8,128)(2,1)}, u32[]{:S(2)}, u32[]{:S(2)}) collective-permute-start(bf16[1536,512]{1,0:T(8,128)(2,1)} %collective-permute-done.25), channel_id=1, source_target_pairs={{8,0},{10,2},{12,4},{14,6},{16,24},{18,26},{20,28},{22,30},{9,1},{... | collective-permute-start | bytes 4718600 | tf_op jit(solution)/shard_map/ppermute | solution.py:163
  256.5 6.1 %fusion.35.proj_ref = f32[1792,384]{1,0:T(8,128)S(1)} fusion(bf16[1792,3072]{1,0:T(8,128)(2,1)S(1)} %get-tuple-element.81, bf16[3072,384]{1,0:T(8,128)(2,1)S(1)} %copy-done.35), kind=kOutput, calls=%fused_computation.214 | convolution fusion | flops 4227858432 | bytes 16121856 | tf_op jit(solution)/shard_map/dot_general | solution.py:341
  262.6 10.2 %attend_images.4 = (bf16[1792,128]{1,0:T(8,128)(2,1)S(1)}, bf16[1792,384]{1,0:T(8,128)(2,1)S(1)}) custom-call(s32[16]{0:T(128)S(1)} %reshape.169.count_ref, f32[1792,384]{1,0:T(8,128)S(1)} %fusion.35.proj_ref, bf16[1792,128]{1,0:T(8,128)(2,1)S(1)} %convolution_convert_fusion.11.grad_ref, f32[2,128]{1,0:T(2,128)S(1)} %pad_maximum_fusion.31.scale_ref), custom_call_target="tpu_custom_call" | custom-call | flops 308281344 | bytes 5505024 | tf_op jit(solution)/shard_map/attend_images/pallas_call | solution.py:403
  272.8 5.8 %convolution_convert_fusion.5 = bf16[384,3072]{1,0:T(8,128)(2,1)} fusion(bf16[1792,384]{1,0:T(8,128)(2,1)S(1)} %get-tuple-element.95, bf16[1792,3072]{1,0:T(8,128)(2,1)S(1)} %get-tuple-element.81), kind=kOutput, calls=%fused_computation.8 | convolution fusion | flops 4229038080 | bytes 14745600 | tf_op jit(solution)/shard_map/dot_general | solution.py:341
  296.0 5.9 %fusion.36.proj_ref = f32[1792,384]{1,0:T(8,128)S(1)} fusion(bf16[1792,3072]{1,0:T(8,128)(2,1)S(1)} %get-tuple-element.81, bf16[3072,384]{1,0:T(8,128)(2,1)S(1)} %fusion.2), kind=kOutput, calls=%fused_computation.215 | convolution fusion | flops 4227858432 | bytes 16121856 | tf_op jit(solution)/shard_map/dot_general | solution.py:341
  302.0 10.6 %attend_images.5 = (bf16[1792,128]{1,0:T(8,128)(2,1)S(1)}, bf16[1792,384]{1,0:T(8,128)(2,1)S(1)}) custom-call(s32[16]{0:T(128)S(1)} %reshape.169.count_ref, f32[1792,384]{1,0:T(8,128)S(1)} %fusion.36.proj_ref, bf16[1792,128]{1,0:T(8,128)(2,1)S(1)} %convolution_convert_fusion.10.grad_ref, f32[2,128]{1,0:T(2,128)S(1)} %pad_maximum_fusion.31.scale_ref), custom_call_target="tpu_custom_call" | custom-call | flops 308281344 | bytes 5505024 | tf_op jit(solution)/shard_map/attend_images/pallas_call | solution.py:403
  312.8 6.5 %collective-permute-done.28 = bf16[512,1536]{1,0:T(8,128)(2,1)} collective-permute-done((bf16[512,1536]{1,0:T(8,128)(2,1)}, bf16[512,1536]{1,0:T(8,128)(2,1)}, u32[]{:S(2)}, u32[]{:S(2)}) %collective-permute-start.28) | collective-permute-done | bytes 1572896 | tf_op jit(solution)/shard_map/ppermute | solution.py:163
  323.5 4.9 convolution_convert_fusion.3
  338.4 4.9 convolution_convert_fusion.2
  348.6 4.7 convolution_convert_fusion.4
  365.0 10.8 %convolution_convert_fusion.1 = bf16[896,3072]{1,0:T(8,128)(2,1)} fusion(bf16[896,1152]{1,0:T(8,128)(2,1)} %get-tuple-element.107, bf16[3072,384]{1,0:T(8,128)(2,1)S(1)} %copy-done.38, bf16[3072,384]{1,0:T(8,128)(2,1)S(1)} %copy-done.36, bf16[3072,384]{1,0:T(8,128)(2,1)S(1)} %copy-done.34), kind=kOutput, calls=%fused_computation.4 | convolution fusion | flops 6365773824 | bytes 14647296 | tf_op jit(solution)/shard_map/dot_general | solution.py:341
  375.8 6.5 %collective-permute-done.33 = bf16[512,1536]{1,0:T(8,128)(2,1)} collective-permute-done((bf16[512,1536]{1,0:T(8,128)(2,1)}, bf16[512,1536]{1,0:T(8,128)(2,1)}, u32[]{:S(2)}, u32[]{:S(2)}) %collective-permute-start.33) | collective-permute-done | bytes 1572896 | tf_op jit(solution)/shard_map/ppermute | solution.py:163
  382.3 9.8 %collective-permute-done.32 = bf16[512,1536]{1,0:T(8,128)(2,1)} collective-permute-done((bf16[512,1536]{1,0:T(8,128)(2,1)S(1)}, bf16[512,1536]{1,0:T(8,128)(2,1)}, u32[]{:S(2)}, u32[]{:S(2)}) %collective-permute-start.32) | collective-permute-done | bytes 1572896 | tf_op jit(solution)/shard_map/ppermute | solution.py:163
  413.4 10.1 %convolution_convert_fusion = bf16[896,3072]{1,0:T(8,128)(2,1)S(1)} fusion(bf16[896,1152]{1,0:T(8,128)(2,1)} %get-tuple-element.114, bf16[3072,384]{1,0:T(8,128)(2,1)} %copy-done.37, bf16[3072,384]{1,0:T(8,128)(2,1)} %fusion.3, bf16[3072,384]{1,0:T(8,128)(2,1)S(1)} %copy-done.34), kind=kOutput, calls=%fused_computation.3 | convolution fusion | flops 6365773824 | bytes 14647296 | tf_op jit(solution)/shard_map/dot_general | solution.py:341
  428.1 21.5 %collective-permute-done.37 = bf16[512,1536]{1,0:T(8,128)(2,1)} collective-permute-done((bf16[512,1536]{1,0:T(8,128)(2,1)}, bf16[512,1536]{1,0:T(8,128)(2,1)}, u32[]{:S(2)}, u32[]{:S(2)}) %collective-permute-start.37) | collective-permute-done | bytes 1572896 | tf_op jit(solution)/shard_map/ppermute | solution.py:163
  452.0 7.5 %collective-permute-done.44 = bf16[1024,768]{1,0:T(8,128)(2,1)S(1)} collective-permute-done((bf16[1024,768]{1,0:T(8,128)(2,1)S(1)}, bf16[1024,768]{1,0:T(8,128)(2,1)S(1)}, u32[]{:S(2)}, u32[]{:S(2)}) %collective-permute-start.44) | collective-permute-done | bytes 1572896 | tf_op jit(solution)/shard_map/ppermute | solution.py:150
  464.4 17.0 %collective-permute-done.41 = bf16[224,3072]{1,0:T(8,128)(2,1)S(1)} collective-permute-done((bf16[224,3072]{1,0:T(8,128)(2,1)S(1)}, bf16[224,3072]{1,0:T(8,128)(2,1)S(1)}, u32[]{:S(2)}, u32[]{:S(2)}) %collective-permute-start.41) | collective-permute-done | bytes 1376288 | tf_op jit(solution)/shard_map/ppermute | solution.py:150
  492.8 6.1 %collective-permute-done.42 = bf16[224,1536]{1,0:T(8,128)(2,1)} collective-permute-done((bf16[224,1536]{1,0:T(8,128)(2,1)}, bf16[224,1536]{1,0:T(8,128)(2,1)}, u32[]{:S(2)}, u32[]{:S(2)}) %collective-permute-start.42) | collective-permute-done | bytes 688160 | tf_op jit(solution)/shard_map/ppermute | solution.py:154
  510.9 19.3 %collective-permute-done.47 = bf16[2,192,1536]{2,1,0:T(8,128)(2,1)S(1)} collective-permute-done((bf16[2,192,1536]{2,1,0:T(8,128)(2,1)S(1)}, bf16[2,192,1536]{2,1,0:T(8,128)(2,1)S(1)}, u32[]{:S(2)}, u32[]{:S(2)}) %collective-permute-start.47) | collective-permute-done | bytes 1179680 | tf_op jit(solution)/shard_map/ppermute | solution.py:150
  530.3 5.5 %place_home.1 = (f32[192,4608]{1,0:T(8,128)}, f32[192,1536]{1,0:T(8,128)}) custom-call(s32[1]{0:T(128)} %bitcast.59.place_ref, bf16[192,1536]{1,0:T(8,128)(2,1)S(1)} %get-tuple-element.157.refs_0_, bf16[192,1536]{1,0:T(8,128)(2,1)S(1)} %get-tuple-element.185.refs_1_, bf16[192,1536]{1,0:T(8,128)(2,1)S(1)} %get-tuple-element.183.refs_2_, ...), custom_call_target="tpu_custom_call" | custom-call | flops 1179648 | bytes 7077888 | tf_op jit(solution)/shard_map/place_home/pallas_call | solution.py:516
  (403 shorter events, 205.7 us)
Async XLA Ops:
  11.4 57.6 %collective-permute-start.5 = (bf16[224,3072]{1,0:T(8,128)(2,1)}, bf16[224,3072]{1,0:T(8,128)(2,1)S(1)}, u32[]{:S(2)}, u32[]{:S(2)}) collective-permute-start(bf16[224,3072]{1,0:T(8,128)(2,1)} %get-tuple-element.151), channel_id=1, source_target_pairs={{0,4},{2,6},{4,0},{6,2},{8,12},{10,14},{12,8},{14,10},{16,20},{18,... | collective-permute-start | bytes 4128776 | tf_op jit(solution)/shard_map/ppermute | solution.py:150
  22.0 47.1 %collective-permute-start.4 = (bf16[448,3072]{1,0:T(8,128)(2,1)}, bf16[448,3072]{1,0:T(8,128)(2,1)S(1)}, u32[]{:S(2)}, u32[]{:S(2)}) collective-permute-start(bf16[448,3072]{1,0:T(8,128)(2,1)} %copy-done.4), channel_id=1, source_target_pairs={{0,2},{2,0},{4,6},{6,4},{8,10},{10,8},{12,14},{14,12},{16,18},{18,... | collective-permute-start | bytes 8257544 | tf_op jit(solution)/shard_map/ppermute | solution.py:150
  22.1 32.7 %collective-permute-start.1 = (bf16[2,112,1536]{2,1,0:T(8,128)(2,1)S(1)}, bf16[2,112,1536]{2,1,0:T(8,128)(2,1)S(1)}, u32[]{:S(2)}, u32[]{:S(2)}) collective-permute-start(bf16[2,112,1536]{2,1,0:T(8,128)(2,1)S(1)} %broadcast_select_fusion.18), channel_id=1, source_target_pairs={{0,16},{2,18},{4,20},{6,22},{8,24},{10,26},{12,28},{14,30},{16,0},... | collective-permute-start | bytes 2064392 | tf_op jit(solution)/shard_map/ppermute | solution.py:150
  22.5 32.2 %collective-permute-start.3 = (bf16[2,112,1536]{2,1,0:T(8,128)(2,1)S(1)}, bf16[2,112,1536]{2,1,0:T(8,128)(2,1)S(1)}, u32[]{:S(2)}, u32[]{:S(2)}) collective-permute-start(bf16[2,112,1536]{2,1,0:T(8,128)(2,1)S(1)} %bitcast.157), channel_id=1, source_target_pairs={{0,8},{2,10},{4,12},{6,14},{8,0},{10,2},{12,4},{14,6},{16,24},{18,... | collective-permute-start | bytes 2064392 | tf_op jit(solution)/shard_map/ppermute | solution.py:150
  25.6 43.4 %collective-permute-start.7 = (bf16[2,192,1536]{2,1,0:T(8,128)(2,1)S(1)}, bf16[2,192,1536]{2,1,0:T(8,128)(2,1)S(1)}, u32[]{:S(2)}, u32[]{:S(2)}) collective-permute-start(bf16[2,192,1536]{2,1,0:T(8,128)(2,1)S(1)} %pad_maximum_fusion.18), channel_id=1, source_target_pairs={{0,4},{2,6},{4,0},{6,2},{8,12},{10,14},{12,8},{14,10},{16,20},{18,... | collective-permute-start | bytes 3538952 | tf_op jit(solution)/shard_map/ppermute | solution.py:150
  55.0 54.4 %collective-permute-start.2 = (bf16[2,112,1536]{2,1,0:T(8,128)(2,1)S(1)}, bf16[2,112,1536]{2,1,0:T(8,128)(2,1)S(1)}, u32[]{:S(2)}, u32[]{:S(2)}) collective-permute-start(bf16[2,112,1536]{2,1,0:T(8,128)(2,1)S(1)} %broadcast_select_fusion.19), channel_id=1, source_target_pairs={{0,1},{1,0},{2,3},{3,2},{4,5},{5,4},{6,7},{7,6},{8,9},{9,8},{10,11... | collective-permute-start | bytes 2064392 | tf_op jit(solution)/shard_map/ppermute | solution.py:154
  56.6 30.2 %collective-permute-start.11 = (bf16[2,112,1536]{2,1,0:T(8,128)(2,1)S(1)}, bf16[2,112,1536]{2,1,0:T(8,128)(2,1)S(1)}, u32[]{:S(2)}, u32[]{:S(2)}) collective-permute-start(bf16[2,112,1536]{2,1,0:T(8,128)(2,1)S(1)} %broadcast_select_fusion.17), channel_id=1, source_target_pairs={{0,16},{2,18},{4,20},{6,22},{8,24},{10,26},{12,28},{14,30},{16,0},... | collective-permute-start | bytes 2064392 | tf_op jit(solution)/shard_map/ppermute | solution.py:150
  72.0 31.0 %collective-permute-start.12 = (bf16[768,512]{1,0:T(8,128)(2,1)S(1)}, bf16[768,512]{1,0:T(8,128)(2,1)S(1)}, u32[]{:S(2)}, u32[]{:S(2)}) collective-permute-start(bf16[768,512]{1,0:T(8,128)(2,1)S(1)} %pad_maximum_fusion.26), channel_id=1, source_target_pairs={{0,8},{2,10},{4,12},{6,14},{8,0},{10,2},{12,4},{14,6},{16,24},{18,... | collective-permute-start | bytes 2359304 | tf_op jit(solution)/shard_map/ppermute | solution.py:150
  87.9 33.7 %collective-permute-start.15 = (bf16[2,112,1536]{2,1,0:T(8,128)(2,1)}, bf16[2,112,1536]{2,1,0:T(8,128)(2,1)}, u32[]{:S(2)}, u32[]{:S(2)}) collective-permute-start(bf16[2,112,1536]{2,1,0:T(8,128)(2,1)} %broadcast_select_fusion.16), channel_id=1, source_target_pairs={{0,1},{1,0},{2,3},{3,2},{4,5},{5,4},{6,7},{7,6},{8,9},{9,8},{10,11... | collective-permute-start | bytes 2064392 | tf_op jit(solution)/shard_map/ppermute | solution.py:154
  89.9 28.9 %collective-permute-start.9 = (bf16[2,112,1536]{2,1,0:T(8,128)(2,1)}, bf16[2,112,1536]{2,1,0:T(8,128)(2,1)S(1)}, u32[]{:S(2)}, u32[]{:S(2)}) collective-permute-start(bf16[2,112,1536]{2,1,0:T(8,128)(2,1)} %collective-permute-done.8), channel_id=1, source_target_pairs={{0,1},{1,0},{2,3},{3,2},{4,5},{5,4},{6,7},{7,6},{8,9},{9,8},{10,11... | collective-permute-start | bytes 2064392 | tf_op jit(solution)/shard_map/ppermute | solution.py:154
  104.5 36.3 %collective-permute-start.14 = (bf16[2,768,512]{2,1,0:T(8,128)(2,1)}, bf16[2,768,512]{2,1,0:T(8,128)(2,1)}, u32[]{:S(2)}, u32[]{:S(2)}) collective-permute-start(bf16[2,768,512]{2,1,0:T(8,128)(2,1)} %pad_maximum_fusion.8), channel_id=1, source_target_pairs={{0,8},{2,10},{4,12},{6,14},{8,0},{10,2},{12,4},{14,6},{16,24},{18,... | collective-permute-start | bytes 4718600 | tf_op jit(solution)/shard_map/ppermute | solution.py:150
  110.3 37.2 %collective-permute-start.13 = (bf16[1536,512]{1,0:T(8,128)(2,1)}, bf16[1536,512]{1,0:T(8,128)(2,1)}, u32[]{:S(2)}, u32[]{:S(2)}) collective-permute-start(bf16[1536,512]{1,0:T(8,128)(2,1)} %pad_maximum_fusion.7), channel_id=1, source_target_pairs={{8,16},{10,18},{12,20},{14,22},{16,8},{18,10},{20,12},{22,14},{9,1... | collective-permute-start | bytes 4718600 | tf_op jit(solution)/shard_map/ppermute | solution.py:163
  122.2 36.4 %collective-permute-start.10 = (bf16[2,2,2,112,1536]{4,3,2,1,0:T(8,128)(2,1)S(1)}, bf16[2,2,2,112,1536]{4,3,2,1,0:T(8,128)(2,1)}, u32[]{:S(2)}, u32[]{:S(2)}) collective-permute-start(bf16[2,2,2,112,1536]{4,3,2,1,0:T(8,128)(2,1)S(1)} %bitcast.134), channel_id=1, source_target_pairs={{0,2},{2,0},{4,6},{6,4},{8,10},{10,8},{12,14},{14,12},{16,18},{18,... | collective-permute-start | bytes 8257544 | tf_op jit(solution)/shard_map/ppermute | solution.py:150
  152.3 38.2 %collective-permute-start.20 = (bf16[1536,512]{1,0:T(8,128)(2,1)}, bf16[1536,512]{1,0:T(8,128)(2,1)}, u32[]{:S(2)}, u32[]{:S(2)}) collective-permute-start(bf16[1536,512]{1,0:T(8,128)(2,1)} %pad_maximum_fusion.9), channel_id=1, source_target_pairs={{8,16},{10,18},{12,20},{14,22},{16,8},{18,10},{20,12},{22,14},{9,1... | collective-permute-start | bytes 4718600 | tf_op jit(solution)/shard_map/ppermute | solution.py:163
  154.6 40.4 %collective-permute-start.22 = (bf16[224,3072]{1,0:T(8,128)(2,1)}, bf16[224,3072]{1,0:T(8,128)(2,1)}, u32[]{:S(2)}, u32[]{:S(2)}) collective-permute-start(bf16[224,3072]{1,0:T(8,128)(2,1)} %get-tuple-element.85), channel_id=1, source_target_pairs={{0,4},{2,6},{4,0},{6,2},{8,12},{10,14},{12,8},{14,10},{16,20},{18,... | collective-permute-start | bytes 4128776 | tf_op jit(solution)/shard_map/ppermute | solution.py:150
  154.9 36.4 %collective-permute-start.19 = (bf16[1536,512]{1,0:T(8,128)(2,1)}, bf16[1536,512]{1,0:T(8,128)(2,1)}, u32[]{:S(2)}, u32[]{:S(2)}) collective-permute-start(bf16[1536,512]{1,0:T(8,128)(2,1)} %collective-permute-done.13), channel_id=1, source_target_pairs={{8,0},{10,2},{12,4},{14,6},{16,24},{18,26},{20,28},{22,30},{9,1},{... | collective-permute-start | bytes 4718600 | tf_op jit(solution)/shard_map/ppermute | solution.py:163
  199.2 43.3 %collective-permute-start.25 = (bf16[1536,512]{1,0:T(8,128)(2,1)}, bf16[1536,512]{1,0:T(8,128)(2,1)}, u32[]{:S(2)}, u32[]{:S(2)}) collective-permute-start(bf16[1536,512]{1,0:T(8,128)(2,1)} %pad_maximum_fusion.10), channel_id=1, source_target_pairs={{8,16},{10,18},{12,20},{14,22},{16,8},{18,10},{20,12},{22,14},{9,1... | collective-permute-start | bytes 4718600 | tf_op jit(solution)/shard_map/ppermute | solution.py:163
  201.5 40.9 %collective-permute-start.24 = (bf16[1536,512]{1,0:T(8,128)(2,1)}, bf16[1536,512]{1,0:T(8,128)(2,1)}, u32[]{:S(2)}, u32[]{:S(2)}) collective-permute-start(bf16[1536,512]{1,0:T(8,128)(2,1)} %collective-permute-done.20), channel_id=1, source_target_pairs={{8,0},{10,2},{12,4},{14,6},{16,24},{18,26},{20,28},{22,30},{9,1},{... | collective-permute-start | bytes 4718600 | tf_op jit(solution)/shard_map/ppermute | solution.py:163
  240.0 42.9 %collective-permute-start.27 = (bf16[512,1536]{1,0:T(8,128)(2,1)}, bf16[512,1536]{1,0:T(8,128)(2,1)}, u32[]{:S(2)}, u32[]{:S(2)}) collective-permute-start(bf16[512,1536]{1,0:T(8,128)(2,1)} %pad_maximum_fusion.11), channel_id=1, source_target_pairs={{0,8},{2,10},{4,12},{6,14},{24,16},{26,18},{28,20},{30,22},{1,9},{... | collective-permute-start | bytes 4718600 | tf_op jit(solution)/shard_map/ppermute | solution.py:163
  249.5 40.2 %collective-permute-start.26 = (bf16[1536,512]{1,0:T(8,128)(2,1)}, bf16[1536,512]{1,0:T(8,128)(2,1)}, u32[]{:S(2)}, u32[]{:S(2)}) collective-permute-start(bf16[1536,512]{1,0:T(8,128)(2,1)} %collective-permute-done.25), channel_id=1, source_target_pairs={{8,0},{10,2},{12,4},{14,6},{16,24},{18,26},{20,28},{22,30},{9,1},{... | collective-permute-start | bytes 4718600 | tf_op jit(solution)/shard_map/ppermute | solution.py:163
  281.6 37.7 %collective-permute-start.28 = (bf16[512,1536]{1,0:T(8,128)(2,1)}, bf16[512,1536]{1,0:T(8,128)(2,1)}, u32[]{:S(2)}, u32[]{:S(2)}) collective-permute-start(bf16[512,1536]{1,0:T(8,128)(2,1)} %pad_maximum_fusion.12), channel_id=1, source_target_pairs={{0,8},{2,10},{4,12},{6,14},{24,16},{26,18},{28,20},{30,22},{1,9},{... | collective-permute-start | bytes 4718600 | tf_op jit(solution)/shard_map/ppermute | solution.py:163
  285.8 37.7 %collective-permute-start.29 = (bf16[512,1536]{1,0:T(8,128)(2,1)}, bf16[512,1536]{1,0:T(8,128)(2,1)}, u32[]{:S(2)}, u32[]{:S(2)}) collective-permute-start(bf16[512,1536]{1,0:T(8,128)(2,1)} %add_convert_fusion.4), channel_id=1, source_target_pairs={{8,16},{10,18},{12,20},{14,22},{16,8},{18,10},{20,12},{22,14},{9,1... | collective-permute-start | bytes 4718600 | tf_op jit(solution)/shard_map/ppermute | solution.py:163
  328.4 26.5 %collective-permute-start.30 = (bf16[2,448,3072]{2,1,0:T(8,128)(2,1)}, bf16[2,448,3072]{2,1,0:T(8,128)(2,1)}, u32[]{:S(2)}, u32[]{:S(2)}) collective-permute-start(bf16[2,448,3072]{2,1,0:T(8,128)(2,1)} %bitcast.169), channel_id=1, source_target_pairs={{0,2},{2,0},{4,6},{6,4},{8,10},{10,8},{12,14},{14,12},{16,18},{18,... | collective-permute-start | bytes 16515080 | tf_op jit(solution)/shard_map/ppermute | solution.py:150
  343.3 38.9 %collective-permute-start.33 = (bf16[512,1536]{1,0:T(8,128)(2,1)}, bf16[512,1536]{1,0:T(8,128)(2,1)}, u32[]{:S(2)}, u32[]{:S(2)}) collective-permute-start(bf16[512,1536]{1,0:T(8,128)(2,1)} %add_convert_fusion.3), channel_id=1, source_target_pairs={{8,16},{10,18},{12,20},{14,22},{16,8},{18,10},{20,12},{22,14},{9,1... | collective-permute-start | bytes 4718600 | tf_op jit(solution)/shard_map/ppermute | solution.py:163
  353.6 38.5 %collective-permute-start.32 = (bf16[512,1536]{1,0:T(8,128)(2,1)S(1)}, bf16[512,1536]{1,0:T(8,128)(2,1)}, u32[]{:S(2)}, u32[]{:S(2)}) collective-permute-start(bf16[512,1536]{1,0:T(8,128)(2,1)S(1)} %pad_maximum_fusion.13), channel_id=1, source_target_pairs={{0,8},{2,10},{4,12},{6,14},{24,16},{26,18},{28,20},{30,22},{1,9},{... | collective-permute-start | bytes 4718600 | tf_op jit(solution)/shard_map/ppermute | solution.py:163
  357.9 41.2 %collective-permute-start.35 = (bf16[224,3072]{1,0:T(8,128)(2,1)}, bf16[224,3072]{1,0:T(8,128)(2,1)}, u32[]{:S(2)}, u32[]{:S(2)}) collective-permute-start(bf16[224,3072]{1,0:T(8,128)(2,1)} %fusion.6), channel_id=1, source_target_pairs={{0,4},{2,6},{4,0},{6,2},{8,12},{10,14},{12,8},{14,10},{16,20},{18,... | collective-permute-start | bytes 4128776 | tf_op jit(solution)/shard_map/ppermute | solution.py:150
  362.6 36.5 %collective-permute-start.31 = (bf16[2,224,1536]{2,1,0:T(8,128)(2,1)S(1)}, bf16[2,224,1536]{2,1,0:T(8,128)(2,1)S(1)}, u32[]{:S(2)}, u32[]{:S(2)}) collective-permute-start(bf16[2,224,1536]{2,1,0:T(8,128)(2,1)S(1)} %constant_dynamic-slice_fusion.19), channel_id=1, source_target_pairs={{0,1},{1,0},{2,3},{3,2},{4,5},{5,4},{6,7},{7,6},{8,9},{9,8},{10,11... | collective-permute-start | bytes 4128776 | tf_op jit(solution)/shard_map/ppermute | solution.py:154
  400.2 49.4 %collective-permute-start.38 = (bf16[2,448,3072]{2,1,0:T(8,128)(2,1)}, bf16[2,448,3072]{2,1,0:T(8,128)(2,1)S(1)}, u32[]{:S(2)}, u32[]{:S(2)}) collective-permute-start(bf16[2,448,3072]{2,1,0:T(8,128)(2,1)} %bitcast.38), channel_id=1, source_target_pairs={{0,2},{2,0},{4,6},{6,4},{8,10},{10,8},{12,14},{14,12},{16,18},{18,... | collective-permute-start | bytes 16515080 | tf_op jit(solution)/shard_map/ppermute | solution.py:150
  411.0 38.6 %collective-permute-start.37 = (bf16[512,1536]{1,0:T(8,128)(2,1)}, bf16[512,1536]{1,0:T(8,128)(2,1)}, u32[]{:S(2)}, u32[]{:S(2)}) collective-permute-start(bf16[512,1536]{1,0:T(8,128)(2,1)} %add_convert_fusion.2), channel_id=1, source_target_pairs={{8,16},{10,18},{12,20},{14,22},{16,8},{18,10},{20,12},{22,14},{9,1... | collective-permute-start | bytes 4718600 | tf_op jit(solution)/shard_map/ppermute | solution.py:163
  423.5 36.0 %collective-permute-start.44 = (bf16[1024,768]{1,0:T(8,128)(2,1)S(1)}, bf16[1024,768]{1,0:T(8,128)(2,1)S(1)}, u32[]{:S(2)}, u32[]{:S(2)}) collective-permute-start(bf16[1024,768]{1,0:T(8,128)(2,1)S(1)} %copy-done.49), channel_id=1, source_target_pairs={{0,8},{2,10},{4,12},{6,14},{8,0},{10,2},{12,4},{14,6},{16,24},{18,... | collective-permute-start | bytes 4718600 | tf_op jit(solution)/shard_map/ppermute | solution.py:150
  450.1 31.2 %collective-permute-start.41 = (bf16[224,3072]{1,0:T(8,128)(2,1)S(1)}, bf16[224,3072]{1,0:T(8,128)(2,1)S(1)}, u32[]{:S(2)}, u32[]{:S(2)}) collective-permute-start(bf16[224,3072]{1,0:T(8,128)(2,1)S(1)} %fusion.8), channel_id=1, source_target_pairs={{0,4},{2,6},{4,0},{6,2},{8,12},{10,14},{12,8},{14,10},{16,20},{18,... | collective-permute-start | bytes 4128776 | tf_op jit(solution)/shard_map/ppermute | solution.py:150
  451.7 32.1 %collective-permute-start.39 = (bf16[2,224,1536]{2,1,0:T(8,128)(2,1)S(1)}, bf16[2,224,1536]{2,1,0:T(8,128)(2,1)S(1)}, u32[]{:S(2)}, u32[]{:S(2)}) collective-permute-start(bf16[2,224,1536]{2,1,0:T(8,128)(2,1)S(1)} %constant_dynamic-slice_fusion.12), channel_id=1, source_target_pairs={{0,1},{1,0},{2,3},{3,2},{4,5},{5,4},{6,7},{7,6},{8,9},{9,8},{10,11... | collective-permute-start | bytes 4128776 | tf_op jit(solution)/shard_map/ppermute | solution.py:154
  (104 other events, 1123.6 us)

commit v4 on v3

--- a/solution.py
+++ b/solution.py
@@ -476,66 +476,52 @@
         )
 
 
-def home_kernel(counts, place_ref, *refs):
-    qkv_ref, out_ref = refs[-2:]
-    at, head = (pl.program_id(0), pl.program_id(1))
-    width = qkv_ref.shape[1]
-    first = 0
-    for group, count in enumerate(counts):
-        inside = (head >= first) & (head < first + count)
-        for step in range(PLANE):
-
-            @pl.when((at == step) & inside)
-            def _():
-                value = refs[group * PLANE + step][...].astype(jnp.float32)
-                qkv_ref[...] = value[:, :width]
-                out_ref[...] = value[:, width:]
-
-        first += count
-
-
-def place_home(groups, my_place, heads, head_dim):
-    rows = groups[0][0].shape[0]
-    head_width = 4 * head_dim
-    qkv_width = 3 * head_dim
-    counts = [blocks[0].shape[1] // head_width for blocks in groups]
-
-    def source(first, count):
-        return pl.BlockSpec(
-            (rows, head_width), lambda at, head, place: (0, jnp.clip(head - first, 0, count - 1))
-        )
-
-    specs = []
-    for group, count in enumerate(counts):
-        specs += [source(sum(counts[:group]), count)] * PLANE
-
-    def target(at, head, place):
-        return (0, (place[0] ^ at) * heads + head)
-
-    total = PLANE * heads
+def home_kernel(heads, place_ref, *refs):
+    block_refs, (qkv_ref, out_ref) = (refs[:PLANE], refs[-2:])
+    at = pl.program_id(0)
+    qkv_width = qkv_ref.shape[1] // heads
+    head_dim = out_ref.shape[1] // heads
+    head_width = qkv_width + head_dim
+    for step in range(PLANE):
+
+        @pl.when(at == step)
+        def _():
+            for head in range(heads):
+                low = head * head_width
+                value = block_refs[step][:, low : low + head_width].astype(jnp.float32)
+                qkv_ref[:, head * qkv_width : (head + 1) * qkv_width] = value[:, :qkv_width]
+                out_ref[:, head * head_dim : (head + 1) * head_dim] = value[:, qkv_width:]
+
+
+def place_home(blocks, my_place, heads, head_dim):
+    rows, width = blocks[0].shape
+
+    def target(at, place):
+        return (0, place[0] ^ at)
+
     return pl.pallas_call(
-        functools.partial(home_kernel, counts),
+        functools.partial(home_kernel, heads),
         grid_spec=pltpu.PrefetchScalarGridSpec(
             num_scalar_prefetch=1,
-            grid=(PLANE, heads),
-            in_specs=specs,
+            grid=(PLANE,),
+            in_specs=[pl.BlockSpec((rows, width), lambda at, place: (0, 0))] * PLANE,
             out_specs=[
-                pl.BlockSpec((rows, qkv_width), target),
-                pl.BlockSpec((rows, head_dim), target),
+                pl.BlockSpec((rows, heads * 3 * head_dim), target),
+                pl.BlockSpec((rows, heads * head_dim), target),
             ],
         ),
         out_shape=[
-            jax.ShapeDtypeStruct((rows, total * qkv_width), jnp.float32),
-            jax.ShapeDtypeStruct((rows, total * head_dim), jnp.float32),
+            jax.ShapeDtypeStruct((rows, PLANE * heads * 3 * head_dim), jnp.float32),
+            jax.ShapeDtypeStruct((rows, PLANE * heads * head_dim), jnp.float32),
         ],
         compiler_params=pltpu.CompilerParams(vmem_limit_bytes=32 * 1024 * 1024),
         cost_estimate=pl.CostEstimate(
-            flops=total * rows * head_width,
-            bytes_accessed=6 * total * rows * head_width,
+            flops=PLANE * rows * width,
+            bytes_accessed=6 * PLANE * rows * width,
             transcendentals=0,
         ),
         name="place_home",
-    )(my_place[None], *[block for blocks in groups for block in blocks])
+    )(my_place[None], *blocks)
 
 
 def per_plane(patches, cotangent, counts, masks, norm_gain, qk_gain, qkv_weight, out_weight):
@@ -742,20 +728,19 @@
     turned = out_scatter.turn(*between)
     reduces[2].cross(*turned)
     early.send(*turned)
-    held = after(back_all[2 * tok_rows :], *turned)
+    held = after(back_all[2 * tok_rows :], *turned, reduces[2].cross_sent)
     back_kept = mm(held, qkv_all, 1, 1).astype(jnp.bfloat16)
     back_added = back_scatter.add_cores(
         after(
             back_kept.reshape(2, tok_rows, model_width),
             out_scatter.last_x,
             out_scatter.last_y,
-            reduces[2].crossed,
         )
     )
     late = PairReduce(reduces[2:], my_plane, *back_added)
     late.send()
     turned = back_scatter.turn(late.sent)
-    total = jnp.concatenate([early.total(*back_added), late.total(*turned)])
+    total = jnp.concatenate([early.total(*turned), late.total(*turned)])
     home = send_home(after(total, *turned))
     attended = out_scatter.total()
     attended = jnp.where(is_live[:, None], attended, 0.0).astype(jnp.bfloat16)
@@ -782,7 +767,7 @@
     grad_rows = factor * (weighted - sums[0][:, None] - centred * sums[1][:, None])
     grad_rows = grad_rows.astype(jnp.bfloat16)
 
-    grad_qkv_weight, grad_out_weight = place_home([home], my_place, heads, head_dim)
+    grad_qkv_weight, grad_out_weight = place_home(home, my_place, heads, head_dim)
     return (attended, grad_rows, grad_qkv_weight, grad_out_weight)
 
 

time: 545 us -> 531 us (0.974)
  the two profiles are of different devices: /device:TPU:20 before, /device:TPU:0 now
where the time goes in v4:
time: 531 us; the launch traced here: 523 us
  waiting for transfers between devices  159 us (30%)
  starting transfers between devices  110 us (21%)
  matrix products  80 us (15%)
  other arithmetic  71.9 us (14%)
  Pallas kernels  47.7 us (9%)
  local copies, waits for them, and re-layouts  47.4 us (9%)
  between operations  7.32 us (1%)
    ppermute x27, waiting for transfers between devices, swap_fsdp(): return lax.ppermute(value, 'fsdp', pairs)  124 us
    dot_general x16, matrix products, mm(): lax.dot_general(left, right, (((left_dim,), (right_dim,)), ((), ())), pre...  80 us
    ppermute x27, starting transfers between devices, swap_fsdp(): return lax.ppermute(value, 'fsdp', pairs)  57.1 us
    ppermute x12, starting transfers between devices, send_planes(): return lax.ppermute(value, 'fsdp', pairs)  44 us
    pallas_call x3, Pallas kernels, attend(): pl.pallas_call(functools.partial(attention_kernel, per_step), grid_spec=p...  31.4 us
    ppermute x12, waiting for transfers between devices, send_planes(): return lax.ppermute(value, 'fsdp', pairs)  22.6 us
    convert_element_type x7, other arithmetic, add_rounded(): (left.astype(jnp.float32) + right.astype(jnp.float32)).astype(jnp.bfloat16)  16.9 us
    unnamed x176, local copies, waits for them, and re-layouts  15.4 us
  transfers between devices with their start and end apart: 48, of which 14 were waited for; matrix products, arithmetic and copies ran while one was open for 34% of the time, Pallas kernels for 9%

profile of v4, /device:TPU:0, one launch (start us, length us, event | category | flops | bytes accessed | tf_op | source)
XLA Modules:
  0.0 523.5 jit_solution(14425151508389997056)
XLA Ops:
  14.1 7.8 %collective-permute-done = bf16[2,112,1536]{2,1,0:T(8,128)(2,1)} collective-permute-done((bf16[2,112,1536]{2,1,0:T(8,128)(2,1)}, bf16[2,112,1536]{2,1,0:T(8,128)(2,1)}, u32[]{:S(2)}, u32[]{:S(2)}) %collective-permute-start) | collective-permute-done | bytes 688160 | tf_op jit(solution)/shard_map/ppermute | solution.py:150
  30.9 26.5 %collective-permute-done.3 = bf16[2,112,1536]{2,1,0:T(8,128)(2,1)S(1)} collective-permute-done((bf16[2,112,1536]{2,1,0:T(8,128)(2,1)S(1)}, bf16[2,112,1536]{2,1,0:T(8,128)(2,1)S(1)}, u32[]{:S(2)}, u32[]{:S(2)}) %collective-permute-start.3) | collective-permute-done | bytes 688160 | tf_op jit(solution)/shard_map/ppermute | solution.py:150
  60.6 9.2 %collective-permute-done.7 = bf16[2,192,1536]{2,1,0:T(8,128)(2,1)S(1)} collective-permute-done((bf16[2,192,1536]{2,1,0:T(8,128)(2,1)S(1)}, bf16[2,192,1536]{2,1,0:T(8,128)(2,1)S(1)}, u32[]{:S(2)}, u32[]{:S(2)}) %collective-permute-start.7) | collective-permute-done | bytes 1179680 | tf_op jit(solution)/shard_map/ppermute | solution.py:150
  74.3 17.1 %collective-permute-done.11 = bf16[2,112,1536]{2,1,0:T(8,128)(2,1)S(1)} collective-permute-done((bf16[2,112,1536]{2,1,0:T(8,128)(2,1)S(1)}, bf16[2,112,1536]{2,1,0:T(8,128)(2,1)S(1)}, u32[]{:S(2)}, u32[]{:S(2)}) %collective-permute-start.11) | collective-permute-done | bytes 688160 | tf_op jit(solution)/shard_map/ppermute | solution.py:150
  96.0 9.5 %collective-permute-done.12 = bf16[768,512]{1,0:T(8,128)(2,1)S(1)} collective-permute-done((bf16[768,512]{1,0:T(8,128)(2,1)S(1)}, bf16[768,512]{1,0:T(8,128)(2,1)S(1)}, u32[]{:S(2)}, u32[]{:S(2)}) %collective-permute-start.12) | collective-permute-done | bytes 786464 | tf_op jit(solution)/shard_map/ppermute | solution.py:150
  112.0 11.4 %collective-permute-done.9 = bf16[2,112,1536]{2,1,0:T(8,128)(2,1)S(1)} collective-permute-done((bf16[2,112,1536]{2,1,0:T(8,128)(2,1)}, bf16[2,112,1536]{2,1,0:T(8,128)(2,1)S(1)}, u32[]{:S(2)}, u32[]{:S(2)}) %collective-permute-start.9) | collective-permute-done | bytes 688160 | tf_op jit(solution)/shard_map/ppermute | solution.py:154
  132.8 7.5 %collective-permute-done.14 = bf16[2,768,512]{2,1,0:T(8,128)(2,1)} collective-permute-done((bf16[2,768,512]{2,1,0:T(8,128)(2,1)}, bf16[2,768,512]{2,1,0:T(8,128)(2,1)}, u32[]{:S(2)}, u32[]{:S(2)}) %collective-permute-start.14) | collective-permute-done | bytes 1572896 | tf_op jit(solution)/shard_map/ppermute | solution.py:150
  155.3 13.7 %norm_rows.1 = (bf16[1792,3072]{1,0:T(8,128)(2,1)S(1)}, f32[1792,128]{1,0:T(8,128)S(1)}) custom-call(s32[17]{0:T(128)S(1)} %pad_add_fusion.pick_ref, s32[16]{0:T(128)S(1)} %reshape.170.count_ref, bf16[2,2,2,112,1536]{4,3,2,1,0:T(8,128)(2,1)S(1)} %bitcast.136, bf16[2,2,2,112,1536]{4,3,2,1,0:T(8,128)(2,1)S(1)} %bitcast.137, ...), custom_call_target="tpu_custom_call" | custom-call | flops 55050240 | bytes 33030144 | tf_op jit(solution)/shard_map/norm_rows/pallas_call | solution.py:318
  169.1 13.0 %collective-permute-done.22 = bf16[224,3072]{1,0:T(8,128)(2,1)} collective-permute-done((bf16[224,3072]{1,0:T(8,128)(2,1)}, bf16[224,3072]{1,0:T(8,128)(2,1)}, u32[]{:S(2)}, u32[]{:S(2)}) %collective-permute-start.22) | collective-permute-done | bytes 1376288 | tf_op jit(solution)/shard_map/ppermute | solution.py:150
  182.1 6.2 %collective-permute-done.19 = bf16[1536,512]{1,0:T(8,128)(2,1)} collective-permute-done((bf16[1536,512]{1,0:T(8,128)(2,1)}, bf16[1536,512]{1,0:T(8,128)(2,1)}, u32[]{:S(2)}, u32[]{:S(2)}) %collective-permute-start.19) | collective-permute-done | bytes 1572896 | tf_op jit(solution)/shard_map/ppermute | solution.py:163
  197.5 7.6 %fusion.34.proj_ref = f32[1792,384]{1,0:T(8,128)S(1)} fusion(bf16[1792,3072]{1,0:T(8,128)(2,1)S(1)} %get-tuple-element.81, bf16[3072,384]{1,0:T(8,128)(2,1)} %fusion.4), kind=kOutput, calls=%fused_computation.213 | convolution fusion | flops 4227858432 | bytes 16121856 | tf_op jit(solution)/shard_map/dot_general | solution.py:341
  217.3 10.6 %attend_images.3 = (bf16[1792,128]{1,0:T(8,128)(2,1)S(1)}, bf16[1792,384]{1,0:T(8,128)(2,1)S(1)}) custom-call(s32[16]{0:T(128)S(1)} %reshape.169.count_ref, f32[1792,384]{1,0:T(8,128)S(1)} %fusion.34.proj_ref, bf16[1792,128]{1,0:T(8,128)(2,1)S(1)} %convolution_convert_fusion.12.grad_ref, f32[2,128]{1,0:T(2,128)S(1)} %pad_maximum_fusion.31.scale_ref), custom_call_target="tpu_custom_call" | custom-call | flops 308281344 | bytes 5505024 | tf_op jit(solution)/shard_map/attend_images/pallas_call | solution.py:403
  229.6 4.7 convolution_convert_fusion.6
  235.8 12.5 %collective-permute-start.27 = (bf16[512,1536]{1,0:T(8,128)(2,1)}, bf16[512,1536]{1,0:T(8,128)(2,1)}, u32[]{:S(2)}, u32[]{:S(2)}) collective-permute-start(bf16[512,1536]{1,0:T(8,128)(2,1)} %pad_maximum_fusion.11), channel_id=1, source_target_pairs={{0,8},{2,10},{4,12},{6,14},{24,16},{26,18},{28,20},{30,22},{1,9},{... | collective-permute-start | bytes 4718600 | tf_op jit(solution)/shard_map/ppermute | solution.py:163
  258.1 6.1 %fusion.35.proj_ref = f32[1792,384]{1,0:T(8,128)S(1)} fusion(bf16[1792,3072]{1,0:T(8,128)(2,1)S(1)} %get-tuple-element.81, bf16[3072,384]{1,0:T(8,128)(2,1)S(1)} %copy-done.35), kind=kOutput, calls=%fused_computation.214 | convolution fusion | flops 4227858432 | bytes 16121856 | tf_op jit(solution)/shard_map/dot_general | solution.py:341
  264.2 10.2 %attend_images.4 = (bf16[1792,128]{1,0:T(8,128)(2,1)S(1)}, bf16[1792,384]{1,0:T(8,128)(2,1)S(1)}) custom-call(s32[16]{0:T(128)S(1)} %reshape.169.count_ref, f32[1792,384]{1,0:T(8,128)S(1)} %fusion.35.proj_ref, bf16[1792,128]{1,0:T(8,128)(2,1)S(1)} %convolution_convert_fusion.11.grad_ref, f32[2,128]{1,0:T(2,128)S(1)} %pad_maximum_fusion.31.scale_ref), custom_call_target="tpu_custom_call" | custom-call | flops 308281344 | bytes 5505024 | tf_op jit(solution)/shard_map/attend_images/pallas_call | solution.py:403
  274.4 5.8 %convolution_convert_fusion.5 = bf16[384,3072]{1,0:T(8,128)(2,1)} fusion(bf16[1792,384]{1,0:T(8,128)(2,1)S(1)} %get-tuple-element.95, bf16[1792,3072]{1,0:T(8,128)(2,1)S(1)} %get-tuple-element.81), kind=kOutput, calls=%fused_computation.8 | convolution fusion | flops 4229038080 | bytes 14745600 | tf_op jit(solution)/shard_map/dot_general | solution.py:341
  283.2 7.0 %collective-permute-start.28 = (bf16[512,1536]{1,0:T(8,128)(2,1)}, bf16[512,1536]{1,0:T(8,128)(2,1)}, u32[]{:S(2)}, u32[]{:S(2)}) collective-permute-start(bf16[512,1536]{1,0:T(8,128)(2,1)} %pad_maximum_fusion.12), channel_id=1, source_target_pairs={{0,8},{2,10},{4,12},{6,14},{24,16},{26,18},{28,20},{30,22},{1,9},{... | collective-permute-start | bytes 4718600 | tf_op jit(solution)/shard_map/ppermute | solution.py:163
  301.5 5.9 %fusion.36.proj_ref = f32[1792,384]{1,0:T(8,128)S(1)} fusion(bf16[1792,3072]{1,0:T(8,128)(2,1)S(1)} %get-tuple-element.81, bf16[3072,384]{1,0:T(8,128)(2,1)S(1)} %fusion.2), kind=kOutput, calls=%fused_computation.215 | convolution fusion | flops 4227858432 | bytes 16121856 | tf_op jit(solution)/shard_map/dot_general | solution.py:341
  307.4 10.6 %attend_images.5 = (bf16[1792,128]{1,0:T(8,128)(2,1)S(1)}, bf16[1792,384]{1,0:T(8,128)(2,1)S(1)}) custom-call(s32[16]{0:T(128)S(1)} %reshape.169.count_ref, f32[1792,384]{1,0:T(8,128)S(1)} %fusion.36.proj_ref, bf16[1792,128]{1,0:T(8,128)(2,1)S(1)} %convolution_convert_fusion.10.grad_ref, f32[2,128]{1,0:T(2,128)S(1)} %pad_maximum_fusion.31.scale_ref), custom_call_target="tpu_custom_call" | custom-call | flops 308281344 | bytes 5505024 | tf_op jit(solution)/shard_map/attend_images/pallas_call | solution.py:403
  318.2 4.1 collective-permute-done.28
  322.4 4.9 convolution_convert_fusion.3
  337.3 4.9 convolution_convert_fusion.2
  345.7 4.7 convolution_convert_fusion.4
  350.6 10.1 %collective-permute-start.32 = (bf16[512,1536]{1,0:T(8,128)(2,1)S(1)}, bf16[512,1536]{1,0:T(8,128)(2,1)}, u32[]{:S(2)}, u32[]{:S(2)}) collective-permute-start(bf16[512,1536]{1,0:T(8,128)(2,1)S(1)} %pad_maximum_fusion.13), channel_id=1, source_target_pairs={{0,8},{2,10},{4,12},{6,14},{24,16},{26,18},{28,20},{30,22},{1,9},{... | collective-permute-start | bytes 4718600 | tf_op jit(solution)/shard_map/ppermute | solution.py:163
  370.4 10.8 %convolution_convert_fusion.1 = bf16[896,3072]{1,0:T(8,128)(2,1)} fusion(bf16[896,1152]{1,0:T(8,128)(2,1)} %get-tuple-element.107, bf16[3072,384]{1,0:T(8,128)(2,1)S(1)} %copy-done.38, bf16[3072,384]{1,0:T(8,128)(2,1)S(1)} %copy-done.36, bf16[3072,384]{1,0:T(8,128)(2,1)S(1)} %copy-done.34), kind=kOutput, calls=%fused_computation.4 | convolution fusion | flops 6365773824 | bytes 14647296 | tf_op jit(solution)/shard_map/dot_general | solution.py:341
  381.3 12.3 %collective-permute-done.32 = bf16[512,1536]{1,0:T(8,128)(2,1)} collective-permute-done((bf16[512,1536]{1,0:T(8,128)(2,1)S(1)}, bf16[512,1536]{1,0:T(8,128)(2,1)}, u32[]{:S(2)}, u32[]{:S(2)}) %collective-permute-start.32) | collective-permute-done | bytes 1572896 | tf_op jit(solution)/shard_map/ppermute | solution.py:163
  411.1 10.3 %convolution_convert_fusion = bf16[896,3072]{1,0:T(8,128)(2,1)S(1)} fusion(bf16[896,1152]{1,0:T(8,128)(2,1)} %get-tuple-element.114, bf16[3072,384]{1,0:T(8,128)(2,1)} %copy-done.37, bf16[3072,384]{1,0:T(8,128)(2,1)} %fusion.3, bf16[3072,384]{1,0:T(8,128)(2,1)} %fusion.4), kind=kOutput, calls=%fused_computation.3 | convolution fusion | flops 6365773824 | bytes 14647296 | tf_op jit(solution)/shard_map/dot_general | solution.py:341
  422.2 5.5 %collective-permute-start.44 = (bf16[1024,768]{1,0:T(8,128)(2,1)S(1)}, bf16[1024,768]{1,0:T(8,128)(2,1)S(1)}, u32[]{:S(2)}, u32[]{:S(2)}) collective-permute-start(bf16[1024,768]{1,0:T(8,128)(2,1)S(1)} %copy-done.48), channel_id=1, source_target_pairs={{0,8},{2,10},{4,12},{6,14},{8,0},{10,2},{12,4},{14,6},{16,24},{18,... | collective-permute-start | bytes 4718600 | tf_op jit(solution)/shard_map/ppermute | solution.py:150
  433.1 29.5 %collective-permute-start.45 = (bf16[512,768]{1,0:T(8,128)(2,1)S(1)}, bf16[512,768]{1,0:T(8,128)(2,1)S(1)}, u32[]{:S(2)}, u32[]{:S(2)}) collective-permute-start(bf16[512,768]{1,0:T(8,128)(2,1)S(1)} %add_convert_fusion.10), channel_id=1, source_target_pairs={{0,8},{2,10},{4,12},{6,14},{8,0},{10,2},{12,4},{14,6},{16,24},{18,... | collective-permute-start | bytes 2359304 | tf_op jit(solution)/shard_map/ppermute | solution.py:150
  467.1 12.3 %collective-permute-done.45 = bf16[512,768]{1,0:T(8,128)(2,1)S(1)} collective-permute-done((bf16[512,768]{1,0:T(8,128)(2,1)S(1)}, bf16[512,768]{1,0:T(8,128)(2,1)S(1)}, u32[]{:S(2)}, u32[]{:S(2)}) %collective-permute-start.45) | collective-permute-done | bytes 786464 | tf_op jit(solution)/shard_map/ppermute | solution.py:150
  499.8 20.8 %collective-permute-done.47 = bf16[2,192,1536]{2,1,0:T(8,128)(2,1)S(1)} collective-permute-done((bf16[2,192,1536]{2,1,0:T(8,128)(2,1)S(1)}, bf16[2,192,1536]{2,1,0:T(8,128)(2,1)S(1)}, u32[]{:S(2)}, u32[]{:S(2)}) %collective-permute-start.47) | collective-permute-done | bytes 1179680 | tf_op jit(solution)/shard_map/ppermute | solution.py:150
  (399 shorter events, 183.0 us)
Async XLA Ops:
  12.5 57.4 %collective-permute-start.5 = (bf16[224,3072]{1,0:T(8,128)(2,1)S(1)}, bf16[224,3072]{1,0:T(8,128)(2,1)}, u32[]{:S(2)}, u32[]{:S(2)}) collective-permute-start(bf16[224,3072]{1,0:T(8,128)(2,1)S(1)} %get-tuple-element.151), channel_id=1, source_target_pairs={{0,4},{2,6},{4,0},{6,2},{8,12},{10,14},{12,8},{14,10},{16,20},{18,... | collective-permute-start | bytes 4128776 | tf_op jit(solution)/shard_map/ppermute | solution.py:150
  23.3 46.6 %collective-permute-start.4 = (bf16[448,3072]{1,0:T(8,128)(2,1)}, bf16[448,3072]{1,0:T(8,128)(2,1)S(1)}, u32[]{:S(2)}, u32[]{:S(2)}) collective-permute-start(bf16[448,3072]{1,0:T(8,128)(2,1)} %copy-done.4), channel_id=1, source_target_pairs={{0,2},{2,0},{4,6},{6,4},{8,10},{10,8},{12,14},{14,12},{16,18},{18,... | collective-permute-start | bytes 8257544 | tf_op jit(solution)/shard_map/ppermute | solution.py:150
  23.4 34.1 %collective-permute-start.1 = (bf16[2,112,1536]{2,1,0:T(8,128)(2,1)S(1)}, bf16[2,112,1536]{2,1,0:T(8,128)(2,1)S(1)}, u32[]{:S(2)}, u32[]{:S(2)}) collective-permute-start(bf16[2,112,1536]{2,1,0:T(8,128)(2,1)S(1)} %broadcast_select_fusion.18), channel_id=1, source_target_pairs={{0,16},{2,18},{4,20},{6,22},{8,24},{10,26},{12,28},{14,30},{16,0},... | collective-permute-start | bytes 2064392 | tf_op jit(solution)/shard_map/ppermute | solution.py:150
  26.3 31.1 %collective-permute-start.3 = (bf16[2,112,1536]{2,1,0:T(8,128)(2,1)S(1)}, bf16[2,112,1536]{2,1,0:T(8,128)(2,1)S(1)}, u32[]{:S(2)}, u32[]{:S(2)}) collective-permute-start(bf16[2,112,1536]{2,1,0:T(8,128)(2,1)S(1)} %bitcast.157), channel_id=1, source_target_pairs={{0,8},{2,10},{4,12},{6,14},{8,0},{10,2},{12,4},{14,6},{16,24},{18,... | collective-permute-start | bytes 2064392 | tf_op jit(solution)/shard_map/ppermute | solution.py:150
  29.3 40.5 %collective-permute-start.7 = (bf16[2,192,1536]{2,1,0:T(8,128)(2,1)S(1)}, bf16[2,192,1536]{2,1,0:T(8,128)(2,1)S(1)}, u32[]{:S(2)}, u32[]{:S(2)}) collective-permute-start(bf16[2,192,1536]{2,1,0:T(8,128)(2,1)S(1)} %pad_maximum_fusion.18), channel_id=1, source_target_pairs={{0,4},{2,6},{4,0},{6,2},{8,12},{10,14},{12,8},{14,10},{16,20},{18,... | collective-permute-start | bytes 3538952 | tf_op jit(solution)/shard_map/ppermute | solution.py:150
  57.7 50.8 %collective-permute-start.2 = (bf16[2,112,1536]{2,1,0:T(8,128)(2,1)S(1)}, bf16[2,112,1536]{2,1,0:T(8,128)(2,1)S(1)}, u32[]{:S(2)}, u32[]{:S(2)}) collective-permute-start(bf16[2,112,1536]{2,1,0:T(8,128)(2,1)S(1)} %broadcast_select_fusion.19), channel_id=1, source_target_pairs={{0,1},{1,0},{2,3},{3,2},{4,5},{5,4},{6,7},{7,6},{8,9},{9,8},{10,11... | collective-permute-start | bytes 2064392 | tf_op jit(solution)/shard_map/ppermute | solution.py:154
  59.3 32.1 %collective-permute-start.11 = (bf16[2,112,1536]{2,1,0:T(8,128)(2,1)S(1)}, bf16[2,112,1536]{2,1,0:T(8,128)(2,1)S(1)}, u32[]{:S(2)}, u32[]{:S(2)}) collective-permute-start(bf16[2,112,1536]{2,1,0:T(8,128)(2,1)S(1)} %broadcast_select_fusion.17), channel_id=1, source_target_pairs={{0,16},{2,18},{4,20},{6,22},{8,24},{10,26},{12,28},{14,30},{16,0},... | collective-permute-start | bytes 2064392 | tf_op jit(solution)/shard_map/ppermute | solution.py:150
  73.8 31.7 %collective-permute-start.12 = (bf16[768,512]{1,0:T(8,128)(2,1)S(1)}, bf16[768,512]{1,0:T(8,128)(2,1)S(1)}, u32[]{:S(2)}, u32[]{:S(2)}) collective-permute-start(bf16[768,512]{1,0:T(8,128)(2,1)S(1)} %pad_maximum_fusion.26), channel_id=1, source_target_pairs={{0,8},{2,10},{4,12},{6,14},{8,0},{10,2},{12,4},{14,6},{16,24},{18,... | collective-permute-start | bytes 2359304 | tf_op jit(solution)/shard_map/ppermute | solution.py:150
  92.4 33.7 %collective-permute-start.15 = (bf16[2,112,1536]{2,1,0:T(8,128)(2,1)}, bf16[2,112,1536]{2,1,0:T(8,128)(2,1)}, u32[]{:S(2)}, u32[]{:S(2)}) collective-permute-start(bf16[2,112,1536]{2,1,0:T(8,128)(2,1)} %broadcast_select_fusion.16), channel_id=1, source_target_pairs={{0,1},{1,0},{2,3},{3,2},{4,5},{5,4},{6,7},{7,6},{8,9},{9,8},{10,11... | collective-permute-start | bytes 2064392 | tf_op jit(solution)/shard_map/ppermute | solution.py:154
  94.6 28.8 %collective-permute-start.9 = (bf16[2,112,1536]{2,1,0:T(8,128)(2,1)}, bf16[2,112,1536]{2,1,0:T(8,128)(2,1)S(1)}, u32[]{:S(2)}, u32[]{:S(2)}) collective-permute-start(bf16[2,112,1536]{2,1,0:T(8,128)(2,1)} %collective-permute-done.8), channel_id=1, source_target_pairs={{0,1},{1,0},{2,3},{3,2},{4,5},{5,4},{6,7},{7,6},{8,9},{9,8},{10,11... | collective-permute-start | bytes 2064392 | tf_op jit(solution)/shard_map/ppermute | solution.py:154
  106.0 34.4 %collective-permute-start.14 = (bf16[2,768,512]{2,1,0:T(8,128)(2,1)}, bf16[2,768,512]{2,1,0:T(8,128)(2,1)}, u32[]{:S(2)}, u32[]{:S(2)}) collective-permute-start(bf16[2,768,512]{2,1,0:T(8,128)(2,1)} %pad_maximum_fusion.8), channel_id=1, source_target_pairs={{0,8},{2,10},{4,12},{6,14},{8,0},{10,2},{12,4},{14,6},{16,24},{18,... | collective-permute-start | bytes 4718600 | tf_op jit(solution)/shard_map/ppermute | solution.py:150
  109.3 32.5 %collective-permute-start.13 = (bf16[1536,512]{1,0:T(8,128)(2,1)}, bf16[1536,512]{1,0:T(8,128)(2,1)}, u32[]{:S(2)}, u32[]{:S(2)}) collective-permute-start(bf16[1536,512]{1,0:T(8,128)(2,1)} %pad_maximum_fusion.7), channel_id=1, source_target_pairs={{8,16},{10,18},{12,20},{14,22},{16,8},{18,10},{20,12},{22,14},{9,1... | collective-permute-start | bytes 4718600 | tf_op jit(solution)/shard_map/ppermute | solution.py:163
  126.9 25.4 %collective-permute-start.10 = (bf16[2,2,2,112,1536]{4,3,2,1,0:T(8,128)(2,1)S(1)}, bf16[2,2,2,112,1536]{4,3,2,1,0:T(8,128)(2,1)}, u32[]{:S(2)}, u32[]{:S(2)}) collective-permute-start(bf16[2,2,2,112,1536]{4,3,2,1,0:T(8,128)(2,1)S(1)} %bitcast.134), channel_id=1, source_target_pairs={{0,2},{2,0},{4,6},{6,4},{8,10},{10,8},{12,14},{14,12},{16,18},{18,... | collective-permute-start | bytes 8257544 | tf_op jit(solution)/shard_map/ppermute | solution.py:150
  144.6 43.6 %collective-permute-start.19 = (bf16[1536,512]{1,0:T(8,128)(2,1)}, bf16[1536,512]{1,0:T(8,128)(2,1)}, u32[]{:S(2)}, u32[]{:S(2)}) collective-permute-start(bf16[1536,512]{1,0:T(8,128)(2,1)} %collective-permute-done.13), channel_id=1, source_target_pairs={{8,0},{10,2},{12,4},{14,6},{16,24},{18,26},{20,28},{22,30},{9,1},{... | collective-permute-start | bytes 4718600 | tf_op jit(solution)/shard_map/ppermute | solution.py:163
  149.6 32.5 %collective-permute-start.22 = (bf16[224,3072]{1,0:T(8,128)(2,1)}, bf16[224,3072]{1,0:T(8,128)(2,1)}, u32[]{:S(2)}, u32[]{:S(2)}) collective-permute-start(bf16[224,3072]{1,0:T(8,128)(2,1)} %get-tuple-element.85), channel_id=1, source_target_pairs={{0,4},{2,6},{4,0},{6,2},{8,12},{10,14},{12,8},{14,10},{16,20},{18,... | collective-permute-start | bytes 4128776 | tf_op jit(solution)/shard_map/ppermute | solution.py:150
  190.4 59.1 %collective-permute-start.25 = (bf16[1536,512]{1,0:T(8,128)(2,1)}, bf16[1536,512]{1,0:T(8,128)(2,1)}, u32[]{:S(2)}, u32[]{:S(2)}) collective-permute-start(bf16[1536,512]{1,0:T(8,128)(2,1)} %pad_maximum_fusion.10), channel_id=1, source_target_pairs={{8,16},{10,18},{12,20},{14,22},{16,8},{18,10},{20,12},{22,14},{9,1... | collective-permute-start | bytes 4718600 | tf_op jit(solution)/shard_map/ppermute | solution.py:163
  192.3 57.2 %collective-permute-start.24 = (bf16[1536,512]{1,0:T(8,128)(2,1)}, bf16[1536,512]{1,0:T(8,128)(2,1)}, u32[]{:S(2)}, u32[]{:S(2)}) collective-permute-start(bf16[1536,512]{1,0:T(8,128)(2,1)} %collective-permute-done.20), channel_id=1, source_target_pairs={{8,0},{10,2},{12,4},{14,6},{16,24},{18,26},{20,28},{22,30},{9,1},{... | collective-permute-start | bytes 4718600 | tf_op jit(solution)/shard_map/ppermute | solution.py:163
  235.8 54.4 %collective-permute-start.27 = (bf16[512,1536]{1,0:T(8,128)(2,1)}, bf16[512,1536]{1,0:T(8,128)(2,1)}, u32[]{:S(2)}, u32[]{:S(2)}) collective-permute-start(bf16[512,1536]{1,0:T(8,128)(2,1)} %pad_maximum_fusion.11), channel_id=1, source_target_pairs={{0,8},{2,10},{4,12},{6,14},{24,16},{26,18},{28,20},{30,22},{1,9},{... | collective-permute-start | bytes 4718600 | tf_op jit(solution)/shard_map/ppermute | solution.py:163
  256.6 38.6 %collective-permute-start.26 = (bf16[1536,512]{1,0:T(8,128)(2,1)}, bf16[1536,512]{1,0:T(8,128)(2,1)}, u32[]{:S(2)}, u32[]{:S(2)}) collective-permute-start(bf16[1536,512]{1,0:T(8,128)(2,1)} %collective-permute-done.25), channel_id=1, source_target_pairs={{8,0},{10,2},{12,4},{14,6},{16,24},{18,26},{20,28},{22,30},{9,1},{... | collective-permute-start | bytes 4718600 | tf_op jit(solution)/shard_map/ppermute | solution.py:163
  283.2 39.1 %collective-permute-start.28 = (bf16[512,1536]{1,0:T(8,128)(2,1)}, bf16[512,1536]{1,0:T(8,128)(2,1)}, u32[]{:S(2)}, u32[]{:S(2)}) collective-permute-start(bf16[512,1536]{1,0:T(8,128)(2,1)} %pad_maximum_fusion.12), channel_id=1, source_target_pairs={{0,8},{2,10},{4,12},{6,14},{24,16},{26,18},{28,20},{30,22},{1,9},{... | collective-permute-start | bytes 4718600 | tf_op jit(solution)/shard_map/ppermute | solution.py:163
  293.1 29.2 %collective-permute-start.29 = (bf16[512,1536]{1,0:T(8,128)(2,1)}, bf16[512,1536]{1,0:T(8,128)(2,1)}, u32[]{:S(2)}, u32[]{:S(2)}) collective-permute-start(bf16[512,1536]{1,0:T(8,128)(2,1)} %add_convert_fusion.4), channel_id=1, source_target_pairs={{8,16},{10,18},{12,20},{14,22},{16,8},{18,10},{20,12},{22,14},{9,1... | collective-permute-start | bytes 4718600 | tf_op jit(solution)/shard_map/ppermute | solution.py:163
  327.3 33.5 %collective-permute-start.30 = (bf16[2,448,3072]{2,1,0:T(8,128)(2,1)}, bf16[2,448,3072]{2,1,0:T(8,128)(2,1)}, u32[]{:S(2)}, u32[]{:S(2)}) collective-permute-start(bf16[2,448,3072]{2,1,0:T(8,128)(2,1)} %bitcast.169), channel_id=1, source_target_pairs={{0,2},{2,0},{4,6},{6,4},{8,10},{10,8},{12,14},{14,12},{16,18},{18,... | collective-permute-start | bytes 16515080 | tf_op jit(solution)/shard_map/ppermute | solution.py:150
  342.2 39.1 %collective-permute-start.33 = (bf16[512,1536]{1,0:T(8,128)(2,1)}, bf16[512,1536]{1,0:T(8,128)(2,1)}, u32[]{:S(2)}, u32[]{:S(2)}) collective-permute-start(bf16[512,1536]{1,0:T(8,128)(2,1)} %add_convert_fusion.3), channel_id=1, source_target_pairs={{8,16},{10,18},{12,20},{14,22},{16,8},{18,10},{20,12},{22,14},{9,1... | collective-permute-start | bytes 4718600 | tf_op jit(solution)/shard_map/ppermute | solution.py:163
  350.6 43.0 %collective-permute-start.32 = (bf16[512,1536]{1,0:T(8,128)(2,1)S(1)}, bf16[512,1536]{1,0:T(8,128)(2,1)}, u32[]{:S(2)}, u32[]{:S(2)}) collective-permute-start(bf16[512,1536]{1,0:T(8,128)(2,1)S(1)} %pad_maximum_fusion.13), channel_id=1, source_target_pairs={{0,8},{2,10},{4,12},{6,14},{24,16},{26,18},{28,20},{30,22},{1,9},{... | collective-permute-start | bytes 4718600 | tf_op jit(solution)/shard_map/ppermute | solution.py:163
  363.7 37.1 %collective-permute-start.35 = (bf16[224,3072]{1,0:T(8,128)(2,1)}, bf16[224,3072]{1,0:T(8,128)(2,1)}, u32[]{:S(2)}, u32[]{:S(2)}) collective-permute-start(bf16[224,3072]{1,0:T(8,128)(2,1)} %fusion.6), channel_id=1, source_target_pairs={{0,4},{2,6},{4,0},{6,2},{8,12},{10,14},{12,8},{14,10},{16,20},{18,... | collective-permute-start | bytes 4128776 | tf_op jit(solution)/shard_map/ppermute | solution.py:150
  368.5 32.4 %collective-permute-start.31 = (bf16[2,224,1536]{2,1,0:T(8,128)(2,1)S(1)}, bf16[2,224,1536]{2,1,0:T(8,128)(2,1)S(1)}, u32[]{:S(2)}, u32[]{:S(2)}) collective-permute-start(bf16[2,224,1536]{2,1,0:T(8,128)(2,1)S(1)} %constant_dynamic-slice_fusion.19), channel_id=1, source_target_pairs={{0,1},{1,0},{2,3},{3,2},{4,5},{5,4},{6,7},{7,6},{8,9},{9,8},{10,11... | collective-permute-start | bytes 4128776 | tf_op jit(solution)/shard_map/ppermute | solution.py:154
  401.9 26.8 %collective-permute-start.37 = (bf16[2,448,3072]{2,1,0:T(8,128)(2,1)}, bf16[2,448,3072]{2,1,0:T(8,128)(2,1)S(1)}, u32[]{:S(2)}, u32[]{:S(2)}) collective-permute-start(bf16[2,448,3072]{2,1,0:T(8,128)(2,1)} %bitcast.38), channel_id=1, source_target_pairs={{0,2},{2,0},{4,6},{6,4},{8,10},{10,8},{12,14},{14,12},{16,18},{18,... | collective-permute-start | bytes 16515080 | tf_op jit(solution)/shard_map/ppermute | solution.py:150
  422.2 57.2 %collective-permute-start.44 = (bf16[1024,768]{1,0:T(8,128)(2,1)S(1)}, bf16[1024,768]{1,0:T(8,128)(2,1)S(1)}, u32[]{:S(2)}, u32[]{:S(2)}) collective-permute-start(bf16[1024,768]{1,0:T(8,128)(2,1)S(1)} %copy-done.48), channel_id=1, source_target_pairs={{0,8},{2,10},{4,12},{6,14},{8,0},{10,2},{12,4},{14,6},{16,24},{18,... | collective-permute-start | bytes 4718600 | tf_op jit(solution)/shard_map/ppermute | solution.py:150
  429.2 33.4 %collective-permute-start.41 = (bf16[224,3072]{1,0:T(8,128)(2,1)S(1)}, bf16[224,3072]{1,0:T(8,128)(2,1)S(1)}, u32[]{:S(2)}, u32[]{:S(2)}) collective-permute-start(bf16[224,3072]{1,0:T(8,128)(2,1)S(1)} %fusion.8), channel_id=1, source_target_pairs={{0,4},{2,6},{4,0},{6,2},{8,12},{10,14},{12,8},{14,10},{16,20},{18,... | collective-permute-start | bytes 4128776 | tf_op jit(solution)/shard_map/ppermute | solution.py:150
  431.6 33.0 %collective-permute-start.38 = (bf16[2,224,1536]{2,1,0:T(8,128)(2,1)S(1)}, bf16[2,224,1536]{2,1,0:T(8,128)(2,1)S(1)}, u32[]{:S(2)}, u32[]{:S(2)}) collective-permute-start(bf16[2,224,1536]{2,1,0:T(8,128)(2,1)S(1)} %constant_dynamic-slice_fusion.12), channel_id=1, source_target_pairs={{0,1},{1,0},{2,3},{3,2},{4,5},{5,4},{6,7},{7,6},{8,9},{9,8},{10,11... | collective-permute-start | bytes 4128776 | tf_op jit(solution)/shard_map/ppermute | solution.py:154
  433.1 46.3 %collective-permute-start.45 = (bf16[512,768]{1,0:T(8,128)(2,1)S(1)}, bf16[512,768]{1,0:T(8,128)(2,1)S(1)}, u32[]{:S(2)}, u32[]{:S(2)}) collective-permute-start(bf16[512,768]{1,0:T(8,128)(2,1)S(1)} %add_convert_fusion.10), channel_id=1, source_target_pairs={{0,8},{2,10},{4,12},{6,14},{8,0},{10,2},{12,4},{14,6},{16,24},{18,... | collective-permute-start | bytes 2359304 | tf_op jit(solution)/shard_map/ppermute | solution.py:150
  493.8 26.8 %collective-permute-start.47 = (bf16[2,192,1536]{2,1,0:T(8,128)(2,1)S(1)}, bf16[2,192,1536]{2,1,0:T(8,128)(2,1)S(1)}, u32[]{:S(2)}, u32[]{:S(2)}) collective-permute-start(bf16[2,192,1536]{2,1,0:T(8,128)(2,1)S(1)} %pad_maximum_fusion.20), channel_id=1, source_target_pairs={{0,4},{2,6},{4,0},{6,2},{8,12},{10,14},{12,8},{14,10},{16,20},{18,... | collective-permute-start | bytes 3538952 | tf_op jit(solution)/shard_map/ppermute | solution.py:150
  (102 other events, 1178.5 us)

commit v5 on v4

--- a/solution.py
+++ b/solution.py
@@ -740,8 +740,9 @@
     late = PairReduce(reduces[2:], my_plane, *back_added)
     late.send()
     turned = back_scatter.turn(late.sent)
-    total = jnp.concatenate([early.total(*turned), late.total(*turned)])
-    home = send_home(after(total, *turned))
+    early_home = send_home(after(early.total(*turned), *turned))
+    late_home = send_home(late.total(*turned, early_home[1]))
+    home = [jnp.concatenate(pair, axis=1) for pair in zip(early_home, late_home)]
     attended = out_scatter.total()
     attended = jnp.where(is_live[:, None], attended, 0.0).astype(jnp.bfloat16)
     grad_normed = back_scatter.total()

time: 531 us -> 543 us (1.023)
  other arithmetic: 71.9 us -> 78.4 us
    ppermute x9, waiting for transfers between devices: 12.4 us -> 20.8 us  [swap_tp(): return lax.ppermute(value, 'tp', [(0, 1), (1, 0)])]
    ppermute x27 -> x29, waiting for transfers between devices: 124 us -> 117 us  [swap_fsdp(): return lax.ppermute(value, 'fsdp', pairs)]
    unnamed x176 -> x210, local copies, waits for them, and re-layouts: 15.4 us -> 13.5 us
    ppermute x27 -> x29, starting transfers between devices: 57.1 us -> 57.9 us  [swap_fsdp(): return lax.ppermute(value, 'fsdp', pairs)]
  transfers between devices with their start and end apart: 48 -> 50, of which waited for: 14 -> 17; matrix products, arithmetic and copies ran while one was open for 34% -> 35% of each run, Pallas kernels for 9% -> 8%
where the time goes in v5:
time: 543 us; the launch traced here: 535 us
  waiting for transfers between devices  159 us (29%)
  starting transfers between devices  112 us (21%)
  matrix products  79.3 us (15%)
  other arithmetic  78.4 us (14%)
  local copies, waits for them, and re-layouts  50.6 us (9%)
  Pallas kernels  47.7 us (9%)
  between operations  7.75 us (1%)
    ppermute x29, waiting for transfers between devices, swap_fsdp(): return lax.ppermute(value, 'fsdp', pairs)  117 us
    dot_general x16, matrix products, mm(): lax.dot_general(left, right, (((left_dim,), (right_dim,)), ((), ())), pre...  79.3 us
    ppermute x29, starting transfers between devices, swap_fsdp(): return lax.ppermute(value, 'fsdp', pairs)  57.9 us
    ppermute x12, starting transfers between devices, send_planes(): return lax.ppermute(value, 'fsdp', pairs)  43.9 us
    pallas_call x3, Pallas kernels, attend(): pl.pallas_call(functools.partial(attention_kernel, per_step), grid_spec=p...  31.4 us
    ppermute x12, waiting for transfers between devices, send_planes(): return lax.ppermute(value, 'fsdp', pairs)  20.8 us
    ppermute x9, waiting for transfers between devices, swap_tp(): return lax.ppermute(value, 'tp', [(0, 1), (1, 0)])  20.8 us
    convert_element_type x7, other arithmetic, add_rounded(): (left.astype(jnp.float32) + right.astype(jnp.float32)).astype(jnp.bfloat16)  16.9 us
  transfers between devices with their start and end apart: 50, of which 17 were waited for; matrix products, arithmetic and copies ran while one was open for 35% of the time, Pallas kernels for 8%

profile of v5, /device:TPU:0, one launch (start us, length us, event | category | flops | bytes accessed | tf_op | source)
XLA Modules:
  0.0 534.5 jit_solution(6207177112664080161)
XLA Ops:
  14.1 7.8 %collective-permute-done = bf16[2,112,1536]{2,1,0:T(8,128)(2,1)} collective-permute-done((bf16[2,112,1536]{2,1,0:T(8,128)(2,1)}, bf16[2,112,1536]{2,1,0:T(8,128)(2,1)}, u32[]{:S(2)}, u32[]{:S(2)}) %collective-permute-start) | collective-permute-done | bytes 688160 | tf_op jit(solution)/shard_map/ppermute | solution.py:150
  30.9 26.5 %collective-permute-done.3 = bf16[2,112,1536]{2,1,0:T(8,128)(2,1)S(1)} collective-permute-done((bf16[2,112,1536]{2,1,0:T(8,128)(2,1)S(1)}, bf16[2,112,1536]{2,1,0:T(8,128)(2,1)S(1)}, u32[]{:S(2)}, u32[]{:S(2)}) %collective-permute-start.3) | collective-permute-done | bytes 688160 | tf_op jit(solution)/shard_map/ppermute | solution.py:150
  60.6 9.2 %collective-permute-done.7 = bf16[2,192,1536]{2,1,0:T(8,128)(2,1)S(1)} collective-permute-done((bf16[2,192,1536]{2,1,0:T(8,128)(2,1)S(1)}, bf16[2,192,1536]{2,1,0:T(8,128)(2,1)S(1)}, u32[]{:S(2)}, u32[]{:S(2)}) %collective-permute-start.7) | collective-permute-done | bytes 1179680 | tf_op jit(solution)/shard_map/ppermute | solution.py:150
  74.3 17.1 %collective-permute-done.11 = bf16[2,112,1536]{2,1,0:T(8,128)(2,1)S(1)} collective-permute-done((bf16[2,112,1536]{2,1,0:T(8,128)(2,1)S(1)}, bf16[2,112,1536]{2,1,0:T(8,128)(2,1)S(1)}, u32[]{:S(2)}, u32[]{:S(2)}) %collective-permute-start.11) | collective-permute-done | bytes 688160 | tf_op jit(solution)/shard_map/ppermute | solution.py:150
  96.0 9.5 %collective-permute-done.12 = bf16[768,512]{1,0:T(8,128)(2,1)S(1)} collective-permute-done((bf16[768,512]{1,0:T(8,128)(2,1)S(1)}, bf16[768,512]{1,0:T(8,128)(2,1)S(1)}, u32[]{:S(2)}, u32[]{:S(2)}) %collective-permute-start.12) | collective-permute-done | bytes 786464 | tf_op jit(solution)/shard_map/ppermute | solution.py:150
  112.1 11.2 %collective-permute-done.9 = bf16[2,112,1536]{2,1,0:T(8,128)(2,1)S(1)} collective-permute-done((bf16[2,112,1536]{2,1,0:T(8,128)(2,1)}, bf16[2,112,1536]{2,1,0:T(8,128)(2,1)S(1)}, u32[]{:S(2)}, u32[]{:S(2)}) %collective-permute-start.9) | collective-permute-done | bytes 688160 | tf_op jit(solution)/shard_map/ppermute | solution.py:154
  133.1 7.3 %collective-permute-done.14 = bf16[2,768,512]{2,1,0:T(8,128)(2,1)} collective-permute-done((bf16[2,768,512]{2,1,0:T(8,128)(2,1)}, bf16[2,768,512]{2,1,0:T(8,128)(2,1)}, u32[]{:S(2)}, u32[]{:S(2)}) %collective-permute-start.14) | collective-permute-done | bytes 1572896 | tf_op jit(solution)/shard_map/ppermute | solution.py:150
  155.3 13.7 %norm_rows.1 = (bf16[1792,3072]{1,0:T(8,128)(2,1)S(1)}, f32[1792,128]{1,0:T(8,128)S(1)}) custom-call(s32[17]{0:T(128)S(1)} %pad_add_fusion.pick_ref, s32[16]{0:T(128)S(1)} %reshape.173.count_ref, bf16[2,2,2,112,1536]{4,3,2,1,0:T(8,128)(2,1)S(1)} %bitcast.147, bf16[2,2,2,112,1536]{4,3,2,1,0:T(8,128)(2,1)S(1)} %bitcast.148, ...), custom_call_target="tpu_custom_call" | custom-call | flops 55050240 | bytes 33030144 | tf_op jit(solution)/shard_map/norm_rows/pallas_call | solution.py:318
  169.1 13.0 %collective-permute-done.22 = bf16[224,3072]{1,0:T(8,128)(2,1)} collective-permute-done((bf16[224,3072]{1,0:T(8,128)(2,1)}, bf16[224,3072]{1,0:T(8,128)(2,1)}, u32[]{:S(2)}, u32[]{:S(2)}) %collective-permute-start.22) | collective-permute-done | bytes 1376288 | tf_op jit(solution)/shard_map/ppermute | solution.py:150
  182.1 6.2 %collective-permute-done.19 = bf16[1536,512]{1,0:T(8,128)(2,1)} collective-permute-done((bf16[1536,512]{1,0:T(8,128)(2,1)}, bf16[1536,512]{1,0:T(8,128)(2,1)}, u32[]{:S(2)}, u32[]{:S(2)}) %collective-permute-start.19) | collective-permute-done | bytes 1572896 | tf_op jit(solution)/shard_map/ppermute | solution.py:163
  197.7 7.6 %fusion.36.proj_ref = f32[1792,384]{1,0:T(8,128)S(1)} fusion(bf16[1792,3072]{1,0:T(8,128)(2,1)S(1)} %get-tuple-element.81, bf16[3072,384]{1,0:T(8,128)(2,1)} %fusion.4), kind=kOutput, calls=%fused_computation.227 | convolution fusion | flops 4227858432 | bytes 16121856 | tf_op jit(solution)/shard_map/dot_general | solution.py:341
  217.4 10.6 %attend_images.3 = (bf16[1792,128]{1,0:T(8,128)(2,1)S(1)}, bf16[1792,384]{1,0:T(8,128)(2,1)S(1)}) custom-call(s32[16]{0:T(128)S(1)} %reshape.172.count_ref, f32[1792,384]{1,0:T(8,128)S(1)} %fusion.36.proj_ref, bf16[1792,128]{1,0:T(8,128)(2,1)S(1)} %convolution_convert_fusion.12.grad_ref, f32[2,128]{1,0:T(2,128)S(1)} %pad_maximum_fusion.36.scale_ref), custom_call_target="tpu_custom_call" | custom-call | flops 308281344 | bytes 5505024 | tf_op jit(solution)/shard_map/attend_images/pallas_call | solution.py:403
  229.7 4.7 convolution_convert_fusion.6
  235.8 12.6 %collective-permute-start.27 = (bf16[512,1536]{1,0:T(8,128)(2,1)}, bf16[512,1536]{1,0:T(8,128)(2,1)}, u32[]{:S(2)}, u32[]{:S(2)}) collective-permute-start(bf16[512,1536]{1,0:T(8,128)(2,1)} %pad_maximum_fusion.10), channel_id=1, source_target_pairs={{0,8},{2,10},{4,12},{6,14},{24,16},{26,18},{28,20},{30,22},{1,9},{... | collective-permute-start | bytes 4718600 | tf_op jit(solution)/shard_map/ppermute | solution.py:163
  258.2 5.9 %fusion.37.proj_ref = f32[1792,384]{1,0:T(8,128)S(1)} fusion(bf16[1792,3072]{1,0:T(8,128)(2,1)S(1)} %get-tuple-element.81, bf16[3072,384]{1,0:T(8,128)(2,1)S(1)} %copy-done.44), kind=kOutput, calls=%fused_computation.228 | convolution fusion | flops 4227858432 | bytes 16121856 | tf_op jit(solution)/shard_map/dot_general | solution.py:341
  264.1 10.2 %attend_images.4 = (bf16[1792,128]{1,0:T(8,128)(2,1)S(1)}, bf16[1792,384]{1,0:T(8,128)(2,1)S(1)}) custom-call(s32[16]{0:T(128)S(1)} %reshape.172.count_ref, f32[1792,384]{1,0:T(8,128)S(1)} %fusion.37.proj_ref, bf16[1792,128]{1,0:T(8,128)(2,1)S(1)} %convolution_convert_fusion.11.grad_ref, f32[2,128]{1,0:T(2,128)S(1)} %pad_maximum_fusion.36.scale_ref), custom_call_target="tpu_custom_call" | custom-call | flops 308281344 | bytes 5505024 | tf_op jit(solution)/shard_map/attend_images/pallas_call | solution.py:403
  274.3 5.8 %convolution_convert_fusion.5 = bf16[384,3072]{1,0:T(8,128)(2,1)} fusion(bf16[1792,384]{1,0:T(8,128)(2,1)S(1)} %get-tuple-element.95, bf16[1792,3072]{1,0:T(8,128)(2,1)S(1)} %get-tuple-element.81), kind=kOutput, calls=%fused_computation.8 | convolution fusion | flops 4229038080 | bytes 14745600 | tf_op jit(solution)/shard_map/dot_general | solution.py:341
  283.1 6.8 %collective-permute-start.28 = (bf16[512,1536]{1,0:T(8,128)(2,1)}, bf16[512,1536]{1,0:T(8,128)(2,1)}, u32[]{:S(2)}, u32[]{:S(2)}) collective-permute-start(bf16[512,1536]{1,0:T(8,128)(2,1)} %pad_maximum_fusion.11), channel_id=1, source_target_pairs={{0,8},{2,10},{4,12},{6,14},{24,16},{26,18},{28,20},{30,22},{1,9},{... | collective-permute-start | bytes 4718600 | tf_op jit(solution)/shard_map/ppermute | solution.py:163
  302.0 5.9 %fusion.38.proj_ref = f32[1792,384]{1,0:T(8,128)S(1)} fusion(bf16[1792,3072]{1,0:T(8,128)(2,1)S(1)} %get-tuple-element.81, bf16[3072,384]{1,0:T(8,128)(2,1)S(1)} %copy-done.46), kind=kOutput, calls=%fused_computation.229 | convolution fusion | flops 4227858432 | bytes 16121856 | tf_op jit(solution)/shard_map/dot_general | solution.py:341
  308.0 10.6 %attend_images.5 = (bf16[1792,128]{1,0:T(8,128)(2,1)S(1)}, bf16[1792,384]{1,0:T(8,128)(2,1)S(1)}) custom-call(s32[16]{0:T(128)S(1)} %reshape.172.count_ref, f32[1792,384]{1,0:T(8,128)S(1)} %fusion.38.proj_ref, bf16[1792,128]{1,0:T(8,128)(2,1)S(1)} %convolution_convert_fusion.10.grad_ref, f32[2,128]{1,0:T(2,128)S(1)} %pad_maximum_fusion.36.scale_ref), custom_call_target="tpu_custom_call" | custom-call | flops 308281344 | bytes 5505024 | tf_op jit(solution)/shard_map/attend_images/pallas_call | solution.py:403
  322.2 4.9 convolution_convert_fusion.3
  333.3 3.5 add_convert_fusion.3
  337.6 4.6 convolution_convert_fusion.2
  345.6 4.7 convolution_convert_fusion.4
  351.8 10.2 %collective-permute-start.32 = (bf16[512,1536]{1,0:T(8,128)(2,1)}, bf16[512,1536]{1,0:T(8,128)(2,1)}, u32[]{:S(2)}, u32[]{:S(2)}) collective-permute-start(bf16[512,1536]{1,0:T(8,128)(2,1)} %pad_maximum_fusion.12), channel_id=1, source_target_pairs={{0,8},{2,10},{4,12},{6,14},{24,16},{26,18},{28,20},{30,22},{1,9},{... | collective-permute-start | bytes 4718600 | tf_op jit(solution)/shard_map/ppermute | solution.py:163
  372.6 10.9 %convolution_convert_fusion.1 = bf16[896,3072]{1,0:T(8,128)(2,1)} fusion(bf16[896,1152]{1,0:T(8,128)(2,1)} %get-tuple-element.107, bf16[3072,384]{1,0:T(8,128)(2,1)S(1)} %copy-done.47, bf16[3072,384]{1,0:T(8,128)(2,1)S(1)} %copy-done.45, bf16[3072,384]{1,0:T(8,128)(2,1)S(1)} %copy-done.42), kind=kOutput, calls=%fused_computation.4 | convolution fusion | flops 6365773824 | bytes 14647296 | tf_op jit(solution)/shard_map/dot_general | solution.py:341
  383.6 11.2 %collective-permute-done.32 = bf16[512,1536]{1,0:T(8,128)(2,1)} collective-permute-done((bf16[512,1536]{1,0:T(8,128)(2,1)}, bf16[512,1536]{1,0:T(8,128)(2,1)}, u32[]{:S(2)}, u32[]{:S(2)}) %collective-permute-start.32) | collective-permute-done | bytes 1572896 | tf_op jit(solution)/shard_map/ppermute | solution.py:163
  415.3 10.0 %convolution_convert_fusion = bf16[896,3072]{1,0:T(8,128)(2,1)S(1)} fusion(bf16[896,1152]{1,0:T(8,128)(2,1)} %get-tuple-element.114, bf16[3072,384]{1,0:T(8,128)(2,1)} %fusion.2, bf16[3072,384]{1,0:T(8,128)(2,1)} %fusion.3, bf16[3072,384]{1,0:T(8,128)(2,1)S(1)} %copy-done.43), kind=kOutput, calls=%fused_computation.3 | convolution fusion | flops 6365773824 | bytes 14647296 | tf_op jit(solution)/shard_map/dot_general | solution.py:341
  426.0 5.4 %collective-permute-start.44 = (bf16[1024,768]{1,0:T(8,128)(2,1)S(1)}, bf16[1024,768]{1,0:T(8,128)(2,1)S(1)}, u32[]{:S(2)}, u32[]{:S(2)}) collective-permute-start(bf16[1024,768]{1,0:T(8,128)(2,1)S(1)} %copy-done.58), channel_id=1, source_target_pairs={{0,8},{2,10},{4,12},{6,14},{8,0},{10,2},{12,4},{14,6},{16,24},{18,... | collective-permute-start | bytes 4718600 | tf_op jit(solution)/shard_map/ppermute | solution.py:150
  438.5 28.8 %collective-permute-start.46 = (bf16[512,768]{1,0:T(8,128)(2,1)}, bf16[512,768]{1,0:T(8,128)(2,1)}, u32[]{:S(2)}, u32[]{:S(2)}) collective-permute-start(bf16[512,768]{1,0:T(8,128)(2,1)} %add_convert_fusion.10), channel_id=1, source_target_pairs={{0,8},{2,10},{4,12},{6,14},{8,0},{10,2},{12,4},{14,6},{16,24},{18,... | collective-permute-start | bytes 2359304 | tf_op jit(solution)/shard_map/ppermute | solution.py:150
  477.5 8.1 %collective-permute-done.42 = bf16[224,1536]{1,0:T(8,128)(2,1)} collective-permute-done((bf16[224,1536]{1,0:T(8,128)(2,1)}, bf16[224,1536]{1,0:T(8,128)(2,1)}, u32[]{:S(2)}, u32[]{:S(2)}) %collective-permute-start.42) | collective-permute-done | bytes 688160 | tf_op jit(solution)/shard_map/ppermute | solution.py:154
  506.4 25.1 %collective-permute-done.49 = bf16[2,192,512]{2,1,0:T(8,128)(2,1)S(1)} collective-permute-done((bf16[2,192,512]{2,1,0:T(8,128)(2,1)S(1)}, bf16[2,192,512]{2,1,0:T(8,128)(2,1)S(1)}, u32[]{:S(2)}, u32[]{:S(2)}) %collective-permute-start.49) | collective-permute-done | bytes 393248 | tf_op jit(solution)/shard_map/ppermute | solution.py:150
  (445 shorter events, 197.0 us)
Async XLA Ops:
  12.5 57.4 %collective-permute-start.5 = (bf16[224,3072]{1,0:T(8,128)(2,1)S(1)}, bf16[224,3072]{1,0:T(8,128)(2,1)}, u32[]{:S(2)}, u32[]{:S(2)}) collective-permute-start(bf16[224,3072]{1,0:T(8,128)(2,1)S(1)} %get-tuple-element.151), channel_id=1, source_target_pairs={{0,4},{2,6},{4,0},{6,2},{8,12},{10,14},{12,8},{14,10},{16,20},{18,... | collective-permute-start | bytes 4128776 | tf_op jit(solution)/shard_map/ppermute | solution.py:150
  23.3 46.6 %collective-permute-start.4 = (bf16[448,3072]{1,0:T(8,128)(2,1)}, bf16[448,3072]{1,0:T(8,128)(2,1)S(1)}, u32[]{:S(2)}, u32[]{:S(2)}) collective-permute-start(bf16[448,3072]{1,0:T(8,128)(2,1)} %copy-done.4), channel_id=1, source_target_pairs={{0,2},{2,0},{4,6},{6,4},{8,10},{10,8},{12,14},{14,12},{16,18},{18,... | collective-permute-start | bytes 8257544 | tf_op jit(solution)/shard_map/ppermute | solution.py:150
  23.4 34.1 %collective-permute-start.1 = (bf16[2,112,1536]{2,1,0:T(8,128)(2,1)S(1)}, bf16[2,112,1536]{2,1,0:T(8,128)(2,1)S(1)}, u32[]{:S(2)}, u32[]{:S(2)}) collective-permute-start(bf16[2,112,1536]{2,1,0:T(8,128)(2,1)S(1)} %broadcast_select_fusion.18), channel_id=1, source_target_pairs={{0,16},{2,18},{4,20},{6,22},{8,24},{10,26},{12,28},{14,30},{16,0},... | collective-permute-start | bytes 2064392 | tf_op jit(solution)/shard_map/ppermute | solution.py:150
  26.3 31.1 %collective-permute-start.3 = (bf16[2,112,1536]{2,1,0:T(8,128)(2,1)S(1)}, bf16[2,112,1536]{2,1,0:T(8,128)(2,1)S(1)}, u32[]{:S(2)}, u32[]{:S(2)}) collective-permute-start(bf16[2,112,1536]{2,1,0:T(8,128)(2,1)S(1)} %bitcast.167), channel_id=1, source_target_pairs={{0,8},{2,10},{4,12},{6,14},{8,0},{10,2},{12,4},{14,6},{16,24},{18,... | collective-permute-start | bytes 2064392 | tf_op jit(solution)/shard_map/ppermute | solution.py:150
  29.3 40.5 %collective-permute-start.7 = (bf16[2,192,1536]{2,1,0:T(8,128)(2,1)S(1)}, bf16[2,192,1536]{2,1,0:T(8,128)(2,1)S(1)}, u32[]{:S(2)}, u32[]{:S(2)}) collective-permute-start(bf16[2,192,1536]{2,1,0:T(8,128)(2,1)S(1)} %pad_maximum_fusion.17), channel_id=1, source_target_pairs={{0,4},{2,6},{4,0},{6,2},{8,12},{10,14},{12,8},{14,10},{16,20},{18,... | collective-permute-start | bytes 3538952 | tf_op jit(solution)/shard_map/ppermute | solution.py:150
  57.7 50.8 %collective-permute-start.2 = (bf16[2,112,1536]{2,1,0:T(8,128)(2,1)S(1)}, bf16[2,112,1536]{2,1,0:T(8,128)(2,1)S(1)}, u32[]{:S(2)}, u32[]{:S(2)}) collective-permute-start(bf16[2,112,1536]{2,1,0:T(8,128)(2,1)S(1)} %broadcast_select_fusion.19), channel_id=1, source_target_pairs={{0,1},{1,0},{2,3},{3,2},{4,5},{5,4},{6,7},{7,6},{8,9},{9,8},{10,11... | collective-permute-start | bytes 2064392 | tf_op jit(solution)/shard_map/ppermute | solution.py:154
  59.3 32.1 %collective-permute-start.11 = (bf16[2,112,1536]{2,1,0:T(8,128)(2,1)S(1)}, bf16[2,112,1536]{2,1,0:T(8,128)(2,1)S(1)}, u32[]{:S(2)}, u32[]{:S(2)}) collective-permute-start(bf16[2,112,1536]{2,1,0:T(8,128)(2,1)S(1)} %broadcast_select_fusion.17), channel_id=1, source_target_pairs={{0,16},{2,18},{4,20},{6,22},{8,24},{10,26},{12,28},{14,30},{16,0},... | collective-permute-start | bytes 2064392 | tf_op jit(solution)/shard_map/ppermute | solution.py:150
  73.8 31.7 %collective-permute-start.12 = (bf16[768,512]{1,0:T(8,128)(2,1)S(1)}, bf16[768,512]{1,0:T(8,128)(2,1)S(1)}, u32[]{:S(2)}, u32[]{:S(2)}) collective-permute-start(bf16[768,512]{1,0:T(8,128)(2,1)S(1)} %pad_maximum_fusion.23), channel_id=1, source_target_pairs={{0,8},{2,10},{4,12},{6,14},{8,0},{10,2},{12,4},{14,6},{16,24},{18,... | collective-permute-start | bytes 2359304 | tf_op jit(solution)/shard_map/ppermute | solution.py:150
  92.4 33.7 %collective-permute-start.15 = (bf16[2,112,1536]{2,1,0:T(8,128)(2,1)}, bf16[2,112,1536]{2,1,0:T(8,128)(2,1)}, u32[]{:S(2)}, u32[]{:S(2)}) collective-permute-start(bf16[2,112,1536]{2,1,0:T(8,128)(2,1)} %broadcast_select_fusion.16), channel_id=1, source_target_pairs={{0,1},{1,0},{2,3},{3,2},{4,5},{5,4},{6,7},{7,6},{8,9},{9,8},{10,11... | collective-permute-start | bytes 2064392 | tf_op jit(solution)/shard_map/ppermute | solution.py:154
  94.6 28.7 %collective-permute-start.9 = (bf16[2,112,1536]{2,1,0:T(8,128)(2,1)}, bf16[2,112,1536]{2,1,0:T(8,128)(2,1)S(1)}, u32[]{:S(2)}, u32[]{:S(2)}) collective-permute-start(bf16[2,112,1536]{2,1,0:T(8,128)(2,1)} %collective-permute-done.8), channel_id=1, source_target_pairs={{0,1},{1,0},{2,3},{3,2},{4,5},{5,4},{6,7},{7,6},{8,9},{9,8},{10,11... | collective-permute-start | bytes 2064392 | tf_op jit(solution)/shard_map/ppermute | solution.py:154
  106.0 34.4 %collective-permute-start.14 = (bf16[2,768,512]{2,1,0:T(8,128)(2,1)}, bf16[2,768,512]{2,1,0:T(8,128)(2,1)}, u32[]{:S(2)}, u32[]{:S(2)}) collective-permute-start(bf16[2,768,512]{2,1,0:T(8,128)(2,1)} %pad_maximum_fusion.7), channel_id=1, source_target_pairs={{0,8},{2,10},{4,12},{6,14},{8,0},{10,2},{12,4},{14,6},{16,24},{18,... | collective-permute-start | bytes 4718600 | tf_op jit(solution)/shard_map/ppermute | solution.py:150
  109.4 32.5 %collective-permute-start.13 = (bf16[1536,512]{1,0:T(8,128)(2,1)}, bf16[1536,512]{1,0:T(8,128)(2,1)}, u32[]{:S(2)}, u32[]{:S(2)}) collective-permute-start(bf16[1536,512]{1,0:T(8,128)(2,1)} %pad_maximum_fusion.6), channel_id=1, source_target_pairs={{8,16},{10,18},{12,20},{14,22},{16,8},{18,10},{20,12},{22,14},{9,1... | collective-permute-start | bytes 4718600 | tf_op jit(solution)/shard_map/ppermute | solution.py:163
  144.7 43.6 %collective-permute-start.19 = (bf16[1536,512]{1,0:T(8,128)(2,1)}, bf16[1536,512]{1,0:T(8,128)(2,1)}, u32[]{:S(2)}, u32[]{:S(2)}) collective-permute-start(bf16[1536,512]{1,0:T(8,128)(2,1)} %collective-permute-done.13), channel_id=1, source_target_pairs={{8,0},{10,2},{12,4},{14,6},{16,24},{18,26},{20,28},{22,30},{9,1},{... | collective-permute-start | bytes 4718600 | tf_op jit(solution)/shard_map/ppermute | solution.py:163
  149.6 32.5 %collective-permute-start.22 = (bf16[224,3072]{1,0:T(8,128)(2,1)}, bf16[224,3072]{1,0:T(8,128)(2,1)}, u32[]{:S(2)}, u32[]{:S(2)}) collective-permute-start(bf16[224,3072]{1,0:T(8,128)(2,1)} %get-tuple-element.85), channel_id=1, source_target_pairs={{0,4},{2,6},{4,0},{6,2},{8,12},{10,14},{12,8},{14,10},{16,20},{18,... | collective-permute-start | bytes 4128776 | tf_op jit(solution)/shard_map/ppermute | solution.py:150
  190.5 59.1 %collective-permute-start.25 = (bf16[1536,512]{1,0:T(8,128)(2,1)}, bf16[1536,512]{1,0:T(8,128)(2,1)}, u32[]{:S(2)}, u32[]{:S(2)}) collective-permute-start(bf16[1536,512]{1,0:T(8,128)(2,1)} %pad_maximum_fusion.9), channel_id=1, source_target_pairs={{8,16},{10,18},{12,20},{14,22},{16,8},{18,10},{20,12},{22,14},{9,1... | collective-permute-start | bytes 4718600 | tf_op jit(solution)/shard_map/ppermute | solution.py:163
  192.3 57.3 %collective-permute-start.24 = (bf16[1536,512]{1,0:T(8,128)(2,1)}, bf16[1536,512]{1,0:T(8,128)(2,1)}, u32[]{:S(2)}, u32[]{:S(2)}) collective-permute-start(bf16[1536,512]{1,0:T(8,128)(2,1)} %collective-permute-done.20), channel_id=1, source_target_pairs={{8,0},{10,2},{12,4},{14,6},{16,24},{18,26},{20,28},{22,30},{9,1},{... | collective-permute-start | bytes 4718600 | tf_op jit(solution)/shard_map/ppermute | solution.py:163
  235.8 54.1 %collective-permute-start.27 = (bf16[512,1536]{1,0:T(8,128)(2,1)}, bf16[512,1536]{1,0:T(8,128)(2,1)}, u32[]{:S(2)}, u32[]{:S(2)}) collective-permute-start(bf16[512,1536]{1,0:T(8,128)(2,1)} %pad_maximum_fusion.10), channel_id=1, source_target_pairs={{0,8},{2,10},{4,12},{6,14},{24,16},{26,18},{28,20},{30,22},{1,9},{... | collective-permute-start | bytes 4718600 | tf_op jit(solution)/shard_map/ppermute | solution.py:163
  256.7 38.2 %collective-permute-start.26 = (bf16[1536,512]{1,0:T(8,128)(2,1)}, bf16[1536,512]{1,0:T(8,128)(2,1)}, u32[]{:S(2)}, u32[]{:S(2)}) collective-permute-start(bf16[1536,512]{1,0:T(8,128)(2,1)} %collective-permute-done.25), channel_id=1, source_target_pairs={{8,0},{10,2},{12,4},{14,6},{16,24},{18,26},{20,28},{22,30},{9,1},{... | collective-permute-start | bytes 4718600 | tf_op jit(solution)/shard_map/ppermute | solution.py:163
  283.1 39.0 %collective-permute-start.28 = (bf16[512,1536]{1,0:T(8,128)(2,1)}, bf16[512,1536]{1,0:T(8,128)(2,1)}, u32[]{:S(2)}, u32[]{:S(2)}) collective-permute-start(bf16[512,1536]{1,0:T(8,128)(2,1)} %pad_maximum_fusion.11), channel_id=1, source_target_pairs={{0,8},{2,10},{4,12},{6,14},{24,16},{26,18},{28,20},{30,22},{1,9},{... | collective-permute-start | bytes 4718600 | tf_op jit(solution)/shard_map/ppermute | solution.py:163
  292.9 29.2 %collective-permute-start.29 = (bf16[512,1536]{1,0:T(8,128)(2,1)}, bf16[512,1536]{1,0:T(8,128)(2,1)}, u32[]{:S(2)}, u32[]{:S(2)}) collective-permute-start(bf16[512,1536]{1,0:T(8,128)(2,1)} %add_convert_fusion.4), channel_id=1, source_target_pairs={{8,16},{10,18},{12,20},{14,22},{16,8},{18,10},{20,12},{22,14},{9,1... | collective-permute-start | bytes 4718600 | tf_op jit(solution)/shard_map/ppermute | solution.py:163
  327.1 34.9 %collective-permute-start.30 = (bf16[2,448,3072]{2,1,0:T(8,128)(2,1)}, bf16[2,448,3072]{2,1,0:T(8,128)(2,1)}, u32[]{:S(2)}, u32[]{:S(2)}) collective-permute-start(bf16[2,448,3072]{2,1,0:T(8,128)(2,1)} %bitcast.179), channel_id=1, source_target_pairs={{0,2},{2,0},{4,6},{6,4},{8,10},{10,8},{12,14},{14,12},{16,18},{18,... | collective-permute-start | bytes 16515080 | tf_op jit(solution)/shard_map/ppermute | solution.py:150
  342.1 41.4 %collective-permute-start.33 = (bf16[512,1536]{1,0:T(8,128)(2,1)}, bf16[512,1536]{1,0:T(8,128)(2,1)}, u32[]{:S(2)}, u32[]{:S(2)}) collective-permute-start(bf16[512,1536]{1,0:T(8,128)(2,1)} %add_convert_fusion.3), channel_id=1, source_target_pairs={{8,16},{10,18},{12,20},{14,22},{16,8},{18,10},{20,12},{22,14},{9,1... | collective-permute-start | bytes 4718600 | tf_op jit(solution)/shard_map/ppermute | solution.py:163
  351.8 43.1 %collective-permute-start.32 = (bf16[512,1536]{1,0:T(8,128)(2,1)}, bf16[512,1536]{1,0:T(8,128)(2,1)}, u32[]{:S(2)}, u32[]{:S(2)}) collective-permute-start(bf16[512,1536]{1,0:T(8,128)(2,1)} %pad_maximum_fusion.12), channel_id=1, source_target_pairs={{0,8},{2,10},{4,12},{6,14},{24,16},{26,18},{28,20},{30,22},{1,9},{... | collective-permute-start | bytes 4718600 | tf_op jit(solution)/shard_map/ppermute | solution.py:163
  364.9 37.1 %collective-permute-start.35 = (bf16[224,3072]{1,0:T(8,128)(2,1)}, bf16[224,3072]{1,0:T(8,128)(2,1)}, u32[]{:S(2)}, u32[]{:S(2)}) collective-permute-start(bf16[224,3072]{1,0:T(8,128)(2,1)} %fusion.6), channel_id=1, source_target_pairs={{0,4},{2,6},{4,0},{6,2},{8,12},{10,14},{12,8},{14,10},{16,20},{18,... | collective-permute-start | bytes 4128776 | tf_op jit(solution)/shard_map/ppermute | solution.py:150
  370.7 31.9 %collective-permute-start.31 = (bf16[2,224,1536]{2,1,0:T(8,128)(2,1)}, bf16[2,224,1536]{2,1,0:T(8,128)(2,1)}, u32[]{:S(2)}, u32[]{:S(2)}) collective-permute-start(bf16[2,224,1536]{2,1,0:T(8,128)(2,1)} %constant_dynamic-slice_fusion.22), channel_id=1, source_target_pairs={{0,1},{1,0},{2,3},{3,2},{4,5},{5,4},{6,7},{7,6},{8,9},{9,8},{10,11... | collective-permute-start | bytes 4128776 | tf_op jit(solution)/shard_map/ppermute | solution.py:154
  402.6 30.1 %collective-permute-start.37 = (bf16[2,448,3072]{2,1,0:T(8,128)(2,1)}, bf16[2,448,3072]{2,1,0:T(8,128)(2,1)S(1)}, u32[]{:S(2)}, u32[]{:S(2)}) collective-permute-start(bf16[2,448,3072]{2,1,0:T(8,128)(2,1)} %bitcast.38), channel_id=1, source_target_pairs={{0,2},{2,0},{4,6},{6,4},{8,10},{10,8},{12,14},{14,12},{16,18},{18,... | collective-permute-start | bytes 16515080 | tf_op jit(solution)/shard_map/ppermute | solution.py:150
  426.0 46.1 %collective-permute-start.44 = (bf16[1024,768]{1,0:T(8,128)(2,1)S(1)}, bf16[1024,768]{1,0:T(8,128)(2,1)S(1)}, u32[]{:S(2)}, u32[]{:S(2)}) collective-permute-start(bf16[1024,768]{1,0:T(8,128)(2,1)S(1)} %copy-done.58), channel_id=1, source_target_pairs={{0,8},{2,10},{4,12},{6,14},{8,0},{10,2},{12,4},{14,6},{16,24},{18,... | collective-permute-start | bytes 4718600 | tf_op jit(solution)/shard_map/ppermute | solution.py:150
  433.3 34.1 %collective-permute-start.41 = (bf16[224,3072]{1,0:T(8,128)(2,1)S(1)}, bf16[224,3072]{1,0:T(8,128)(2,1)S(1)}, u32[]{:S(2)}, u32[]{:S(2)}) collective-permute-start(bf16[224,3072]{1,0:T(8,128)(2,1)S(1)} %fusion.8), channel_id=1, source_target_pairs={{0,4},{2,6},{4,0},{6,2},{8,12},{10,14},{12,8},{14,10},{16,20},{18,... | collective-permute-start | bytes 4128776 | tf_op jit(solution)/shard_map/ppermute | solution.py:150
  435.7 33.9 %collective-permute-start.38 = (bf16[2,224,1536]{2,1,0:T(8,128)(2,1)S(1)}, bf16[2,224,1536]{2,1,0:T(8,128)(2,1)S(1)}, u32[]{:S(2)}, u32[]{:S(2)}) collective-permute-start(bf16[2,224,1536]{2,1,0:T(8,128)(2,1)S(1)} %constant_dynamic-slice_fusion.15), channel_id=1, source_target_pairs={{0,1},{1,0},{2,3},{3,2},{4,5},{5,4},{6,7},{7,6},{8,9},{9,8},{10,11... | collective-permute-start | bytes 4128776 | tf_op jit(solution)/shard_map/ppermute | solution.py:154
  438.5 57.4 %collective-permute-start.46 = (bf16[512,768]{1,0:T(8,128)(2,1)}, bf16[512,768]{1,0:T(8,128)(2,1)}, u32[]{:S(2)}, u32[]{:S(2)}) collective-permute-start(bf16[512,768]{1,0:T(8,128)(2,1)} %add_convert_fusion.10), channel_id=1, source_target_pairs={{0,8},{2,10},{4,12},{6,14},{8,0},{10,2},{12,4},{14,6},{16,24},{18,... | collective-permute-start | bytes 2359304 | tf_op jit(solution)/shard_map/ppermute | solution.py:150
  504.0 27.5 %collective-permute-start.48 = (bf16[2,192,1024]{2,1,0:T(8,128)(2,1)S(1)}, bf16[2,192,1024]{2,1,0:T(8,128)(2,1)S(1)}, u32[]{:S(2)}, u32[]{:S(2)}) collective-permute-start(bf16[2,192,1024]{2,1,0:T(8,128)(2,1)S(1)} %pad_maximum_fusion.27), channel_id=1, source_target_pairs={{0,4},{2,6},{4,0},{6,2},{8,12},{10,14},{12,8},{14,10},{16,20},{18,... | collective-permute-start | bytes 2359304 | tf_op jit(solution)/shard_map/ppermute | solution.py:150
  504.5 27.0 %collective-permute-start.49 = (bf16[2,192,512]{2,1,0:T(8,128)(2,1)S(1)}, bf16[2,192,512]{2,1,0:T(8,128)(2,1)S(1)}, u32[]{:S(2)}, u32[]{:S(2)}) collective-permute-start(bf16[2,192,512]{2,1,0:T(8,128)(2,1)S(1)} %pad_maximum_fusion.34), channel_id=1, source_target_pairs={{0,4},{2,6},{4,0},{6,2},{8,12},{10,14},{12,8},{14,10},{16,20},{18,... | collective-permute-start | bytes 1179656 | tf_op jit(solution)/shard_map/ppermute | solution.py:150
  (121 other events, 1253.2 us)
